TPU v7x, 32 devices: a whole 2x2x4 slice. The times are simulated.
32 devices in a mesh: dp: 8 (over y, x, core), tensor: 4 (over z).
Axes of the slice: x: 2, y: 2, z: 4, core: 2. Of those that a mesh axis runs over, the one named last changes fastest.
Arguments:
- inputs: bfloat16 [4096, 1024], P(('dp', 'tensor')), may hold values from -6 to 6
- segment_ids: int32 [4096], P('dp'), may hold values from -1 to 31, as said below
- ln1_gain: float32 [1024], replicated, may hold values from 0.5 to 1.5
- ln1_bias: float32 [1024], replicated, may hold values from -1.75 to 1.75
- ln2_gain: float32 [1024], replicated, may hold values from 0.5 to 1.5
- ln2_bias: float32 [1024], replicated, may hold values from -1.75 to 1.75
- qkv_weight: bfloat16 [1024, 3072], P('dp', 'tensor'), may hold values from -0.1875 to 0.1875
- qkv_bias: float32 [3072], P('tensor'), may hold values from -1.75 to 1.75
- dense_weight: bfloat16 [1024, 1024], P('dp', 'tensor'), may hold values from -0.5 to 0.5
- dense_bias: float32 [1024], replicated, may hold values from -1.75 to 1.75
- fc1_weight: bfloat16 [1024, 4096], P('dp', 'tensor'), may hold values from -0.1875 to 0.1875
- fc1_bias: float32 [4096], P('tensor'), may hold values from -1.75 to 1.75
- fc2_weight: bfloat16 [1024, 4096], P('dp', 'tensor'), may hold values from -0.09375 to 0.09375
- fc2_bias: float32 [1024], replicated, may hold values from -1.75 to 1.75
- cotangent: bfloat16 [4096, 1024], P(('dp', 'tensor')), may hold values from -6 to 6
Outputs:
- output: bfloat16 [4096, 1024], P(('dp', 'tensor'))
- input_grad: float32 [4096, 1024], P(('dp', 'tensor'))
- ln1_gain_grad: float32 [1024], replicated
- ln1_bias_grad: float32 [1024], replicated
- ln2_gain_grad: float32 [1024], replicated
- ln2_bias_grad: float32 [1024], replicated
- qkv_weight_grad: float32 [1024, 3072], P('dp', 'tensor')
- qkv_bias_grad: float32 [3072], P('tensor')
- dense_weight_grad: float32 [1024, 1024], P('dp', 'tensor')
- dense_bias_grad: float32 [1024], replicated
- fc1_weight_grad: float32 [1024, 4096], P('dp', 'tensor')
- fc1_bias_grad: float32 [4096], P('tensor')
- fc2_weight_grad: float32 [1024, 4096], P('dp', 'tensor')
- fc2_bias_grad: float32 [1024], replicated
Inputs may be any that keep to these rules, and one draw needn't show every extreme that they name: `segment_ids`: in each group of 512 rows the tokens with id >= 0 come first, 128 times a whole number of them (at least one block); their ids start at 0 and never fall, and a new sequence starts only at a multiple of 16 slots. Padding has id -1. In every draw some group has no padding and starts a sequence at every such multiple.
All inputs are finite; a program needn't handle non-finite values.
Results may differ from a plain program's by a relative error of at most 0.01.
Values may be sent and summed in bfloat16 or wider, within the bound.
No kernel may reach another device: no remote copies, remote signals or barrier semaphores. Data moves between devices by JAX's collectives and lax.ppermute only.
A program may use at most 128 MiB of HBM per device.

v0:
```python
from functools import partial

import jax
import jax.numpy as jnp
from jax import lax
from jax.sharding import PartitionSpec as P

HD = 64
ROT = 16


EPS = 1e-05


def normalize(embedded, gain, shift):
    center = embedded - jnp.mean(embedded, axis=-1, keepdims=True)
    inv_std = lax.rsqrt(jnp.mean(center * center, axis=-1, keepdims=True) + EPS)
    scaled = center * inv_std
    return ((scaled * gain + shift).astype(jnp.bfloat16), scaled, inv_std)


def normalize_back(grads, gain, scaled, inv_std):
    grad_scaled = grads * gain
    grad_input = inv_std * (
        grad_scaled
        - jnp.mean(grad_scaled, axis=-1, keepdims=True)
        - scaled * jnp.mean(grad_scaled * scaled, axis=-1, keepdims=True)
    )
    return (grad_input, jnp.sum(grads * scaled, axis=0), jnp.sum(grads, axis=0))


def rotary_tables(segment_ids):
    row_index = jnp.arange(segment_ids.shape[0], dtype=jnp.int32)
    earlier = (segment_ids[None, :] >= 0) & (segment_ids[None, :] < segment_ids[:, None])
    position = (row_index - jnp.sum(earlier.astype(jnp.int32), axis=1)).astype(jnp.float32)
    half_rot = ROT // 2
    frequency = 10000.0 ** (-2.0 * jnp.arange(half_rot, dtype=jnp.float32) / ROT)
    angles = position[:, None] * frequency[None, :]
    angles = jnp.concatenate([angles, angles], axis=1)
    return (jnp.cos(angles)[:, None, :], jnp.sin(angles)[:, None, :])


def allowed_mask(segment_ids):
    row_index = jnp.arange(segment_ids.shape[0], dtype=jnp.int32)
    same_segment = (segment_ids[:, None] == segment_ids[None, :]) & (segment_ids[:, None] >= 0)
    same_segment = same_segment & (row_index[None, :] < row_index[:, None])
    return same_segment | (row_index[:, None] == row_index[None, :])


def rotate(heads_in, cos_table, sine_table):
    half_rot = ROT // 2
    rotated_part = heads_in[..., :ROT]
    turned = jnp.concatenate([-rotated_part[..., half_rot:], rotated_part[..., :half_rot]], axis=-1)
    return jnp.concatenate(
        [rotated_part * cos_table + turned * sine_table, heads_in[..., ROT:]], axis=-1
    )


def rotate_back(grads, cos_table, sine_table):
    half_rot = ROT // 2
    rotated_part = grads[..., :ROT]
    scaled_sin = rotated_part * sine_table
    turned = jnp.concatenate([scaled_sin[..., half_rot:], -scaled_sin[..., :half_rot]], axis=-1)
    return jnp.concatenate([rotated_part * cos_table + turned, grads[..., ROT:]], axis=-1)


def score_block(queries, key_rows, allowed):
    scores = jnp.einsum("qhd,khd->hqk", queries, key_rows, preferred_element_type=jnp.float32)
    scores = scores * queries.shape[-1] ** (-0.5)
    return jnp.where(allowed[None, :, :], scores, -jnp.inf)


def attend(queries, key_rows, value_rows, allowed, validity):
    scores = score_block(queries, key_rows, allowed)
    row_max = jnp.max(scores, axis=-1, keepdims=True)
    logsum = row_max + jnp.log(jnp.sum(jnp.exp(scores - row_max), axis=-1, keepdims=True))
    soft_weights = jnp.exp(scores - logsum).astype(jnp.bfloat16)
    attended = jnp.einsum(
        "hqk,khd->qhd", soft_weights, value_rows, preferred_element_type=jnp.float32
    )
    return ((attended * validity[:, None, None]).astype(jnp.bfloat16), logsum)


def attend_back(queries, key_rows, value_rows, allowed, logsum, grad_out):
    scores = score_block(queries, key_rows, allowed)
    probs_full = jnp.exp(scores - logsum)
    soft_weights = probs_full.astype(jnp.bfloat16)
    grad_soft = jnp.einsum("qhd,khd->hqk", grad_out, value_rows, preferred_element_type=jnp.float32)
    row_inner = jnp.sum(probs_full * grad_soft, axis=-1, keepdims=True)
    grad_scores = (probs_full * (grad_soft - row_inner) * queries.shape[-1] ** (-0.5)).astype(
        jnp.bfloat16
    )
    grad_query = jnp.einsum(
        "hqk,khd->qhd", grad_scores, key_rows, preferred_element_type=jnp.float32
    )
    grad_key = jnp.einsum("hqk,qhd->khd", grad_scores, queries, preferred_element_type=jnp.float32)
    grad_value = jnp.einsum(
        "hqk,qhd->khd", soft_weights, grad_out, preferred_element_type=jnp.float32
    )
    return (grad_query, grad_key, grad_value)


def on_device(
    inputs,
    segment_ids,
    ln1_gain,
    ln1_bias,
    ln2_gain,
    ln2_bias,
    qkv_weight,
    qkv_bias,
    dense_weight,
    dense_bias,
    fc1_weight,
    fc1_bias,
    fc2_weight,
    fc2_bias,
    cotangent,
):
    local_rows = inputs.shape[0]
    length = segment_ids.shape[0]
    embedded = inputs.astype(jnp.float32)
    validity = (segment_ids >= 0).astype(jnp.float32)
    own_validity = lax.dynamic_slice_in_dim(
        validity, lax.axis_index("tensor") * local_rows, local_rows
    )
    allowed = allowed_mask(segment_ids)
    cos_table, sine_table = rotary_tables(segment_ids)
    normed1, scaled1, spread1 = normalize(embedded, ln1_gain, ln1_bias)
    normed2, scaled2, spread2 = normalize(embedded, ln2_gain, ln2_bias)
    whole1, whole2 = (
        lax.all_gather(normed1, "tensor", axis=0, tiled=True),
        lax.all_gather(normed2, "tensor", axis=0, tiled=True),
    )
    gathered = (
        lax.all_gather(qkv_weight, "dp", axis=0, tiled=True),
        lax.all_gather(dense_weight, "dp", axis=0, tiled=True),
        lax.all_gather(fc1_weight, "dp", axis=0, tiled=True),
        lax.all_gather(fc2_weight, "dp", axis=0, tiled=True),
    )
    qkv_full, dense_full, fc1_full, fc2_full = gathered
    projected = jnp.dot(whole1, qkv_full, preferred_element_type=jnp.float32) + qkv_bias
    projected = projected.reshape(length, -1, 3, HD)
    queries = rotate(projected[:, :, 0], cos_table, sine_table).astype(jnp.bfloat16)
    key_rows = rotate(projected[:, :, 1], cos_table, sine_table).astype(jnp.bfloat16)
    value_rows = projected[:, :, 2].astype(jnp.bfloat16)
    attended, logsum = attend(queries, key_rows, value_rows, allowed, validity)
    attended_flat = attended.reshape(length, -1)
    hidden = jnp.dot(whole2, fc1_full, preferred_element_type=jnp.float32) + fc1_bias
    active = jax.nn.gelu(hidden, approximate=False).astype(jnp.bfloat16)
    branch = jnp.dot(attended_flat, dense_full.T, preferred_element_type=jnp.float32)
    branch = branch + jnp.dot(active, fc2_full.T, preferred_element_type=jnp.float32)
    summed = lax.psum_scatter(branch, "tensor", scatter_dimension=0, tiled=True)
    output = (embedded + summed + dense_bias + fc2_bias).astype(jnp.bfloat16)
    masked = cotangent.astype(jnp.float32) * own_validity[:, None]
    out_bias = jnp.sum(masked, axis=0)
    grad_whole = lax.all_gather(masked.astype(jnp.bfloat16), "tensor", axis=0, tiled=True)
    qkv_back, dense_back, fc1_back, fc2_back = (
        lax.all_gather(qkv_weight, "dp", axis=0, tiled=True),
        lax.all_gather(dense_weight, "dp", axis=0, tiled=True),
        lax.all_gather(fc1_weight, "dp", axis=0, tiled=True),
        lax.all_gather(fc2_weight, "dp", axis=0, tiled=True),
    )
    grad_attended = jnp.dot(grad_whole, dense_back, preferred_element_type=jnp.float32)
    dense_grad = jnp.dot(grad_whole.T, attended_flat, preferred_element_type=jnp.float32)
    grad_active = jnp.dot(grad_whole, fc2_back, preferred_element_type=jnp.float32)
    fc2_grad = jnp.dot(grad_whole.T, active, preferred_element_type=jnp.float32)
    grad_hidden = jax.vjp(partial(jax.nn.gelu, approximate=False), hidden)[1](grad_active)[0]
    fc1_bias_part = jnp.sum(grad_hidden, axis=0)
    grad_hidden_b = grad_hidden.astype(jnp.bfloat16)
    fc1_grad = jnp.dot(whole2.T, grad_hidden_b, preferred_element_type=jnp.float32)
    grad_normed2 = jnp.dot(grad_hidden_b, fc1_back.T, preferred_element_type=jnp.float32)
    grad_out = (grad_attended * validity[:, None]).astype(jnp.bfloat16).reshape(length, -1, HD)
    grad_query, grad_key, grad_value = attend_back(
        queries, key_rows, value_rows, allowed, logsum, grad_out
    )
    grad_projected = jnp.stack(
        [
            rotate_back(grad_query, cos_table, sine_table),
            rotate_back(grad_key, cos_table, sine_table),
            grad_value,
        ],
        axis=2,
    )
    grad_projected = grad_projected.reshape(length, -1)
    qkv_bias_part = jnp.sum(grad_projected, axis=0)
    grad_projected_b = grad_projected.astype(jnp.bfloat16)
    qkv_grad = jnp.dot(whole1.T, grad_projected_b, preferred_element_type=jnp.float32)
    grad_normed1 = jnp.dot(grad_projected_b, qkv_back.T, preferred_element_type=jnp.float32)
    own_grad1, own_grad2 = (
        lax.psum_scatter(
            grad_normed1.astype(jnp.bfloat16), "tensor", scatter_dimension=0, tiled=True
        ).astype(jnp.float32),
        lax.psum_scatter(
            grad_normed2.astype(jnp.bfloat16), "tensor", scatter_dimension=0, tiled=True
        ).astype(jnp.float32),
    )
    back1, gain1, shift1 = normalize_back(own_grad1, ln1_gain, scaled1, spread1)
    back2, gain2, shift2 = normalize_back(own_grad2, ln2_gain, scaled2, spread2)
    input_grad = masked + back1 + back2
    qkv_owned, dense_owned, fc1_owned, fc2_owned = (
        lax.psum_scatter(qkv_grad, "dp", scatter_dimension=0, tiled=True),
        lax.psum_scatter(dense_grad, "dp", scatter_dimension=0, tiled=True),
        lax.psum_scatter(fc1_grad, "dp", scatter_dimension=0, tiled=True),
        lax.psum_scatter(fc2_grad, "dp", scatter_dimension=0, tiled=True),
    )
    qkv_bias_grad, fc1_bias_grad = lax.psum((qkv_bias_part, fc1_bias_part), "dp")
    gain1_sum, shift1_sum, gain2_sum, shift2_sum, out_bias_sum = lax.psum(
        (gain1, shift1, gain2, shift2, out_bias), ("dp", "tensor")
    )
    return (
        output,
        input_grad,
        gain1_sum,
        shift1_sum,
        gain2_sum,
        shift2_sum,
        qkv_owned,
        qkv_bias_grad,
        dense_owned,
        out_bias_sum,
        fc1_owned,
        fc1_bias_grad,
        fc2_owned,
        out_bias_sum,
    )


def solution(mesh):
    return jax.shard_map(
        on_device,
        mesh=mesh,
        in_specs=(
            P(("dp", "tensor"), None),
            P("dp"),
            P(),
            P(),
            P(),
            P(),
            P("dp", "tensor"),
            P("tensor"),
            P("dp", "tensor"),
            P(),
            P("dp", "tensor"),
            P("tensor"),
            P("dp", "tensor"),
            P(),
            P(("dp", "tensor"), None),
        ),
        out_specs=(
            P(("dp", "tensor"), None),
            P(("dp", "tensor"), None),
            P(),
            P(),
            P(),
            P(),
            P("dp", "tensor"),
            P("tensor"),
            P("dp", "tensor"),
            P(),
            P("dp", "tensor"),
            P("tensor"),
            P("dp", "tensor"),
            P(),
        ),
        check_vma=False,
    )
```

profile of v0, /device:TPU:0, one launch (start us, length us, event | category | flops | bytes accessed | tf_op | source)
XLA Modules:
  0.0 497.0 jit_solution(16422729326752073748)
XLA Ops:
  7.3 0.7 fusion.88
  8.0 1.8 fusion.67
  9.9 1.1 convert_reduce_fusion.3
  10.9 1.2 fusion.55
  12.1 2.0 fusion.46
  14.2 0.7 all-gather.9.cloned.1.call-update
  15.0 0.5 all-gather.11.cloned.1.call-update
  15.6 0.5 all-gather.13.cloned.1.call-update
  16.1 0.5 all-gather.15.cloned.1.call-update
  16.8 0.2 convert_reduce_fusion
  17.0 0.3 fusion.32
  17.4 11.3 %all_gather.27 = bf16[1024,256]{1,0:T(8,128)(2,1)S(1)} all-gather(bf16[128,256]{1,0:T(8,128)(2,1)S(1)} %copy-done.23), channel_id=1, replica_groups=mesh['dp'=8,'tensor'=4] {'dp'}, dimensions={0}, use_global_device_ids=true | all-gather | bytes 589824 | tf_op jit(solution)/shard_map/all_gather | solution.py:137
  28.8 12.1 %all-gather.17.cloned.1.call-done = bf16[512,1024]{1,0:T(8,128)(2,1)} async-done(((bf16[128,1024]{1,0:T(8,128)(2,1)}), bf16[512,1024]{1,0:T(8,128)(2,1)}) %all-gather.17.cloned.1.call-update) | async-done | bytes 1048592 | tf_op jit(solution)/shard_map/all_gather | solution.py:157
  40.8 1.7 fusion.25
  42.5 27.9 %all-gather.7.cloned.1.call-done = bf16[512,1024]{1,0:T(8,128)(2,1)} async-done(((bf16[128,1024]{1,0:T(8,128)(2,1)}), bf16[512,1024]{1,0:T(8,128)(2,1)}) %all-gather.7.cloned.1.call-update) | async-done | bytes 1048592 | tf_op jit(solution)/shard_map/all_gather | solution.py:132
  70.5 27.1 %all-gather.9.cloned.1.call-done = bf16[1024,768]{1,0:T(8,128)(2,1)} async-done(((bf16[128,768]{1,0:T(8,128)(2,1)}), bf16[1024,768]{1,0:T(8,128)(2,1)}) %all-gather.9.cloned.1.call-update) | async-done | bytes 1572880 | tf_op jit(solution)/shard_map/all_gather | solution.py:136
  97.6 3.9 convolution_add_fusion.1
  101.5 1.9 copy.45
  103.8 0.9 fusion.2
  104.8 0.9 exponential_reduce_fusion
  105.7 1.0 copy-done.6
  106.7 2.7 fusion.74
  109.5 7.4 %fusion.22 = f32[512,4,64]{0,2,1:T(8,128)S(1)} fusion(f32[4,512,512]{1,2,0:T(8,128)} %fusion.74, bf16[512,4,48]{0,2,1:T(8,128)(2,1)S(1)} %copy-done.22, bf16[512,4,16]{0,2,1:T(8,128)(2,1)S(1)} %copy-done.26, f32[4,512,512]{1,2,0:T(8,128)} %copy-done.6, f32[4,512]{1,0:T(4,128)S(1)} %log_add_fusion, pred[512,512]{0,1:T(8,128)(4,1)S(1)} %fusion.32), kind=kOutput, calls=%fused_computation.36 | convolution fusion | flops 146278912 | bytes 9445376 | tf_op jit(solution)/shard_map/hqk,qhd->khd/dot_general | solution.py:96
  116.9 9.6 %fusion.19 = f32[512,4,64]{0,2,1:T(8,128)} fusion(f32[4,512,512]{1,2,0:T(8,128)} %fusion.74, bf16[512,4,48]{0,2,1:T(8,128)(2,1)} %copy-done.20, bf16[512,4,16]{0,2,1:T(8,128)(2,1)} %copy-done.24, f32[4,512,512]{1,2,0:T(8,128)} %copy-done.6, f32[4,512]{1,0:T(4,128)S(1)} %log_add_fusion, pred[512,512]{0,1:T(8,128)(4,1)S(1)} %fusion.32), kind=kOutput, calls=%fused_computation.35 | convolution fusion | flops 146278912 | bytes 9445376 | tf_op jit(solution)/shard_map/hqk,khd->qhd/dot_general | solution.py:93
  126.6 1.2 slice.97
  127.7 1.1 slice_multiply_fusion.3
  128.9 1.0 maximum_add_fusion
  130.0 1.2 convolution_bitcast_fusion
  131.5 0.6 copy-done.11
  132.1 0.9 copy-done.8
  132.9 2.0 convolution_convert_fusion
  135.0 0.2 reduce-scatter.12.cloned.1.call-start
  135.3 21.5 %all-gather.13.cloned.1.call-done = bf16[1024,1024]{1,0:T(8,128)(2,1)} async-done(((bf16[128,1024]{1,0:T(8,128)(2,1)}), bf16[1024,1024]{1,0:T(8,128)(2,1)}) %all-gather.13.cloned.1.call-update) | async-done | bytes 2097168 | tf_op jit(solution)/shard_map/all_gather | solution.py:138
  156.7 4.5 fusion.92
  161.3 25.1 %all-gather.15.cloned.1.call-done = bf16[1024,1024]{1,0:T(8,128)(2,1)} async-done(((bf16[128,1024]{1,0:T(8,128)(2,1)}), bf16[1024,1024]{1,0:T(8,128)(2,1)}) %all-gather.15.cloned.1.call-update) | async-done | bytes 2097168 | tf_op jit(solution)/shard_map/all_gather | solution.py:139
  186.4 8.8 %fusion.86 = (f32[1024]{0:T(1024)S(1)}, bf16[512,1024]{1,0:T(8,128)(2,1)S(1)}, f32[512,1024]{1,0:T(8,128)}) fusion(f32[512,1024]{1,0:T(8,128)} %fusion.92, f32[1024]{0:T(1024)S(1)} %copy-done.35, bf16[512,1024]{1,0:T(8,128)(2,1)S(1)} %copy-done, bf16[1024,1024]{1,0:T(8,128)(2,1)} %all-gather.15.cloned.1.call-done), kind=kOutput, calls=%fused_computation.144 | convolution fusion | flops 1112538112 | bytes 8396800 | tf_op jit(solution)/shard_map/dot_general | solution.py:166
  195.2 1.0 copy-done.16
  196.1 2.3 convolution_convert_fusion.1
  198.5 3.5 fusion.26
  202.1 0.5 multiply_convert_fusion.1
  202.6 1.1 copy-done.38
  203.7 1.3 fusion.93
  205.0 1.9 convolution_add_fusion
  207.0 1.5 fusion.95
  208.6 4.2 fusion.94
  212.9 3.3 fusion.96
  216.1 0.3 reduce-scatter.18.cloned.1.call-start
  216.4 0.9 copy-done.13
  217.3 0.3 copy-done.17
  217.6 3.3 fusion.63
  221.0 1.0 copy-done.3
  222.0 0.2 copy-done.5
  222.1 0.2 copy-done.12
  222.3 0.2 fusion.27
  222.6 14.7 %all-reduce.1 = (f32[768]{0:T(1024)}, f32[1024]{0:T(1024)}) all-reduce(f32[768]{0:T(1024)S(1)} %reduce_sum.168, f32[1024]{0:T(1024)S(1)} %get-tuple-element.32), channel_id=1, replica_groups=mesh['dp'=8,'tensor'=4] {'dp'}, use_global_device_ids=true, to_apply=%region_23.24 | all-reduce | flops 1792 | bytes 14336 | tf_op jit(solution)/shard_map/psum | solution.py:207
  237.3 6.8 %reduce-scatter.12.cloned.1.call-done = bf16[128,1024]{1,0:T(8,128)(2,1)} async-done(((bf16[512,1024]{1,0:T(8,128)(2,1)}), bf16[128,1024]{1,0:T(8,128)(2,1)}) %reduce-scatter.12.cloned.1.call-update) | async-done | bytes 262160 | tf_op jit(solution)/shard_map/reduce_scatter | solution.py:194
  244.1 1.5 fusion.62
  245.6 43.3 %reduce-scatter.8.cloned.1.call-done = f32[128,1024]{1,0:T(8,128)} async-done(((f32[512,1024]{1,0:T(8,128)}), f32[128,1024]{1,0:T(8,128)}) %reduce-scatter.8.cloned.1.call-update) | async-done | bytes 524304 | tf_op jit(solution)/shard_map/reduce_scatter | solution.py:153
  288.9 2.5 fusion.66
  291.5 39.8 %all-reduce = (f32[1024]{0:T(1024)}, f32[1024]{0:T(1024)}, f32[1024]{0:T(1024)}, f32[1024]{0:T(1024)}, f32[1024]{0:T(1024)S(1)}) all-reduce(f32[1024]{0:T(1024)S(1)} %get-tuple-element.22, f32[1024]{0:T(1024)S(1)} %get-tuple-element.23, f32[1024]{0:T(1024)S(1)} %get-tuple-element.14, ...), channel_id=1, replica_groups=mesh['dp'=8,'tensor'=4] {'dp','tensor'}, use_global_device_ids=true, to_apply=%region_14.15 | all-reduce | flops 5120 | bytes 40960 | tf_op jit(solution)/shard_map/psum | solution.py:208
  331.3 47.8 %reduce-scatter.14.cloned.1.call-done = f32[128,768]{1,0:T(8,128)} async-done(((f32[1024,768]{1,0:T(8,128)}), f32[128,768]{1,0:T(8,128)}) %reduce-scatter.14.cloned.1.call-update) | async-done | bytes 393232 | tf_op jit(solution)/shard_map/reduce_scatter | solution.py:202
  379.1 55.1 %reduce-scatter.20.cloned.1.call-done = f32[128,1024]{1,0:T(8,128)} async-done(((f32[1024,1024]{1,0:T(8,128)}), f32[128,1024]{1,0:T(8,128)}) %reduce-scatter.20.cloned.1.call-update) | async-done | bytes 524304 | tf_op jit(solution)/shard_map/reduce_scatter | solution.py:205
  434.2 55.7 %reduce-scatter.18.cloned.1.call-done = f32[128,1024]{1,0:T(8,128)} async-done(((f32[1024,1024]{1,0:T(8,128)}), f32[128,1024]{1,0:T(8,128)}) %reduce-scatter.18.cloned.1.call-update) | async-done | bytes 524304 | tf_op jit(solution)/shard_map/reduce_scatter | solution.py:204
  489.9 0.6 copy.70
  (125 shorter events, 1.8 us)
Async XLA Ops:
  7.2 9.6 %copy-start.27 = (s32[512]{0:T(512)S(1)}, s32[512]{0:T(512)}, u32[]{:S(2)}) copy-start(s32[512]{0:T(512)} %param.16) | copy-start | bytes 6148
  7.2 10.2 %copy-start.23 = (bf16[128,256]{1,0:T(8,128)(2,1)S(1)}, bf16[128,256]{1,0:T(8,128)(2,1)}, u32[]{:S(2)}) copy-start(bf16[128,256]{1,0:T(8,128)(2,1)} %param.23) | copy-start | bytes 196612
  7.2 33.6 %all-gather.17.cloned.1.call-start = ((), (), s32[]{:S(2)}) async-start(), calls=%async_computation.13 | async-start | bytes 1310720 | tf_op jit(solution)/shard_map/all_gather | solution.py:157
  8.0 2.9 copy-start.36
  9.8 60.7 %all-gather.7.cloned.1.call-start = ((), (), s32[]{:S(2)}) async-start(), calls=%async_computation.7 | async-start | bytes 1310720 | tf_op jit(solution)/shard_map/all_gather | solution.py:132
  12.1 4.6 copy-start.30
  14.2 83.4 %copy-start.41 = (f32[768]{0:T(1024)S(1)}, f32[768]{0:T(1024)}, u32[]{:S(2)}) copy-start(f32[768]{0:T(1024)} %param.22) | copy-start | bytes 9220
  14.2 83.4 %all-gather.9.cloned.1.call-start = ((), (), s32[]{:S(2)}) async-start(), calls=%async_computation.8 | async-start | bytes 1769472 | tf_op jit(solution)/shard_map/all_gather | solution.py:136
  14.9 120.3 %all-gather.11.cloned.1.call-start = ((), (), s32[]{:S(2)}) async-start(), calls=%async_computation.9 | async-start | bytes 1310720 | tf_op jit(solution)/shard_map/all_gather | solution.py:133
  15.5 141.2 %all-gather.13.cloned.1.call-start = ((), (), s32[]{:S(2)}) async-start(), calls=%async_computation.10 | async-start | bytes 2359296 | tf_op jit(solution)/shard_map/all_gather | solution.py:138
  16.1 170.3 %all-gather.15.cloned.1.call-start = ((), (), s32[]{:S(2)}) async-start(), calls=%async_computation.11 | async-start | bytes 2359296 | tf_op jit(solution)/shard_map/all_gather | solution.py:139
  16.7 220.6 %reduce-scatter.10.cloned.1.call-start = ((), (), s32[]{:S(2)}) async-start(), calls=%async_computation.14 | async-start | bytes 1310720 | tf_op jit(solution)/shard_map/reduce_scatter | solution.py:191
  17.2 112.7 %copy-start.14 = (pred[512,512]{0,1:T(8,128)(4,1)}, pred[512,512]{0,1:T(8,128)(4,1)S(1)}, u32[]{:S(2)}) copy-start(pred[512,512]{0,1:T(8,128)(4,1)S(1)} %fusion.32) | copy-start | bytes 786436
  17.4 86.3 %copy-start.18 = (f32[512,16]{0,1:T(8,128)}, f32[512,16]{0,1:T(8,128)S(1)}, u32[]{:S(2)}) copy-start(f32[512,16]{0,1:T(8,128)S(1)} %get-tuple-element.58) | copy-start | bytes 98308
  17.4 86.3 %copy-start.19 = (f32[512,16]{0,1:T(8,128)}, f32[512,16]{0,1:T(8,128)S(1)}, u32[]{:S(2)}) copy-start(f32[512,16]{0,1:T(8,128)S(1)} %get-tuple-element.59) | copy-start | bytes 98308
  103.6 1.1 copy-start.20
  103.7 1.0 copy-start.21
  103.8 1.0 copy-start.24
  103.8 1.0 copy-start.25
  104.7 2.0 copy-start.6
  106.7 2.8 copy-start.22
  106.7 2.8 copy-start.26
  126.5 3.4 copy-start.7
  129.9 1.3 copy-start.2
  130.0 1.3 copy-start.4
  131.3 0.8 copy-start.11
  131.3 1.7 copy-start.40
  132.1 0.9 copy-start.8
  135.0 51.4 %copy-start = (bf16[512,1024]{1,0:T(8,128)(2,1)S(1)}, bf16[512,1024]{1,0:T(8,128)(2,1)}, u32[]{:S(2)}) copy-start(bf16[512,1024]{1,0:T(8,128)(2,1)} %all-gather.17.cloned.1.call-done) | copy-start | bytes 3145732
  135.0 51.4 %copy-start.35 = (f32[1024]{0:T(1024)S(1)}, f32[1024]{0:T(1024)}, u32[]{:S(2)}) copy-start(f32[1024]{0:T(1024)} %param.26) | copy-start | bytes 12292
  135.0 109.1 %reduce-scatter.12.cloned.1.call-start = ((), (), s32[]{:S(2)}) async-start(), calls=%async_computation.15 | async-start | bytes 1310720 | tf_op jit(solution)/shard_map/reduce_scatter | solution.py:194
  186.4 9.8 %copy-start.39 = (bf16[1024,1024]{1,0:T(8,128)(2,1)S(1)}, bf16[1024,1024]{1,0:T(8,128)(2,1)}, u32[]{:S(2)}) copy-start(bf16[1024,1024]{1,0:T(8,128)(2,1)} %all-gather.13.cloned.1.call-done) | copy-start | bytes 6291460
  195.2 1.0 copy-start.16
  198.5 90.5 %reduce-scatter.8.cloned.1.call-start = ((), (), s32[]{:S(2)}) async-start(), calls=%async_computation.12 | async-start | bytes 2621440 | tf_op jit(solution)/shard_map/reduce_scatter | solution.py:153
  198.5 3.6 copy-start.9
  198.5 3.6 copy-start.10
  202.1 1.6 copy-start.38
  207.0 124.3 %reduce-scatter.16.cloned.1.call-start = ((), (), s32[]{:S(2)}) async-start(), calls=%async_computation.17 | async-start | bytes 1179648 | tf_op jit(solution)/shard_map/reduce_scatter | solution.py:203
  208.5 170.6 %reduce-scatter.14.cloned.1.call-start = ((), (), s32[]{:S(2)}) async-start(), calls=%async_computation.16 | async-start | bytes 3538944 | tf_op jit(solution)/shard_map/reduce_scatter | solution.py:202
  212.8 221.4 %reduce-scatter.20.cloned.1.call-start = ((), (), s32[]{:S(2)}) async-start(), calls=%async_computation.19 | async-start | bytes 4718592 | tf_op jit(solution)/shard_map/reduce_scatter | solution.py:205
  216.1 1.2 copy-start.13
  216.1 1.5 copy-start.17
  216.1 273.7 %reduce-scatter.18.cloned.1.call-start = ((), (), s32[]{:S(2)}) async-start(), calls=%async_computation.18 | async-start | bytes 4718592 | tf_op jit(solution)/shard_map/reduce_scatter | solution.py:204
  220.9 1.0 copy-start.3
  220.9 1.2 copy-start.5
  220.9 1.4 copy-start.12
  220.9 23.2 %copy-start.1 = (bf16[128,1024]{1,0:T(8,128)(2,1)S(1)}, bf16[128,1024]{1,0:T(8,128)(2,1)}, u32[]{:S(2)}) copy-start(bf16[128,1024]{1,0:T(8,128)(2,1)} %param.15) | copy-start | bytes 786436
  220.9 23.2 %copy-start.28 = (f32[1024]{0:T(1024)S(1)}, f32[1024]{0:T(1024)}, u32[]{:S(2)}) copy-start(f32[1024]{0:T(1024)} %param.17) | copy-start | bytes 12292
  220.9 23.1 %copy-start.29 = (f32[1024]{0:T(1024)S(1)}, f32[1024]{0:T(1024)}, u32[]{:S(2)}) copy-start(f32[1024]{0:T(1024)} %param.19) | copy-start | bytes 12292
  221.0 23.1 %copy-start.31 = (f32[128]{0:T(128)S(1)}, f32[128]{0:T(128)}, u32[]{:S(2)}) copy-start(f32[128]{0:T(128)} %copy-done.30) | copy-start | bytes 1540
  222.3 66.6 %copy-start.15 = (bf16[128,1024]{1,0:T(8,128)(2,1)S(1)}, bf16[128,1024]{1,0:T(8,128)(2,1)}, u32[]{:S(2)}) copy-start(bf16[128,1024]{1,0:T(8,128)(2,1)} %param.29) | copy-start | bytes 786436
  222.3 66.6 %copy-start.32 = (f32[1024]{0:T(1024)S(1)}, f32[1024]{0:T(1024)}, u32[]{:S(2)}) copy-start(f32[1024]{0:T(1024)} %param.28) | copy-start | bytes 12292
  222.3 66.6 %copy-start.33 = (f32[1024]{0:T(1024)S(1)}, f32[1024]{0:T(1024)}, u32[]{:S(2)}) copy-start(f32[1024]{0:T(1024)} %param.24) | copy-start | bytes 12292
  222.3 66.6 %copy-start.37 = (f32[128]{0:T(128)S(1)}, f32[128]{0:T(128)}, u32[]{:S(2)}) copy-start(f32[128]{0:T(128)} %copy-done.36) | copy-start | bytes 1540
  331.3 159.2 %copy-start.34 = (f32[1024]{0:T(1024)}, f32[1024]{0:T(1024)S(1)}, u32[]{:S(2)}) copy-start(f32[1024]{0:T(1024)S(1)} %get-tuple-element.94) | copy-start | bytes 12292
Sparse Core Ops, SparseCore 0:
  10.2 30.6 all-gather.16
  43.0 27.4 all-gather.6
  72.4 25.1 all-gather.8
  99.6 27.9 all-gather.10
  129.3 27.3 all-gather.12
  158.5 27.8 all-gather.14
  188.7 27.1 reduce-scatter.9
  218.3 25.7 reduce-scatter.11
  246.4 42.4 reduce-scatter.7
  292.8 35.4 reduce-scatter.15
  332.7 46.3 reduce-scatter.13
  382.9 51.2 reduce-scatter.19
  438.5 51.3 reduce-scatter.17
where the time goes:
time: 498 us; the launch traced here: 497 us
  waiting for transfers between devices  325 us (65%)
  blocking collectives  65.8 us (13%)
  matrix products  64.1 us (13%)
  other arithmetic  15.5 us (3%)
  between operations  14.5 us (3%)
  local copies, waits for them, and re-layouts  11.4 us (2%)
    reduce_scatter x1, waiting for transfers between devices, on_device(): lax.psum_scatter(fc1_grad, 'dp', scatter_dimension=0, tiled=True)  55.7 us
    reduce_scatter x1, waiting for transfers between devices, on_device(): lax.psum_scatter(fc2_grad, 'dp', scatter_dimension=0, tiled=True)  55.1 us
    reduce_scatter x1, waiting for transfers between devices, on_device(): lax.psum_scatter(qkv_grad, 'dp', scatter_dimension=0, tiled=True)  47.8 us
    reduce_scatter x1, waiting for transfers between devices, on_device(): summed = lax.psum_scatter(branch, 'tensor', scatter_dimension=0, tiled=True)  43.3 us
    psum x1, blocking collectives, on_device(): lax.psum((gain1, shift1, gain2, shift2, out_bias), ('dp', 'tensor'))  39.8 us
    all_gather x1, waiting for transfers between devices, on_device(): lax.all_gather(normed1, 'tensor', axis=0, tiled=True)  27.9 us
    all_gather x1, waiting for transfers between devices, on_device(): lax.all_gather(qkv_weight, 'dp', axis=0, tiled=True)  27.1 us
    all_gather x1, waiting for transfers between devices, on_device(): lax.all_gather(fc2_weight, 'dp', axis=0, tiled=True)  25.1 us
  transfers between devices with their start and end apart: 13, of which 10 were waited for; matrix products, arithmetic and copies ran while one was open for 16% of the time, Pallas kernels for 0%

commit v1 on v0

v1 whole, which is shorter than its diff:
```python
from functools import partial

import jax
import jax.numpy as jnp
from jax import lax
from jax.experimental import pallas as pl
from jax.experimental.pallas import tpu as pltpu
from jax.sharding import PartitionSpec as P

HD = 64
ROT = 16
EPS = 1e-05
BF = jnp.bfloat16
F32 = jnp.float32
CHUNK = 64
ANY = pl.BlockSpec(memory_space=pl.ANY)
VMEM = pl.BlockSpec(memory_space=pltpu.VMEM)
SMEM = pl.BlockSpec(memory_space=pltpu.SMEM)
VMEM_LIMIT = 16 * 1024 * 1024
PEAK = 1.15e9
LITTLE = 0.01


def dot(a, b):
    return jnp.dot(a, b, preferred_element_type=F32)


def dot_nt(a, b):
    return lax.dot_general(a, b, (((1,), (1,)), ((), ())), preferred_element_type=F32)


def dot_tn(a, b):
    return lax.dot_general(a, b, (((0,), (0,)), ((), ())), preferred_element_type=F32)


def shape(dims, dtype):
    return jax.ShapeDtypeStruct(dims, dtype)


def kernel_call(body, name, outs, operands, scratch, micros, fetched=(), placed=False):
    return pl.pallas_call(
        body,
        name=name,
        out_shape=outs,
        in_specs=[SMEM] + [VMEM] * (len(operands) - 1) + [ANY] * len(fetched),
        out_specs=[ANY if placed else VMEM] * len(outs),
        scratch_shapes=scratch,
        cost_estimate=pl.CostEstimate(
            flops=int(micros * PEAK), bytes_accessed=0, transcendentals=0
        ),
        compiler_params=pltpu.CompilerParams(vmem_limit_bytes=VMEM_LIMIT),
    )(*operands, *fetched)


def start_all(pairs, sems, first=0):
    copies = [
        pltpu.make_async_copy(src, dst, sems.at[first + i]) for i, (src, dst) in enumerate(pairs)
    ]
    for one in copies:
        one.start()
    return copies


def wait_all(copies):
    for one in copies:
        one.wait()


def rows_at(start, size):
    return pl.ds(pl.multiple_of(start, size), size)


def shard_rows(place, tz, rows, i):
    return i // tz * tz * rows + (place[1] ^ (i % tz)) * rows


def weight_rows(place, size, i):
    return (i - i % 2 + (place[0] ^ (i % 2))) * size


def rotated(values, cos_table, sine_table):
    lane = lax.broadcasted_iota(jnp.int32, values.shape, 1)
    lanes = values.shape[1]
    turned = jnp.where(
        lane % ROT < ROT // 2,
        pltpu.roll(values, lanes - ROT // 2, 1),
        pltpu.roll(values, ROT // 2, 1),
    )
    return values * cos_table + turned * sine_table


def head_mask(value, head, heads):
    lane = lax.broadcasted_iota(jnp.int32, value.shape, 1)
    return (lane // (value.shape[1] // heads)) == head


def allowed_block(first_row, rows, keys, lower):
    row = lax.broadcasted_iota(jnp.int32, (rows, keys), 0) + first_row
    col = lax.broadcasted_iota(jnp.int32, (rows, keys), 1)
    return (col <= row) & (col >= lower)


def store_shards(place, tz, outs, group, cols, value):
    rows = value.shape[0] // tz
    for b in range(tz):
        outs[group][rows_at((place[1] ^ b) * rows, rows), cols] = value[
            b * rows : (b + 1) * rows
        ].astype(BF)


def forward_body(tz, dp, count, sizes, *refs):
    length, width, nq, nf, nd = sizes
    heads = nd // HD
    place, table, gains, shift_qkv, shift_fc1 = refs[:5]
    at = 5
    shards, pieces_w = refs[at : at + 2 * tz], refs[at + 2 * tz : at + 2 * tz + count]
    at += 2 * tz + count
    out_own, out_sib, x, cot, w, n1, n2, qkv, lse, aa, dgelu, stats = refs[at : at + 12]
    hid, x_sems, w_sems, cot_sems = refs[at + 12 :]
    rows = length // tz
    size = width // dp
    x_in = start_all(
        [
            (one.at[0:rows], x.at[rows_at(shard_rows(place, tz, rows, i), rows)])
            for i, one in enumerate(shards)
        ],
        x_sems,
    )
    parts_w = [
        one.at[j * size : (j + 1) * size] for one in pieces_w for j in range(one.shape[0] // size)
    ]
    w_in = start_all(
        [(one, w.at[rows_at(weight_rows(place, size, i), size)]) for i, one in enumerate(parts_w)],
        w_sems,
    )
    cot_in = start_all(
        [
            (one.at[rows : 2 * rows], cot.at[rows_at(shard_rows(place, tz, rows, i), rows)])
            for i, one in enumerate(shards)
        ],
        cot_sems,
    )
    for i in range(2 * tz):
        x_in[i].wait()
        start = shard_rows(place, tz, rows, i)

        def norm_rows(j, _):
            there = rows_at(start + j * CHUNK, CHUNK)
            value = x[there, :].astype(F32)
            mean = jnp.mean(value, axis=1, keepdims=True)
            center = value - mean
            spread = lax.rsqrt(jnp.mean(center * center, axis=1, keepdims=True) + EPS)
            scaled = center * spread
            n1[there, :] = (scaled * gains[0:1, :] + gains[1:2, :]).astype(BF)
            n2[there, :] = (scaled * gains[2:3, :] + gains[3:4, :]).astype(BF)
            lane = lax.broadcasted_iota(jnp.int32, (CHUNK, 128), 1)
            stats[there, :] = jnp.where(lane == 0, mean, spread)
            return 0

        lax.fori_loop(0, rows // CHUNK, norm_rows, 0)
    wait_all(w_in)
    for g in range(2):
        group = slice(g * length, (g + 1) * length)
        cos_table, sine_table = table[group, 0:nd], table[group, nd : 2 * nd]
        projected = dot(n1[group, :], w[:, 0:nq]) + shift_qkv[...]
        qkv[group, 0:nd] = rotated(projected[:, 0:nd], cos_table, sine_table).astype(BF)
        qkv[group, nd : 2 * nd] = rotated(projected[:, nd : 2 * nd], cos_table, sine_table).astype(
            BF
        )
        qkv[group, 2 * nd : 3 * nd] = projected[:, 2 * nd : 3 * nd].astype(BF)
        hid[...] = dot(n2[group, :], w[:, nq : nq + nf]) + shift_fc1[...]

        def gelu_rows(i, _):
            here = rows_at(i * CHUNK, CHUNK)
            there = rows_at(g * length + i * CHUNK, CHUNK)
            h = hid[here, :]
            phi = 0.5 * (1.0 + lax.erf(h * 0.7071067811865476))
            aa[there, nd : nd + nf] = (h * phi).astype(BF)
            dgelu[there, :] = (phi + h * (0.3989422804014327 * jnp.exp(-0.5 * h * h))).astype(BF)
            return 0

        lax.fori_loop(0, length // CHUNK, gelu_rows, 0)

        half = length // 2
        for block in range(2):
            keys = (block + 1) * half
            q_rows = slice(g * length + block * half, g * length + (block + 1) * half)
            k_rows = slice(g * length, g * length + keys)
            q = qkv[q_rows, 0:nd]
            k = qkv[k_rows, nd : 2 * nd]
            v = qkv[k_rows, 2 * nd : 3 * nd]
            lower = table[q_rows, 2 * nd : 2 * nd + 1].astype(jnp.int32)
            allowed = allowed_block(block * half, half, keys, lower)
            gathered = jnp.zeros((half, nd), F32)
            kept = jnp.zeros((half, 128), F32)
            lane = lax.broadcasted_iota(jnp.int32, (half, 128), 1)
            for h in range(heads):
                mine = head_mask(q, h, heads)
                scores = dot_nt(jnp.where(mine, q, jnp.zeros_like(q)), k) * HD ** (-0.5)
                scores = jnp.where(allowed, scores, -jnp.inf)
                top = jnp.max(scores, axis=1, keepdims=True)
                raised = jnp.exp(scores - top)
                total = jnp.sum(raised, axis=1, keepdims=True)
                soft = (raised * (1.0 / total)).astype(BF)
                gathered = jnp.where(mine, dot(soft, v), gathered)
                kept = jnp.where(lane == h, top + jnp.log(total), kept)
            valid = table[q_rows, 2 * nd + 64 : 2 * nd + 65]
            aa[q_rows, 0:nd] = (gathered * valid).astype(BF)
            lse[q_rows, :] = kept

        quarter = width // 4
        for part in range(4):
            cols = slice(part * quarter, (part + 1) * quarter)
            value = dot_nt(aa[group, :], w[cols, nq + nf :])
            store_shards(place, tz, (out_own, out_sib), g, cols, value)
    wait_all(cot_in)


def second_grads_body(dp, packets, place, aa, cot, *outs):
    grads_out(dp, packets, place, outs, lambda cols: dot_tn(cot[:, cols], aa[...]))


def first_grads_body(dp, packets, nq, place, n1, n2, gg, *outs):
    grads_out(
        dp,
        packets,
        place,
        outs,
        lambda cols: jnp.concatenate(
            [dot_tn(n1[:, cols], gg[:, 0:nq]), dot_tn(n2[:, cols], gg[:, nq:])], axis=1
        ),
    )


def grads_out(dp, packets, place, outs, product):
    size = outs[0].shape[0]
    slots = {i: (out, slot) for out, packet in zip(outs, packets) for slot, i in enumerate(packet)}
    for r in range(dp // 2):
        value = product(slice(2 * r * size, (2 * r + 2) * size)).astype(BF)
        low, high = value[0:size], value[size : 2 * size]
        first = place[0] == 0
        for i, (one, two) in ((2 * r, (low, high)), (2 * r + 1, (high, low))):
            out, slot = slots[i]
            out[slot * size : (slot + 1) * size, :] = jnp.where(first, one, two)


def backward_body(tz, sizes, *refs):
    length, width, nq, nf, nd = sizes
    heads = nd // HD
    place, table, gains, cot, w, qkv, lse, dgelu, stats, x = refs[:10]
    out_own, out_sib, gg, sums, bias_sums = refs[10:15]
    gact, g1, g2, acc, dk, dv = refs[15:]
    rows = length // tz
    acc[...] = jnp.zeros_like(acc)
    bias_sums[...] = jnp.zeros_like(bias_sums)
    for g in range(2):
        group = slice(g * length, (g + 1) * length)
        both = dot(cot[group, :], w[:, nq + nf :])
        grad_out = both[:, 0:nd].astype(BF)
        gact[...] = both[:, nd:]

        def hidden_rows(i, total):
            there = rows_at(g * length + i * CHUNK, CHUNK)
            value = gact[rows_at(i * CHUNK, CHUNK), :] * dgelu[there, :].astype(F32)
            gg[there, nq : nq + nf] = value.astype(BF)
            return total + jnp.sum(value.reshape(CHUNK // 8, 8, nf), axis=0)

        total = lax.fori_loop(0, length // CHUNK, hidden_rows, jnp.zeros((8, nf), F32))
        bias_sums[:, nq : nq + nf] += total

        half = length // 2
        dk[...] = jnp.zeros_like(dk)
        dv[...] = jnp.zeros_like(dv)
        for block in range(2):
            keys = (block + 1) * half
            q_rows = slice(g * length + block * half, g * length + (block + 1) * half)
            k_rows = slice(g * length, g * length + keys)
            q = qkv[q_rows, 0:nd]
            k = qkv[k_rows, nd : 2 * nd]
            v = qkv[k_rows, 2 * nd : 3 * nd]
            go = grad_out[block * half : (block + 1) * half]
            lower = table[q_rows, 2 * nd : 2 * nd + 1].astype(jnp.int32)
            allowed = allowed_block(block * half, half, keys, lower)
            dq = jnp.zeros((half, nd), F32)
            for h in range(heads):
                mine = head_mask(q, h, heads)
                zero = jnp.zeros_like(q)
                q_h = jnp.where(mine, q, zero)
                go_h = jnp.where(mine, go, zero)
                scores = dot_nt(q_h, k) * HD ** (-0.5)
                probs = jnp.exp(jnp.where(allowed, scores - lse[q_rows, h : h + 1], -jnp.inf))
                grad_soft = dot_nt(go_h, v)
                inner = jnp.sum(probs * grad_soft, axis=1, keepdims=True)
                grad_scores = (probs * (grad_soft - inner) * HD ** (-0.5)).astype(BF)
                dq = jnp.where(mine, dot(grad_scores, k), dq)
                dk[0:keys, :] += dot_tn(grad_scores, q_h)
                dv[0:keys, :] += dot_tn(probs.astype(BF), go_h)
            grads_q = rotated(dq, table[q_rows, 0:nd], -table[q_rows, nd : 2 * nd])
            gg[q_rows, 0:nd] = grads_q.astype(BF)
            bias_sums[:, 0:nd] += jnp.sum(grads_q.reshape(half // 8, 8, nd), axis=0)
        grads_k = rotated(dk[...], table[group, 0:nd], -table[group, nd : 2 * nd])
        gg[group, nd : 2 * nd] = grads_k.astype(BF)
        gg[group, 2 * nd : 3 * nd] = dv[...].astype(BF)
        bias_sums[:, nd : 2 * nd] += jnp.sum(grads_k.reshape(length // 8, 8, nd), axis=0)
        bias_sums[:, 2 * nd : 3 * nd] += jnp.sum(dv[...].reshape(length // 8, 8, nd), axis=0)

        quarter = width // 4
        for part in range(4):
            cols = slice(part * quarter, (part + 1) * quarter)
            g1[:, cols] = dot_nt(gg[group, 0:nq], w[cols, 0:nq])
            g2[:, cols] = dot_nt(gg[group, nq:], w[cols, nq : nq + nf])

        out = (out_own, out_sib)[g]
        for r in range(tz):
            start = (place[1] ^ r) * rows

            def back_rows(j, _):
                inside = rows_at(start + j * CHUNK, CHUNK)
                there = rows_at(g * length + start + j * CHUNK, CHUNK)
                scaled = (x[there, :].astype(F32) - stats[there, 0:1]) * stats[there, 1:2]
                one, two = g1[inside, :], g2[inside, :]

                def add(slot, value):
                    acc[slot] += jnp.sum(value.reshape(CHUNK // 8, 8, width), axis=0)

                add(0, one * scaled)
                add(1, one)
                add(2, two * scaled)
                add(3, two)
                out[rows_at(r * rows + j * CHUNK, CHUNK), :] = (
                    one * gains[0:1, :] + two * gains[2:3, :]
                ).astype(BF)
                return 0

            lax.fori_loop(0, rows // CHUNK, back_rows, 0)
    for i in range(4):
        sums[i : i + 1, :] = jnp.sum(acc[i], axis=0, keepdims=True)


def combine_body(tz, place, own, other, *outs):
    rows = own.shape[0] // tz
    for r, out in enumerate(outs):
        at = slice(r * rows, (r + 1) * rows)
        out[...] = (own[at, :].astype(F32) + other[at, :].astype(F32)).astype(out.dtype)


def by_kind(values, heads):
    parts = [
        values[..., (h * 3 + kind) * HD : (h * 3 + kind + 1) * HD]
        for kind in range(3)
        for h in range(heads)
    ]
    return jnp.concatenate(parts, axis=-1)


def by_head(values, heads):
    parts = [
        values[..., (kind * heads + h) * HD : (kind * heads + h + 1) * HD]
        for h in range(heads)
        for kind in range(3)
    ]
    return jnp.concatenate(parts, axis=-1)


def pack_body(sizes, place, qkv_in, fc1_in, dense_in, fc2_in, kept, given, *scratch):
    nq, nf, nd = sizes
    qkv, fc1, dense, fc2, sems = scratch
    wait_all(
        start_all([(qkv_in, qkv), (fc1_in, fc1), (dense_in, dense), (fc2_in, fc2)], sems)
    )
    for out, which in ((given, 1 - place[0]), (kept, place[0])):

        def half(ref, size):
            return ref[:, pl.ds(pl.multiple_of(which * size, size), size)]

        out[:, 0:nq] = by_kind(half(qkv, nq), nd // HD)
        out[:, nq : nq + nf] = half(fc1, nf)
        out[:, nq + nf : nq + nf + nd] = half(dense, nd)
        out[:, nq + nf + nd :] = half(fc2, nf)


def halves_body(place, one, two, first, last, sems):
    size = one.shape[0] // 2
    wait_all(start_all([(one.at[0:size], first), (two.at[size : 2 * size], last)], sems))


def messages_body(place, to_x, to_y, from_y, from_x, out_x, out_y):
    size = to_x.shape[0]
    out_x[...] = to_x[...] + from_y[size : 2 * size, :]
    out_y[...] = to_y[...] + from_x[size : 2 * size, :]


def split_body(tz, place, own, other, mine, from_x, from_y, *outs):
    combine_body(tz, place, own, other, *outs[:tz])
    shard_sum(mine, from_x, from_y, outs[tz])


def shard_sum(mine, first, second, out):
    size = out.shape[0]
    out[...] = (
        mine[...].astype(F32) + first[0:size, :].astype(F32) + second[...].astype(F32)
    ).astype(BF)


def relay_body(place, shard, passed, to_x, to_y, from_y, from_x, sums, others, *outs):
    out_shard, out_x, out_y, out_sums = outs
    keep = (place[2] == 1).astype(F32)
    out_shard[...] = (shard[...].astype(F32) + keep * passed[...].astype(F32)).astype(BF)
    messages_body(place, to_x, to_y, from_y, from_x, out_x, out_y)
    out_sums[...] = sums[...] + others[...]


def finish_body(place, own, first, second, across, rows, mine, from_x, from_y, sums, others, *outs):
    out_rows, out_shard, out_sums = outs
    size = own.shape[0]
    keep = (place[2] == 1).astype(F32)
    back = (
        own[...]
        + first[...].astype(F32)
        + second[...].astype(F32)
        + keep * across[...].astype(F32)
    )
    value = rows[0:size, :].astype(F32)
    center = value - jnp.mean(value, axis=1, keepdims=True)
    spread = lax.rsqrt(jnp.mean(center * center, axis=1, keepdims=True) + EPS)
    scaled = center * spread
    out_rows[...] = rows[size : 2 * size, :].astype(F32) + spread * (
        back
        - jnp.mean(back, axis=1, keepdims=True)
        - scaled * jnp.mean(back * scaled, axis=1, keepdims=True)
    )
    shard_sum(mine, from_x, from_y, out_shard)
    out_sums[...] = sums[...] + others[...]


def join_body(heads, widths, count, place, *refs):
    parts, other, outs = refs[:count], refs[count], refs[count + 1 :]
    rows = other.shape[0]
    total = parts[0][0:rows, :].astype(F32)
    for one in parts[1:]:
        total = total + one[0:rows, :].astype(F32)
    for half, which in ((total, place[0]), (other[...].astype(F32), 1 - place[0])):
        at = 0
        for i, (out, size) in enumerate(zip(outs, widths)):
            value = half[:, at : at + size]
            if i == 0 and heads:
                value = by_head(value, heads)
            out[:, pl.ds(pl.multiple_of(which * size, size), size)] = value
            at += size


def xor_pairs(size, flip):
    return [(i, i ^ flip) for i in range(size)]


def on_device(
    dp,
    tz,
    inputs,
    segment_ids,
    ln1_gain,
    ln1_bias,
    ln2_gain,
    ln2_bias,
    qkv_weight,
    qkv_bias,
    dense_weight,
    dense_bias,
    fc1_weight,
    fc1_bias,
    fc2_weight,
    fc2_bias,
    cotangent,
):
    rows, width = inputs.shape
    length = segment_ids.shape[0]
    tokens = 2 * length
    chips = dp // 2
    here = lax.axis_index("dp")
    core = here % 2
    chip = here // 2
    tensor = lax.axis_index("tensor")
    step = width // chips
    nq, nf, nd = qkv_weight.shape[1] // 2, fc1_weight.shape[1] // 2, dense_weight.shape[1] // 2
    wide = nq + nf + nd + nf
    heads = nd // HD
    sizes = (length, width, nq, nf, nd)
    middle = (tensor == 1) | (tensor == 2)
    place = jnp.stack([core, tensor, middle]).astype(jnp.int32)

    def turn(values):
        parts = [
            lax.dynamic_slice_in_dim(values, (chip ^ r) * step, step, axis=values.ndim - 1)
            for r in range(chips)
        ]
        return jnp.concatenate(parts, axis=-1)

    def sibling(values):
        return lax.ppermute(values, "dp", xor_pairs(dp, 1))

    def over_chip(values, flip):
        return lax.ppermute(values, "dp", xor_pairs(dp, 2 * flip))

    def over_tensor(values, flip):
        return lax.ppermute(values, "tensor", xor_pairs(tz, flip))

    def together(*values):
        return lax.optimization_barrier(values)

    def after(values, event):
        return lax.optimization_barrier((values, event))[0]

    def over_middle(values):
        return lax.ppermute(values, "tensor", [(0, 0), (1, 2), (2, 1), (3, 3)])

    def add_sibling(place, own, other):
        dtypes = [F32] + [BF] * (tz - 1)
        return kernel_call(
            partial(combine_body, tz),
            "add_sibling",
            [shape((rows, width), d) for d in dtypes],
            (place, own, other),
            [],
            LITTLE,
        )

    def added(parts):
        total = parts[0]
        for one in parts[1:]:
            total = total + one.astype(F32)
        return total

    def gather(kept, given, own_rows):
        given, own_rows = together(sibling(given), own_rows)
        if chips != 4 or tz != 4:
            blocks = [(kept, given)]
            flip = 1
            while flip < chips:
                blocks = blocks + [(over_chip(a, flip), over_chip(b, flip)) for a, b in blocks]
                flip *= 2
            shards = [own_rows] + [over_tensor(own_rows, r) for r in range(1, tz)]
            return [one for block in blocks for one in block], shards + [
                sibling(one) for one in shards
            ]
        pair = jnp.concatenate([kept, given], axis=0)
        second, first, from_x, from_y, sib_own = together(
            over_tensor(own_rows, 2),
            over_tensor(own_rows, 1),
            over_chip(pair, 1),
            over_chip(pair, 2),
            sibling(own_rows),
        )
        to_y, to_x = kernel_call(
            halves_body,
            "halves",
            [shape(kept.shape, BF)] * 2,
            (place,),
            [pltpu.SemaphoreType.DMA((2,))],
            LITTLE,
            (from_x, from_y),
            True,
        )
        across, relayed, far_own, far_other, sib_second = together(
            over_middle(own_rows),
            over_tensor(second, 1),
            over_chip(to_y, 2),
            over_chip(to_x, 1),
            sibling(second),
        )
        third = jnp.where(middle, across, relayed)
        return [kept, given, from_x, from_y, far_own, far_other], [
            own_rows,
            first,
            second,
            third,
            sib_own,
            sibling(first),
            sib_second,
            sibling(third),
        ]

    rounds = chips == 4 and tz == 4
    packets = [[0], [1], [4, 6], [3, 7], [2], [5]] if rounds else [[i] for i in range(dp)]

    def first_round(parts):
        if rounds:
            return [over_chip(parts[2], 2), over_chip(parts[3], 1)]
        return []

    def chip_sums(parts):
        blocks = [(parts[2 * r], parts[2 * r + 1]) for r in range(chips)]
        flip = chips // 2
        while flip:
            blocks = [
                tuple(
                    (a.astype(F32) + over_chip(b, flip).astype(F32)).astype(BF)
                    for a, b in zip(blocks[r], blocks[r + flip])
                )
                for r in range(flip)
            ]
            flip //= 2
        return blocks[0]

    def join(terms, other, widths, own_heads):
        return kernel_call(
            partial(join_body, own_heads, widths, len(terms)),
            "join_halves",
            [shape((width // dp, 2 * one), F32) for one in widths],
            (place, *terms, other),
            [],
            LITTLE,
        )

    def half_of(values, which):
        size = values.shape[-1] // 2
        return lax.dynamic_slice_in_dim(values, which * size, size, axis=values.ndim - 1)


    kept, given = kernel_call(
        partial(pack_body, (nq, nf, nd)),
        "pack_weights",
        [shape((width // dp, wide), BF)] * 2,
        (place,),
        [
            pltpu.VMEM(one.shape, BF) for one in (qkv_weight, fc1_weight, dense_weight, fc2_weight)
        ]
        + [pltpu.SemaphoreType.DMA((4,))],
        LITTLE,
        (qkv_weight, fc1_weight, dense_weight, fc2_weight),
    )

    own_rows = turn(after(inputs, kept))
    own_validity = lax.dynamic_slice_in_dim(segment_ids, tensor * rows, rows) >= 0
    masked = jnp.where(own_validity[:, None], turn(cotangent), jnp.zeros((), BF))
    weights, shards = gather(kept, given, jnp.concatenate([own_rows, masked], axis=0))

    both_ids = jnp.stack([segment_ids, sibling(segment_ids)])
    earlier = (both_ids[:, None, :] >= 0) & (both_ids[:, None, :] < both_ids[:, :, None])
    begins = jnp.sum(earlier.astype(jnp.int32), axis=2).reshape(tokens)
    flat_ids = both_ids.reshape(tokens)
    index = jnp.arange(tokens, dtype=jnp.int32) % length
    position = (index - begins).astype(F32)
    lane = jnp.arange(nd, dtype=jnp.int32) % HD
    half_rot = ROT // 2
    frequency = jnp.where(
        lane < ROT, 10000.0 ** (-2.0 * (lane % half_rot).astype(F32) / ROT), 0.0
    )
    angles = position[:, None] * frequency[None, :]
    sign = jnp.where(lane < half_rot, -1.0, 1.0)
    lower = jnp.where(flat_ids >= 0, begins, index).astype(F32)
    valid = (flat_ids >= 0).astype(F32)
    last = jnp.where(jnp.arange(128)[None, :] < 64, lower[:, None], valid[:, None])
    table = jnp.concatenate([jnp.cos(angles), jnp.sin(angles) * sign, last], axis=1)

    gains = turn(jnp.stack([ln1_gain, ln1_bias, ln2_gain, ln2_bias]))
    shift_qkv = by_kind(half_of(qkv_bias, core), heads)[None, :]
    shift_fc1 = half_of(fc1_bias, core)[None, :]

    part_own, part_sib, x, cot, w, n1, n2, qkv, lse, aa, dgelu, stats = kernel_call(
        partial(forward_body, tz, dp, len(weights), sizes),
        "forward",
        [
            shape((length, width), BF),
            shape((length, width), BF),
            shape((tokens, width), BF),
            shape((tokens, width), BF),
            shape((width, wide), BF),
            shape((tokens, width), BF),
            shape((tokens, width), BF),
            shape((tokens, nq), BF),
            shape((tokens, 128), F32),
            shape((tokens, nd + nf), BF),
            shape((tokens, nf), BF),
            shape((tokens, 128), F32),
        ],
        (place, table, gains, shift_qkv, shift_fc1),
        [
            pltpu.VMEM((length, nf), F32),
            pltpu.SemaphoreType.DMA((2 * tz,)),
            pltpu.SemaphoreType.DMA((dp,)),
            pltpu.SemaphoreType.DMA((2 * tz,)),
        ],
        16,
        (*shards, *weights),
    )

    part_other = sibling(part_sib)
    second_parts = kernel_call(
        partial(second_grads_body, dp, packets),
        "second_grads",
        [shape((width // dp * len(packet), nd + nf), BF) for packet in packets],
        (place, aa, cot),
        [],
        LITTLE,
    )
    branch_shards = add_sibling(after(place, second_parts[0]), part_own, part_other)

    branch_moved = [over_tensor(branch_shards[r], r) for r in range(1, tz)]
    second_first = first_round(second_parts)
    back_own, back_sib, gg, sums, bias_sums = kernel_call(
        partial(backward_body, tz, sizes),
        "backward",
        [
            shape((length, width), BF),
            shape((length, width), BF),
            shape((tokens, nq + nf), BF),
            shape((4, width), F32),
            shape((8, nq + nf), F32),
        ],
        (
            after(place, branch_shards[1]),
            table,
            gains,
            cot,
            w,
            qkv,
            lse,
            dgelu,
            stats,
            x,
        ),
        [
            pltpu.VMEM((length, nf), F32),
            pltpu.VMEM((length, width), F32),
            pltpu.VMEM((length, width), F32),
            pltpu.VMEM((4, 8, width), F32),
            pltpu.VMEM((length, nd), F32),
            pltpu.VMEM((length, nd), F32),
        ],
        14,
    )
    first_parts = kernel_call(
        partial(first_grads_body, dp, packets, nq),
        "first_grads",
        [shape((width // dp * len(packet), nq + nf), BF) for packet in packets],
        (place, n1, n2, gg),
        [],
        LITTLE,
    )
    back_sib, sums, bias_sums = after(
        (back_sib, sums, bias_sums), (branch_moved, second_first, first_parts[0])
    )
    output = (
        inputs.astype(F32)
        + turn(added([branch_shards[0]] + branch_moved))
        + dense_bias
        + fc2_bias
    ).astype(BF)

    out_bias = jnp.sum(masked.astype(F32), axis=0, keepdims=True)
    sums = turn(jnp.concatenate([sums, out_bias], axis=0))
    bias_part = jnp.sum(bias_sums, axis=0)
    biases = jnp.zeros((2 * width,), F32)
    biases = lax.dynamic_update_slice_in_dim(biases, by_head(bias_part[:nq], heads), core * nq, 0)
    biases = lax.dynamic_update_slice_in_dim(biases, bias_part[nq:], width + core * nf, 0)
    sums = jnp.concatenate([sums, biases.reshape(2, width)], axis=0)

    if rounds:
        now = after(place, (branch_moved, second_first, first_parts[0]))
        second_messages = kernel_call(
            messages_body,
            "second_messages",
            [shape(second_parts[4].shape, BF)] * 2,
            (now, second_parts[4], second_parts[5], *second_first),
            [],
            LITTLE,
        )
        second_x, second_y = over_chip(second_messages[0], 1), over_chip(second_messages[1], 2)
        back_other = sibling(back_sib)
        first_first = first_round(first_parts)
        sums_core = sibling(sums)
        *back_shards, second_other = kernel_call(
            partial(split_body, tz),
            "split_back",
            [shape((rows, width), F32)]
            + [shape((rows, width), BF)] * 3
            + [shape(second_parts[1].shape, BF)],
            (place, back_own, back_other, second_parts[1], second_first[1], second_y),
            [],
            LITTLE,
        )
        sums = sums + sums_core
        passed, across = over_tensor(back_shards[3], 1), over_middle(back_shards[3])
        sums_x = over_chip(sums, 1)
        second_sib = sibling(second_other)
        now = after(place, (across, second_sib))
        shard, first_x, first_y, sums = kernel_call(
            relay_body,
            "second_round",
            [
                shape((rows, width), BF),
                shape(first_parts[4].shape, BF),
                shape(first_parts[5].shape, BF),
                shape(sums.shape, F32),
            ],
            (
                now,
                back_shards[2],
                passed,
                first_parts[4],
                first_parts[5],
                *first_first,
                sums,
                sums_x,
            ),
            [],
            LITTLE,
        )
        back_second, back_first = over_tensor(shard, 2), over_tensor(back_shards[1], 1)
        first_x, first_y = over_chip(first_x, 1), over_chip(first_y, 2)
        sums_y = over_chip(sums, 2)
        input_grad, first_other, sums = kernel_call(
            finish_body,
            "finish_rows",
            [
                shape((rows, width), F32),
                shape(first_parts[1].shape, BF),
                shape(sums.shape, F32),
            ],
            (
                place,
                back_shards[0],
                back_first,
                back_second,
                across,
                shards[0],
                first_parts[1],
                first_first[1],
                first_y,
                sums,
                sums_y,
            ),
            [],
            LITTLE,
        )
        first_terms = [first_parts[0], first_first[0], first_x]
        second_terms = [second_parts[0], second_first[0], second_x]
        first_sib = sibling(first_other)
    else:
        back = added(
            [
                one if r == 0 else over_tensor(one, r)
                for r, one in enumerate(add_sibling(place, back_own, sibling(back_sib)))
            ]
        )
        value = own_rows.astype(F32)
        center = value - jnp.mean(value, axis=1, keepdims=True)
        spread = lax.rsqrt(jnp.mean(center * center, axis=1, keepdims=True) + EPS)
        scaled = center * spread
        input_grad = masked.astype(F32) + spread * (
            back
            - jnp.mean(back, axis=1, keepdims=True)
            - scaled * jnp.mean(back * scaled, axis=1, keepdims=True)
        )
        (second_own, second_other), (first_own, first_other) = (
            chip_sums(second_parts),
            chip_sums(first_parts),
        )
        second_terms, first_terms = [second_own], [first_own]
        second_sib, first_sib = sibling(second_other), sibling(first_other)
        flip = 1
        while flip < dp:
            sums = sums + lax.ppermute(sums, "dp", xor_pairs(dp, flip))
            flip *= 2
    input_grad = turn(input_grad)
    dense_grad, fc2_grad = join(second_terms, second_sib, (nd, nf), 0)
    qkv_grad, fc1_grad = join(first_terms, first_sib, (nq, nf), heads)
    biases = sums[5:]
    sums = added([sums[:5]] + [over_tensor(sums[:5], r) for r in range(1, tz)])

    return (
        output,
        input_grad,
        sums[0],
        sums[1],
        sums[2],
        sums[3],
        qkv_grad,
        biases[0, : 2 * nq],
        dense_grad,
        sums[4],
        fc1_grad,
        biases[1, : 2 * nf],
        fc2_grad,
        sums[4],
    )


def solution(mesh):
    return jax.shard_map(
        partial(on_device, mesh.shape["dp"], mesh.shape["tensor"]),
        mesh=mesh,
        in_specs=(
            P(("dp", "tensor"), None),
            P("dp"),
            P(),
            P(),
            P(),
            P(),
            P("dp", "tensor"),
            P("tensor"),
            P("dp", "tensor"),
            P(),
            P("dp", "tensor"),
            P("tensor"),
            P("dp", "tensor"),
            P(),
            P(("dp", "tensor"), None),
        ),
        out_specs=(
            P(("dp", "tensor"), None),
            P(("dp", "tensor"), None),
            P(),
            P(),
            P(),
            P(),
            P("dp", "tensor"),
            P("tensor"),
            P("dp", "tensor"),
            P(),
            P("dp", "tensor"),
            P("tensor"),
            P("dp", "tensor"),
            P(),
        ),
        check_vma=False,
    )
```

time: 498 us -> 167 us (0.34)
  waiting for transfers between devices: 325 us -> 42.9 us
  blocking collectives: 65.8 us -> 0 us
  matrix products: 64.1 us -> 0 us
  starting transfers between devices: 0.93 us -> 46.1 us
  Pallas kernels: 0 us -> 45 us
  between operations: 14.5 us -> 1.25 us
  local copies, waits for them, and re-layouts: 11.4 us -> 21.2 us
  other arithmetic: 15.5 us -> 10.3 us
    reduce_scatter x7 -> x0, waiting for transfers between devices: 209 us -> none  [the longest x1 55.7 us: on_device(): lax.psum_scatter(fc1_grad, 'dp', scatter_dimension=0, tiled=True)]
    all_gather x6 -> x0, waiting for transfers between devices: 114 us -> none  [the longest x1 27.9 us: on_device(): lax.all_gather(normed1, 'tensor', axis=0, tiled=True)]
    dot_general x18 -> x0, matrix products: 64.1 us -> none  [the longest x1 9.65 us: attend_back(): jnp.einsum('hqk,khd->qhd', grad_scores, key_rows, preferred_element_type=...]
    psum x2 -> x0, blocking collectives: 54.5 us -> none  [the longest x1 39.8 us: on_device(): lax.psum((gain1, shift1, gain2, shift2, out_bias), ('dp', 'tensor'))]
    ppermute x0 -> x39, starting transfers between devices: none -> 46.1 us  [the longest x12 26.2 us: over_tensor(): return lax.ppermute(values, 'tensor', xor_pairs(tz, flip))]
    pallas_call x0 -> x13, Pallas kernels: none -> 45 us  [kernel_call(): pl.pallas_call(body, name=name, out_shape=outs, in_specs=[SMEM] + [VMEM]...]
    ppermute x0 -> x39, waiting for transfers between devices: none -> 42.9 us  [the longest x12 31.3 us: over_tensor(): return lax.ppermute(values, 'tensor', xor_pairs(tz, flip))]
    all_gather x1 -> x0, blocking collectives: 11.3 us -> none  [on_device(): lax.all_gather(dense_weight, 'dp', axis=0, tiled=True)]
  transfers between devices with their start and end apart: 13 -> 39, of which waited for: 10 -> 8; matrix products, arithmetic and copies ran while one was open for 16% -> 12% of each run, Pallas kernels for 0% -> 16%
where the time goes in v1:
time: 167 us
  starting transfers between devices  46.1 us (28%)
  Pallas kernels  45 us (27%)
  waiting for transfers between devices  42.9 us (26%)
  local copies, waits for them, and re-layouts  21.2 us (13%)
  other arithmetic  10.3 us (6%)
    pallas_call x13, Pallas kernels, kernel_call(): pl.pallas_call(body, name=name, out_shape=outs, in_specs=[SMEM] + [VMEM]...  45 us
    ppermute x12, waiting for transfers between devices, over_tensor(): return lax.ppermute(values, 'tensor', xor_pairs(tz, flip))  31.3 us
    ppermute x12, starting transfers between devices, over_tensor(): return lax.ppermute(values, 'tensor', xor_pairs(tz, flip))  26.2 us
    ppermute x14, starting transfers between devices, over_chip(): return lax.ppermute(values, 'dp', xor_pairs(dp, 2 * flip))  15.5 us
    unnamed x87, local copies, waits for them, and re-layouts  11.7 us
    ppermute x14, waiting for transfers between devices, over_chip(): return lax.ppermute(values, 'dp', xor_pairs(dp, 2 * flip))  11.5 us
  transfers between devices with their start and end apart: 39, of which 8 were waited for; matrix products, arithmetic and copies ran while one was open for 12% of the time, Pallas kernels for 16%

profile of v1, /device:TPU:0, one launch (start us, length us, event | category | flops | bytes accessed | tf_op | source)
XLA Modules:
  0.0 166.8 jit_solution(1390283681405214152)
XLA Ops:
  0.8 0.9 copy-done.2
  1.7 0.9 copy-done.3
  2.7 0.9 copy-done.10
  3.6 0.8 copy-done.19
  4.4 1.1 pack_weights.1
  6.1 0.8 dynamic-slice_compare_fusion
  6.9 1.2 constant_dynamic-slice_fusion.11
  8.0 0.7 convert_reduce_fusion.1
  8.9 0.8 constant_dynamic-update-slice_fusion.1
  9.6 0.8 constant_dynamic-update-slice_fusion
  10.4 2.5 %collective-permute-start.4 = (bf16[256,1536]{1,0:T(8,128)(2,1)}, bf16[256,1536]{1,0:T(8,128)(2,1)S(1)}, u32[]{:S(2)}, u32[]{:S(2)}) collective-permute-start(bf16[256,1536]{1,0:T(8,128)(2,1)} %constant_dynamic-update-slice_fusion), channel_id=1, source_target_pairs={{0,8},{4,12},{8,0},{12,4},{16,24},{20,28},{24,16},{28,20},{1,9},{5... | collective-permute-start | bytes 2359304 | tf_op jit(solution)/shard_map/ppermute | solution.py:502
  13.0 1.5 collective-permute-start.5
  14.5 2.7 %collective-permute-start.2 = (bf16[256,1024]{1,0:T(8,128)(2,1)S(1)}, bf16[256,1024]{1,0:T(8,128)(2,1)S(1)}, u32[]{:S(2)}, u32[]{:S(2)}) collective-permute-start(bf16[256,1024]{1,0:T(8,128)(2,1)S(1)} %pad_maximum_fusion.1.refs_5_.rows), channel_id=1, source_target_pairs={{0,2},{1,3},{2,0},{3,1},{4,6},{5,7},{6,4},{7,5},{8,10},{9,11},{10,... | collective-permute-start | bytes 1572872 | tf_op jit(solution)/shard_map/ppermute | solution.py:505
  17.2 1.6 collective-permute-start.3
  18.9 21.7 %collective-permute-done.2.refs_7_ = bf16[256,1024]{1,0:T(8,128)(2,1)S(1)} collective-permute-done((bf16[256,1024]{1,0:T(8,128)(2,1)S(1)}, bf16[256,1024]{1,0:T(8,128)(2,1)S(1)}, u32[]{:S(2)}, u32[]{:S(2)}) %collective-permute-start.2) | collective-permute-done | bytes 524320 | tf_op jit(solution)/shard_map/ppermute | solution.py:505
  40.9 1.4 collective-permute-start.7
  42.8 2.1 %collective-permute-start.8 = (bf16[256,1024]{1,0:T(8,128)(2,1)S(1)}, bf16[256,1024]{1,0:T(8,128)(2,1)}, u32[]{:S(2)}, u32[]{:S(2)}) collective-permute-start(bf16[256,1024]{1,0:T(8,128)(2,1)S(1)} %collective-permute-done.2.refs_7_), channel_id=1, source_target_pairs={{0,1},{1,0},{2,3},{3,2},{4,5},{5,4},{6,7},{7,6},{8,9},{9,8},{10,11... | collective-permute-start | bytes 1572872 | tf_op jit(solution)/shard_map/ppermute | solution.py:505
  44.9 1.4 halves.1
  48.1 9.8 %collective-permute-done.10.refs_18_ = bf16[128,1536]{1,0:T(8,128)(2,1)} collective-permute-done((bf16[128,1536]{1,0:T(8,128)(2,1)}, bf16[128,1536]{1,0:T(8,128)(2,1)}, u32[]{:S(2)}, u32[]{:S(2)}) %collective-permute-start.10) | collective-permute-done | bytes 393248 | tf_op jit(solution)/shard_map/ppermute | solution.py:502
  58.1 1.1 broadcast_select_fusion.refs_8_
  59.6 1.9 %multiply_cosine_fusion = (f32[1024,128]{1,0:T(8,128)S(1)}, f32[1024,128]{1,0:T(8,128)S(1)}) fusion(f32[128]{0:T(128)S(1)} %get-tuple-element.212, f32[1024]{0:T(1024)S(1)} %get-tuple-element.203, f32[128]{0:T(128)S(1)} %get-tuple-element.211), kind=kLoop, calls=%fused_computation.3 | loop fusion | flops 262144 | bytes 1053696 | tf_op jit(solution)/shard_map/cos | solution.py:653
  61.7 14.9 %forward.1 = (bf16[512,1024]{1,0:T(8,128)(2,1)S(1)}, bf16[512,1024]{1,0:T(8,128)(2,1)S(1)}, bf16[1024,1024]{1,0:T(8,128)(2,1)S(1)}, bf16[1024,1024]{1,0:T(8,128)...) custom-call(s32[3]{0:T(128)S(1)} %pad_add_fusion.1.place.refs_0_, ...), custom_call_target="tpu_custom_call" | custom-call | flops 18400000000 | tf_op jit(solution)/shard_map/forward/pallas_call | solution.py:41
  77.2 2.4 %second_grads.1 = (bf16[128,640]{1,0:T(8,128)(2,1)S(1)}, bf16[128,640]{1,0:T(8,128)(2,1)S(1)}, bf16[256,640]{1,0:T(8,128)(2,1)S(1)}, bf16[256,640]{1,0:T(8,128)(...) custom-call(s32[3]{0:T(128)S(1)} %pad_add_fusion.1.place.refs_0_, ...), custom_call_target="tpu_custom_call" | custom-call | flops 11500000 | tf_op jit(solution)/shard_map/second_grads/pallas_call | solution.py:41
  80.2 1.5 collective-permute-start.19
  81.7 0.8 add_sibling.1
  82.9 2.8 %collective-permute-start.16 = (bf16[128,1024]{1,0:T(8,128)(2,1)S(1)}, bf16[128,1024]{1,0:T(8,128)(2,1)S(1)}, u32[]{:S(2)}, u32[]{:S(2)}) collective-permute-start(bf16[128,1024]{1,0:T(8,128)(2,1)S(1)} %get-tuple-element.114), channel_id=1, source_target_pairs={{0,2},{1,3},{2,0},{3,1},{4,6},{5,7},{6,4},{7,5},{8,10},{9,11},{10,... | collective-permute-start | bytes 786440 | tf_op jit(solution)/shard_map/ppermute | solution.py:505
  85.6 1.3 collective-permute-start.17
  86.9 14.0 %backward.1 = (bf16[512,1024]{1,0:T(8,128)(2,1)S(1)}, bf16[512,1024]{1,0:T(8,128)(2,1)}, bf16[1024,896]{1,0:T(8,128)(2,1)S(1)}, f32[4,1024]{1,0:T(4,128)S(1)}, f32[8,896]{1,0:T(8,128)S(1)}) custom-call(s32[3]{0:T(128)S(1)} %pad_add_fusion.1.place.refs_0_, f32[1024,384]{1,0:T(8,128)S(1)} %pad_maximum_fusion.refs_1_, f32[4,1024]{1,0:T(4,128)S(1)} %pad_maximum_fusion.5.refs_2_, ...), custom_call_target="tpu_custom_call" | custom-call | flops 16099999744 | tf_op jit(solution)/shard_map/backward/pallas_call | solution.py:41
  100.9 3.0 %first_grads.1 = (bf16[128,896]{1,0:T(8,128)(2,1)S(1)}, bf16[128,896]{1,0:T(8,128)(2,1)S(1)}, bf16[256,896]{1,0:T(8,128)(2,1)S(1)}, bf16[256,896]{1,0:T(8,128)(2...) custom-call(s32[3]{0:T(128)S(1)} %pad_add_fusion.1.place.refs_0_, ...), custom_call_target="tpu_custom_call" | custom-call | flops 11500000 | tf_op jit(solution)/shard_map/first_grads/pallas_call | solution.py:41
  104.0 0.7 copy-done.4
  104.7 0.7 copy-done.6
  105.4 0.7 copy-done.8
  106.1 0.7 copy-done.20
  107.2 0.9 copy-done.14
  108.1 0.9 copy-done.16
  109.0 1.2 second_messages.1
  110.9 1.5 collective-permute-start.21
  113.1 1.1 fusion.16
  114.8 1.4 dynamic_update_slice.6
  116.3 1.4 slice_dynamic-update-slice_fusion
  117.6 1.4 fusion.5
  119.0 0.7 reshape.127
  119.8 0.8 pad_maximum_fusion.3
  121.9 0.9 copy-done.12
  122.8 1.3 split_back.1
  124.3 1.5 collective-permute-start.29
  125.8 0.9 collective-permute-start.23
  126.8 5.2 %collective-permute-start.25 = (bf16[128,1024]{1,0:T(8,128)(2,1)S(1)}, bf16[128,1024]{1,0:T(8,128)(2,1)S(1)}, u32[]{:S(2)}, u32[]{:S(2)}) collective-permute-start(bf16[128,1024]{1,0:T(8,128)(2,1)S(1)} %get-tuple-element.141), channel_id=1, source_target_pairs={{0,1},{1,0},{2,3},{3,2},{4,5},{5,4},{6,7},{7,6},{8,9},{9,8},{10,11... | collective-permute-start | bytes 786440 | tf_op jit(solution)/shard_map/ppermute | solution.py:505
  132.2 1.2 collective-permute-start.38
  133.4 1.4 collective-permute-done.29.others
  134.8 4.8 %collective-permute-start.22 = (bf16[128,1024]{1,0:T(8,128)(2,1)S(1)}, bf16[128,1024]{1,0:T(8,128)(2,1)S(1)}, u32[]{:S(2)}, u32[]{:S(2)}) collective-permute-start(bf16[128,1024]{1,0:T(8,128)(2,1)S(1)} %get-tuple-element.140), channel_id=1, source_target_pairs={{0,1},{1,0},{2,3},{3,2},{4,5},{5,4},{6,7},{7,6},{8,9},{9,8},{10,11... | collective-permute-start | bytes 786440 | tf_op jit(solution)/shard_map/ppermute | solution.py:505
  140.3 1.1 collective-permute-start.30
  141.4 1.6 collective-permute-start.31
  143.5 0.8 fusion.3
  144.3 1.4 join_halves.3
  145.7 0.9 collective-permute-start.36
  146.7 3.2 %collective-permute-done.22.first = bf16[128,1024]{1,0:T(8,128)(2,1)S(1)} collective-permute-done((bf16[128,1024]{1,0:T(8,128)(2,1)S(1)}, bf16[128,1024]{1,0:T(8,128)(2,1)S(1)}, u32[]{:S(2)}, u32[]{:S(2)}) %collective-permute-start.22) | collective-permute-done | bytes 262176 | tf_op jit(solution)/shard_map/ppermute | solution.py:505
  149.9 4.1 %collective-permute-done.30.second = bf16[128,1024]{1,0:T(8,128)(2,1)S(1)} collective-permute-done((bf16[128,1024]{1,0:T(8,128)(2,1)S(1)}, bf16[128,1024]{1,0:T(8,128)(2,1)S(1)}, u32[]{:S(2)}, u32[]{:S(2)}) %collective-permute-start.30) | collective-permute-done | bytes 262176 | tf_op jit(solution)/shard_map/ppermute | solution.py:505
  153.9 1.2 finish_rows.1
  155.2 3.0 %collective-permute-start.34 = (f32[5,1024]{1,0:T(8,128)S(1)}, f32[5,1024]{1,0:T(8,128)S(1)}, u32[]{:S(2)}, u32[]{:S(2)}) collective-permute-start(f32[5,1024]{1,0:T(8,128)S(1)} %bitcast.21), channel_id=1, source_target_pairs={{0,2},{1,3},{2,0},{3,1},{4,6},{5,7},{6,4},{7,5},{8,10},{9,11},{10,... | collective-permute-start | bytes 61448 | tf_op jit(solution)/shard_map/ppermute | solution.py:505
  158.2 1.4 collective-permute-start.35
  159.6 0.9 pad_maximum_fusion.2
  161.7 2.2 %collective-permute-done.35 = f32[5,1024]{1,0:T(8,128)S(1)} collective-permute-done((f32[5,1024]{1,0:T(8,128)S(1)}, f32[5,1024]{1,0:T(8,128)S(1)}, u32[]{:S(2)}, u32[]{:S(2)}) %collective-permute-start.35) | collective-permute-done | bytes 20512 | tf_op jit(solution)/shard_map/ppermute | solution.py:505
  164.6 1.6 join_halves.2
  (159 shorter events, 13.5 us)
Async XLA Ops:
  0.6 8.1 %copy-start.40 = (f32[768]{0:T(1024)S(1)}, f32[768]{0:T(1024)}, u32[]{:S(2)}) copy-start(f32[768]{0:T(1024)} %param.22) | copy-start | bytes 9220
  5.5 4.1 %collective-permute-start.1 = (bf16[128,1536]{1,0:T(8,128)(2,1)S(1)}, bf16[128,1536]{1,0:T(8,128)(2,1)S(1)}, u32[]{:S(2)}, u32[]{:S(2)}) collective-permute-start(bf16[128,1536]{1,0:T(8,128)(2,1)S(1)} %get-tuple-element.89), channel_id=1, source_target_pairs={{0,4},{4,0},{8,12},{12,8},{16,20},{20,16},{24,28},{28,24},{1,5},{5... | collective-permute-start | bytes 1179656 | tf_op jit(solution)/shard_map/ppermute | solution.py:499
  6.8 7.7 %copy-start.36 = (f32[1024]{0:T(1024)S(1)}, f32[1024]{0:T(1024)}, u32[]{:S(2)}) copy-start(f32[1024]{0:T(1024)} %param.20) | copy-start | bytes 12292
  6.8 7.7 %copy-start.37 = (f32[1024]{0:T(1024)S(1)}, f32[1024]{0:T(1024)}, u32[]{:S(2)}) copy-start(f32[1024]{0:T(1024)} %param.19) | copy-start | bytes 12292
  6.8 7.7 %copy-start.38 = (f32[1024]{0:T(1024)S(1)}, f32[1024]{0:T(1024)}, u32[]{:S(2)}) copy-start(f32[1024]{0:T(1024)} %param.18) | copy-start | bytes 12292
  6.8 7.7 %copy-start.39 = (f32[1024]{0:T(1024)S(1)}, f32[1024]{0:T(1024)}, u32[]{:S(2)}) copy-start(f32[1024]{0:T(1024)} %param.17) | copy-start | bytes 12292
  6.8 33.7 %copy-start.33 = (s32[512]{0:T(512)S(1)}, s32[512]{0:T(512)}, u32[]{:S(2)}) copy-start(s32[512]{0:T(512)} %param.16) | copy-start | bytes 6148
  6.8 33.8 %copy-start.41 = (f32[1024]{0:T(1024)S(1)}, f32[1024]{0:T(1024)}, u32[]{:S(2)}) copy-start(f32[1024]{0:T(1024)} %param.26) | copy-start | bytes 12292
  10.4 31.9 %collective-permute-start.4 = (bf16[256,1536]{1,0:T(8,128)(2,1)}, bf16[256,1536]{1,0:T(8,128)(2,1)S(1)}, u32[]{:S(2)}, u32[]{:S(2)}) collective-permute-start(bf16[256,1536]{1,0:T(8,128)(2,1)} %constant_dynamic-update-slice_fusion), channel_id=1, source_target_pairs={{0,8},{4,12},{8,0},{12,4},{16,24},{20,28},{24,16},{28,20},{1,9},{5... | collective-permute-start | bytes 2359304 | tf_op jit(solution)/shard_map/ppermute | solution.py:502
  13.0 29.3 %collective-permute-start.5 = (bf16[256,1536]{1,0:T(8,128)(2,1)}, bf16[256,1536]{1,0:T(8,128)(2,1)S(1)}, u32[]{:S(2)}, u32[]{:S(2)}) collective-permute-start(bf16[256,1536]{1,0:T(8,128)(2,1)} %constant_dynamic-update-slice_fusion), channel_id=1, source_target_pairs={{0,16},{4,20},{8,24},{12,28},{16,0},{20,4},{24,8},{28,12},{1,17},{... | collective-permute-start | bytes 2359304 | tf_op jit(solution)/shard_map/ppermute | solution.py:502
  14.5 26.0 %collective-permute-start.2 = (bf16[256,1024]{1,0:T(8,128)(2,1)S(1)}, bf16[256,1024]{1,0:T(8,128)(2,1)S(1)}, u32[]{:S(2)}, u32[]{:S(2)}) collective-permute-start(bf16[256,1024]{1,0:T(8,128)(2,1)S(1)} %pad_maximum_fusion.1.refs_5_.rows), channel_id=1, source_target_pairs={{0,2},{1,3},{2,0},{3,1},{4,6},{5,7},{6,4},{7,5},{8,10},{9,11},{10,... | collective-permute-start | bytes 1572872 | tf_op jit(solution)/shard_map/ppermute | solution.py:505
  17.2 23.7 %collective-permute-start.3 = (bf16[256,1024]{1,0:T(8,128)(2,1)S(1)}, bf16[256,1024]{1,0:T(8,128)(2,1)}, u32[]{:S(2)}, u32[]{:S(2)}) collective-permute-start(bf16[256,1024]{1,0:T(8,128)(2,1)S(1)} %pad_maximum_fusion.1.refs_5_.rows), channel_id=1, source_target_pairs={{0,1},{1,0},{2,3},{3,2},{4,5},{5,4},{6,7},{7,6},{8,9},{9,8},{10,11... | collective-permute-start | bytes 1572872 | tf_op jit(solution)/shard_map/ppermute | solution.py:505
  18.8 23.5 %collective-permute-start.6 = (bf16[256,1024]{1,0:T(8,128)(2,1)S(1)}, bf16[256,1024]{1,0:T(8,128)(2,1)}, u32[]{:S(2)}, u32[]{:S(2)}) collective-permute-start(bf16[256,1024]{1,0:T(8,128)(2,1)S(1)} %pad_maximum_fusion.1.refs_5_.rows), channel_id=1, source_target_pairs={{0,4},{4,0},{8,12},{12,8},{16,20},{20,16},{24,28},{28,24},{1,5},{5... | collective-permute-start | bytes 1572872 | tf_op jit(solution)/shard_map/ppermute | solution.py:499
  40.6 4.3 %collective-permute-start = (s32[512]{0:T(512)S(1)}, s32[512]{0:T(512)S(1)}, u32[]{:S(2)}, u32[]{:S(2)}) collective-permute-start(s32[512]{0:T(512)S(1)} %copy-done.33), channel_id=1, source_target_pairs={{0,4},{4,0},{8,12},{12,8},{16,20},{20,16},{24,28},{28,24},{1,5},{5... | collective-permute-start | bytes 6152 | tf_op jit(solution)/shard_map/ppermute | solution.py:499
  40.9 7.1 %collective-permute-start.7 = (bf16[256,1024]{1,0:T(8,128)(2,1)S(1)}, bf16[256,1024]{1,0:T(8,128)(2,1)}, u32[]{:S(2)}, u32[]{:S(2)}) collective-permute-start(bf16[256,1024]{1,0:T(8,128)(2,1)S(1)} %pad_maximum_fusion.1.refs_5_.rows), channel_id=1, source_target_pairs={{0,0},{1,2},{2,1},{3,3},{4,4},{5,6},{6,5},{7,7},{8,8},{9,10},{10,9... | collective-permute-start | bytes 1572872 | tf_op jit(solution)/shard_map/ppermute | solution.py:514
  42.3 15.8 %collective-permute-start.11 = (bf16[256,1024]{1,0:T(8,128)(2,1)S(1)}, bf16[256,1024]{1,0:T(8,128)(2,1)}, u32[]{:S(2)}, u32[]{:S(2)}) collective-permute-start(bf16[256,1024]{1,0:T(8,128)(2,1)S(1)} %collective-permute-done.2.refs_7_), channel_id=1, source_target_pairs={{0,4},{4,0},{8,12},{12,8},{16,20},{20,16},{24,28},{28,24},{1,5},{5... | collective-permute-start | bytes 1572872 | tf_op jit(solution)/shard_map/ppermute | solution.py:499
  42.8 15.3 %collective-permute-start.8 = (bf16[256,1024]{1,0:T(8,128)(2,1)S(1)}, bf16[256,1024]{1,0:T(8,128)(2,1)}, u32[]{:S(2)}, u32[]{:S(2)}) collective-permute-start(bf16[256,1024]{1,0:T(8,128)(2,1)S(1)} %collective-permute-done.2.refs_7_), channel_id=1, source_target_pairs={{0,1},{1,0},{2,3},{3,2},{4,5},{5,4},{6,7},{7,6},{8,9},{9,8},{10,11... | collective-permute-start | bytes 1572872 | tf_op jit(solution)/shard_map/ppermute | solution.py:505
  46.3 11.6 %collective-permute-start.10 = (bf16[128,1536]{1,0:T(8,128)(2,1)}, bf16[128,1536]{1,0:T(8,128)(2,1)}, u32[]{:S(2)}, u32[]{:S(2)}) collective-permute-start(bf16[128,1536]{1,0:T(8,128)(2,1)} %get-tuple-element.99), channel_id=1, source_target_pairs={{0,8},{4,12},{8,0},{12,4},{16,24},{20,28},{24,16},{28,20},{1,9},{5... | collective-permute-start | bytes 1179656 | tf_op jit(solution)/shard_map/ppermute | solution.py:502
  46.9 11.2 %collective-permute-start.9 = (bf16[128,1536]{1,0:T(8,128)(2,1)}, bf16[128,1536]{1,0:T(8,128)(2,1)}, u32[]{:S(2)}, u32[]{:S(2)}) collective-permute-start(bf16[128,1536]{1,0:T(8,128)(2,1)} %get-tuple-element.98), channel_id=1, source_target_pairs={{0,16},{4,20},{8,24},{12,28},{16,0},{20,4},{24,8},{28,12},{1,17},{... | collective-permute-start | bytes 1179656 | tf_op jit(solution)/shard_map/ppermute | solution.py:502
  48.0 13.7 %collective-permute-start.12 = (bf16[256,1024]{1,0:T(8,128)(2,1)}, bf16[256,1024]{1,0:T(8,128)(2,1)S(1)}, u32[]{:S(2)}, u32[]{:S(2)}) collective-permute-start(bf16[256,1024]{1,0:T(8,128)(2,1)} %collective-permute-done.3.refs_6_), channel_id=1, source_target_pairs={{0,4},{4,0},{8,12},{12,8},{16,20},{20,16},{24,28},{28,24},{1,5},{5... | collective-permute-start | bytes 1572872 | tf_op jit(solution)/shard_map/ppermute | solution.py:499
  59.2 2.5 %collective-permute-start.13 = (bf16[256,1024]{1,0:T(8,128)(2,1)S(1)}, bf16[256,1024]{1,0:T(8,128)(2,1)S(1)}, u32[]{:S(2)}, u32[]{:S(2)}) collective-permute-start(bf16[256,1024]{1,0:T(8,128)(2,1)S(1)} %broadcast_select_fusion.refs_8_), channel_id=1, source_target_pairs={{0,4},{4,0},{8,12},{12,8},{16,20},{20,16},{24,28},{28,24},{1,5},{5... | collective-permute-start | bytes 1572872 | tf_op jit(solution)/shard_map/ppermute | solution.py:499
  76.6 5.1 %collective-permute-start.14 = (bf16[512,1024]{1,0:T(8,128)(2,1)S(1)}, bf16[512,1024]{1,0:T(8,128)(2,1)S(1)}, u32[]{:S(2)}, u32[]{:S(2)}) collective-permute-start(bf16[512,1024]{1,0:T(8,128)(2,1)S(1)} %get-tuple-element.111), channel_id=1, source_target_pairs={{0,4},{4,0},{8,12},{12,8},{16,20},{20,16},{24,28},{28,24},{1,5},{5... | collective-permute-start | bytes 3145736 | tf_op jit(solution)/shard_map/ppermute | solution.py:499
  79.6 7.3 %copy-start.11 = (bf16[128,640]{1,0:T(8,128)(2,1)}, bf16[128,640]{1,0:T(8,128)(2,1)S(1)}, u32[]{:S(2)}) copy-start(bf16[128,640]{1,0:T(8,128)(2,1)S(1)} %get-tuple-element.134.mine) | copy-start | bytes 491524
  79.6 21.3 %copy-start.13 = (bf16[128,640]{1,0:T(8,128)(2,1)}, bf16[128,640]{1,0:T(8,128)(2,1)S(1)}, u32[]{:S(2)}) copy-start(bf16[128,640]{1,0:T(8,128)(2,1)S(1)} %get-tuple-element.136.to_x) | copy-start | bytes 491524
  79.6 21.3 %copy-start.15 = (bf16[128,640]{1,0:T(8,128)(2,1)}, bf16[128,640]{1,0:T(8,128)(2,1)S(1)}, u32[]{:S(2)}) copy-start(bf16[128,640]{1,0:T(8,128)(2,1)S(1)} %get-tuple-element.137.to_y) | copy-start | bytes 491524
  79.6 21.3 %copy-start.17 = (bf16[128,640]{1,0:T(8,128)(2,1)}, bf16[128,640]{1,0:T(8,128)(2,1)S(1)}, u32[]{:S(2)}) copy-start(bf16[128,640]{1,0:T(8,128)(2,1)S(1)} %get-tuple-element.108.refs_0_) | copy-start | bytes 491524
  79.6 26.4 %collective-permute-start.18 = (bf16[256,640]{1,0:T(8,128)(2,1)S(1)}, bf16[256,640]{1,0:T(8,128)(2,1)S(1)}, u32[]{:S(2)}, u32[]{:S(2)}) collective-permute-start(bf16[256,640]{1,0:T(8,128)(2,1)S(1)} %get-tuple-element.127), channel_id=1, source_target_pairs={{0,16},{4,20},{8,24},{12,28},{16,0},{20,4},{24,8},{28,12},{1,17},{... | collective-permute-start | bytes 983048 | tf_op jit(solution)/shard_map/ppermute | solution.py:502
  80.2 25.8 %collective-permute-start.19 = (bf16[256,640]{1,0:T(8,128)(2,1)S(1)}, bf16[256,640]{1,0:T(8,128)(2,1)S(1)}, u32[]{:S(2)}, u32[]{:S(2)}) collective-permute-start(bf16[256,640]{1,0:T(8,128)(2,1)S(1)} %get-tuple-element.128), channel_id=1, source_target_pairs={{0,8},{4,12},{8,0},{12,4},{16,24},{20,28},{24,16},{28,20},{1,9},{5... | collective-permute-start | bytes 983048 | tf_op jit(solution)/shard_map/ppermute | solution.py:502
  82.5 18.5 %copy-start = (f32[128,1024]{1,0:T(8,128)}, f32[128,1024]{1,0:T(8,128)S(1)}, u32[]{:S(2)}) copy-start(f32[128,1024]{1,0:T(8,128)S(1)} %get-tuple-element.112) | copy-start | bytes 1572868
  82.5 23.6 %collective-permute-start.15 = (bf16[128,1024]{1,0:T(8,128)(2,1)S(1)}, bf16[128,1024]{1,0:T(8,128)(2,1)S(1)}, u32[]{:S(2)}, u32[]{:S(2)}) collective-permute-start(bf16[128,1024]{1,0:T(8,128)(2,1)S(1)} %get-tuple-element.113), channel_id=1, source_target_pairs={{0,1},{1,0},{2,3},{3,2},{4,5},{5,4},{6,7},{7,6},{8,9},{9,8},{10,11... | collective-permute-start | bytes 786440 | tf_op jit(solution)/shard_map/ppermute | solution.py:505
  82.9 23.2 %collective-permute-start.16 = (bf16[128,1024]{1,0:T(8,128)(2,1)S(1)}, bf16[128,1024]{1,0:T(8,128)(2,1)S(1)}, u32[]{:S(2)}, u32[]{:S(2)}) collective-permute-start(bf16[128,1024]{1,0:T(8,128)(2,1)S(1)} %get-tuple-element.114), channel_id=1, source_target_pairs={{0,2},{1,3},{2,0},{3,1},{4,6},{5,7},{6,4},{7,5},{8,10},{9,11},{10,... | collective-permute-start | bytes 786440 | tf_op jit(solution)/shard_map/ppermute | solution.py:505
  85.6 20.5 %collective-permute-start.17 = (bf16[128,1024]{1,0:T(8,128)(2,1)S(1)}, bf16[128,1024]{1,0:T(8,128)(2,1)S(1)}, u32[]{:S(2)}, u32[]{:S(2)}) collective-permute-start(bf16[128,1024]{1,0:T(8,128)(2,1)S(1)} %get-tuple-element.115), channel_id=1, source_target_pairs={{0,3},{1,2},{2,1},{3,0},{4,7},{5,6},{6,5},{7,4},{8,11},{9,10},{10,... | collective-permute-start | bytes 786440 | tf_op jit(solution)/shard_map/ppermute | solution.py:505
  107.2 14.7 %collective-permute-start.20 = (bf16[512,1024]{1,0:T(8,128)(2,1)}, bf16[512,1024]{1,0:T(8,128)(2,1)S(1)}, u32[]{:S(2)}, u32[]{:S(2)}) collective-permute-start(bf16[512,1024]{1,0:T(8,128)(2,1)} %get-tuple-element.133), channel_id=1, source_target_pairs={{0,4},{4,0},{8,12},{12,8},{16,20},{20,16},{24,28},{28,24},{1,5},{5... | collective-permute-start | bytes 3145736 | tf_op jit(solution)/shard_map/ppermute | solution.py:499
  110.9 10.9 %collective-permute-start.21 = (bf16[128,640]{1,0:T(8,128)(2,1)}, bf16[128,640]{1,0:T(8,128)(2,1)}, u32[]{:S(2)}, u32[]{:S(2)}) collective-permute-start(bf16[128,640]{1,0:T(8,128)(2,1)} %get-tuple-element.138), channel_id=1, source_target_pairs={{0,16},{4,20},{8,24},{12,28},{16,0},{20,4},{24,8},{28,12},{1,17},{... | collective-permute-start | bytes 491528 | tf_op jit(solution)/shard_map/ppermute | solution.py:502
  119.0 5.2 %copy-start.31 = (f32[5,256]{1,0:T(8,128)S(1)}, f32[5,256]{1,0:T(8,128)}, u32[]{:S(2)}) copy-start(f32[5,256]{1,0:T(8,128)} %get-tuple-element.190) | copy-start | bytes 15364
  119.8 12.2 %copy-start.1 = (f32[128,1024]{1,0:T(8,128)S(1)}, f32[128,1024]{1,0:T(8,128)}, u32[]{:S(2)}) copy-start(f32[128,1024]{1,0:T(8,128)} %copy-done) | copy-start | bytes 1572868
  120.5 3.7 %collective-permute-start.28 = (f32[7,1024]{1,0:T(8,128)S(1)}, f32[7,1024]{1,0:T(8,128)S(1)}, u32[]{:S(2)}, u32[]{:S(2)}) collective-permute-start(f32[7,1024]{1,0:T(8,128)S(1)} %pad_maximum_fusion.3), channel_id=1, source_target_pairs={{0,4},{4,0},{8,12},{12,8},{16,20},{20,16},{24,28},{28,24},{1,5},{5... | collective-permute-start | bytes 86024 | tf_op jit(solution)/shard_map/ppermute | solution.py:499
  120.8 18.7 %collective-permute-start.26 = (bf16[256,896]{1,0:T(8,128)(2,1)}, bf16[256,896]{1,0:T(8,128)(2,1)S(1)}, u32[]{:S(2)}, u32[]{:S(2)}) collective-permute-start(bf16[256,896]{1,0:T(8,128)(2,1)} %copy-done.21), channel_id=1, source_target_pairs={{0,16},{4,20},{8,24},{12,28},{16,0},{20,4},{24,8},{28,12},{1,17},{... | collective-permute-start | bytes 1376264 | tf_op jit(solution)/shard_map/ppermute | solution.py:502
  121.3 18.2 %collective-permute-start.27 = (bf16[256,896]{1,0:T(8,128)(2,1)}, bf16[256,896]{1,0:T(8,128)(2,1)S(1)}, u32[]{:S(2)}, u32[]{:S(2)}) collective-permute-start(bf16[256,896]{1,0:T(8,128)(2,1)} %copy-done.20), channel_id=1, source_target_pairs={{0,8},{4,12},{8,0},{12,4},{16,24},{20,28},{24,16},{28,20},{1,9},{5... | collective-permute-start | bytes 1376264 | tf_op jit(solution)/shard_map/ppermute | solution.py:502
  122.8 9.2 %copy-start.26 = (bf16[128,1024]{1,0:T(8,128)(2,1)S(1)}, bf16[128,1024]{1,0:T(8,128)(2,1)}, u32[]{:S(2)}) copy-start(bf16[128,1024]{1,0:T(8,128)(2,1)} %copy-done.25) | copy-start | bytes 786436
  122.8 9.2 %copy-start.28 = (bf16[128,1024]{1,0:T(8,128)(2,1)S(1)}, bf16[128,1024]{1,0:T(8,128)(2,1)}, u32[]{:S(2)}) copy-start(bf16[128,1024]{1,0:T(8,128)(2,1)} %copy-done.27) | copy-start | bytes 786436
  122.8 9.2 %copy-start.30 = (bf16[128,1024]{1,0:T(8,128)(2,1)S(1)}, bf16[128,1024]{1,0:T(8,128)(2,1)}, u32[]{:S(2)}) copy-start(bf16[128,1024]{1,0:T(8,128)(2,1)} %copy-done.29) | copy-start | bytes 786436
  122.8 9.4 %copy-start.23 = (bf16[128,640]{1,0:T(8,128)(2,1)S(1)}, bf16[128,640]{1,0:T(8,128)(2,1)}, u32[]{:S(2)}) copy-start(bf16[128,640]{1,0:T(8,128)(2,1)} %copy-done.22) | copy-start | bytes 491524
  122.8 16.8 %copy-start.7 = (bf16[128,896]{1,0:T(8,128)(2,1)S(1)}, bf16[128,896]{1,0:T(8,128)(2,1)}, u32[]{:S(2)}) copy-start(bf16[128,896]{1,0:T(8,128)(2,1)} %copy-done.6) | copy-start | bytes 688132
  122.8 16.8 %copy-start.9 = (bf16[128,896]{1,0:T(8,128)(2,1)S(1)}, bf16[128,896]{1,0:T(8,128)(2,1)}, u32[]{:S(2)}) copy-start(bf16[128,896]{1,0:T(8,128)(2,1)} %copy-done.8) | copy-start | bytes 688132
  124.2 2.6 %collective-permute-start.24 = (bf16[128,640]{1,0:T(8,128)(2,1)S(1)}, bf16[128,640]{1,0:T(8,128)(2,1)S(1)}, u32[]{:S(2)}, u32[]{:S(2)}) collective-permute-start(bf16[128,640]{1,0:T(8,128)(2,1)S(1)} %get-tuple-element.142), channel_id=1, source_target_pairs={{0,4},{4,0},{8,12},{12,8},{16,20},{20,16},{24,28},{28,24},{1,5},{5... | collective-permute-start | bytes 491528 | tf_op jit(solution)/shard_map/ppermute | solution.py:499
  124.3 10.5 %collective-permute-start.29 = (f32[7,1024]{1,0:T(8,128)S(1)}, f32[7,1024]{1,0:T(8,128)S(1)}, u32[]{:S(2)}, u32[]{:S(2)}) collective-permute-start(f32[7,1024]{1,0:T(8,128)S(1)} %fusion.18.sums), channel_id=1, source_target_pairs={{0,8},{4,12},{8,0},{12,4},{16,24},{20,28},{24,16},{28,20},{1,9},{5... | collective-permute-start | bytes 86024 | tf_op jit(solution)/shard_map/ppermute | solution.py:502
  125.8 6.3 %collective-permute-start.23 = (bf16[128,1024]{1,0:T(8,128)(2,1)S(1)}, bf16[128,1024]{1,0:T(8,128)(2,1)S(1)}, u32[]{:S(2)}, u32[]{:S(2)}) collective-permute-start(bf16[128,1024]{1,0:T(8,128)(2,1)S(1)} %get-tuple-element.141), channel_id=1, source_target_pairs={{0,0},{1,2},{2,1},{3,3},{4,4},{5,6},{6,5},{7,7},{8,8},{9,10},{10,9... | collective-permute-start | bytes 786440 | tf_op jit(solution)/shard_map/ppermute | solution.py:514
  126.8 12.8 %collective-permute-start.25 = (bf16[128,1024]{1,0:T(8,128)(2,1)S(1)}, bf16[128,1024]{1,0:T(8,128)(2,1)S(1)}, u32[]{:S(2)}, u32[]{:S(2)}) collective-permute-start(bf16[128,1024]{1,0:T(8,128)(2,1)S(1)} %get-tuple-element.141), channel_id=1, source_target_pairs={{0,1},{1,0},{2,3},{3,2},{4,5},{5,4},{6,7},{7,6},{8,9},{9,8},{10,11... | collective-permute-start | bytes 786440 | tf_op jit(solution)/shard_map/ppermute | solution.py:505
  132.0 11.5 %copy-start.24 = (bf16[128,1024]{1,0:T(8,128)(2,1)S(1)}, bf16[128,1024]{1,0:T(8,128)(2,1)}, u32[]{:S(2)}) copy-start(bf16[128,1024]{1,0:T(8,128)(2,1)} %param.15) | copy-start | bytes 786436
  132.0 11.5 %copy-start.34 = (f32[1024]{0:T(1024)S(1)}, f32[1024]{0:T(1024)}, u32[]{:S(2)}) copy-start(f32[1024]{0:T(1024)} %param.28) | copy-start | bytes 12292
  132.0 11.5 %copy-start.35 = (f32[1024]{0:T(1024)S(1)}, f32[1024]{0:T(1024)}, u32[]{:S(2)}) copy-start(f32[1024]{0:T(1024)} %param.24) | copy-start | bytes 12292
  132.1 12.1 %copy-start.18 = (bf16[128,640]{1,0:T(8,128)(2,1)S(1)}, bf16[128,640]{1,0:T(8,128)(2,1)}, u32[]{:S(2)}) copy-start(bf16[128,640]{1,0:T(8,128)(2,1)} %copy-done.17) | copy-start | bytes 491524
  132.2 12.1 %collective-permute-start.38 = (bf16[128,640]{1,0:T(8,128)(2,1)S(1)}, bf16[128,640]{1,0:T(8,128)(2,1)S(1)}, u32[]{:S(2)}, u32[]{:S(2)}) collective-permute-start(bf16[128,640]{1,0:T(8,128)(2,1)S(1)} %copy-done.23), channel_id=1, source_target_pairs={{0,8},{4,12},{8,0},{12,4},{16,24},{20,28},{24,16},{28,20},{1,9},{5... | collective-permute-start | bytes 491528 | tf_op jit(solution)/shard_map/ppermute | solution.py:502
  134.8 15.0 %collective-permute-start.22 = (bf16[128,1024]{1,0:T(8,128)(2,1)S(1)}, bf16[128,1024]{1,0:T(8,128)(2,1)S(1)}, u32[]{:S(2)}, u32[]{:S(2)}) collective-permute-start(bf16[128,1024]{1,0:T(8,128)(2,1)S(1)} %get-tuple-element.140), channel_id=1, source_target_pairs={{0,1},{1,0},{2,3},{3,2},{4,5},{5,4},{6,7},{7,6},{8,9},{9,8},{10,11... | collective-permute-start | bytes 786440 | tf_op jit(solution)/shard_map/ppermute | solution.py:505
  140.3 13.7 %collective-permute-start.30 = (bf16[128,1024]{1,0:T(8,128)(2,1)S(1)}, bf16[128,1024]{1,0:T(8,128)(2,1)S(1)}, u32[]{:S(2)}, u32[]{:S(2)}) collective-permute-start(bf16[128,1024]{1,0:T(8,128)(2,1)S(1)} %get-tuple-element.151), channel_id=1, source_target_pairs={{0,2},{1,3},{2,0},{3,1},{4,6},{5,7},{6,4},{7,5},{8,10},{9,11},{10,... | collective-permute-start | bytes 786440 | tf_op jit(solution)/shard_map/ppermute | solution.py:505
  141.4 8.4 %collective-permute-start.31 = (bf16[128,896]{1,0:T(8,128)(2,1)S(1)}, bf16[128,896]{1,0:T(8,128)(2,1)S(1)}, u32[]{:S(2)}, u32[]{:S(2)}) collective-permute-start(bf16[128,896]{1,0:T(8,128)(2,1)S(1)} %get-tuple-element.153), channel_id=1, source_target_pairs={{0,16},{4,20},{8,24},{12,28},{16,0},{20,4},{24,8},{28,12},{1,17},{... | collective-permute-start | bytes 688136 | tf_op jit(solution)/shard_map/ppermute | solution.py:502
  143.0 6.9 %collective-permute-start.32 = (f32[7,1024]{1,0:T(8,128)S(1)}, f32[7,1024]{1,0:T(8,128)S(1)}, u32[]{:S(2)}, u32[]{:S(2)}) collective-permute-start(f32[7,1024]{1,0:T(8,128)S(1)} %get-tuple-element.154.sums), channel_id=1, source_target_pairs={{0,16},{4,20},{8,24},{12,28},{16,0},{20,4},{24,8},{28,12},{1,17},{... | collective-permute-start | bytes 86024 | tf_op jit(solution)/shard_map/ppermute | solution.py:502
  145.7 18.8 %collective-permute-start.36 = (bf16[128,896]{1,0:T(8,128)(2,1)S(1)}, bf16[128,896]{1,0:T(8,128)(2,1)S(1)}, u32[]{:S(2)}, u32[]{:S(2)}) collective-permute-start(bf16[128,896]{1,0:T(8,128)(2,1)S(1)} %get-tuple-element.157), channel_id=1, source_target_pairs={{0,8},{4,12},{8,0},{12,4},{16,24},{20,28},{24,16},{28,20},{1,9},{5... | collective-permute-start | bytes 688136 | tf_op jit(solution)/shard_map/ppermute | solution.py:502
  153.9 10.6 %copy-start.5 = (bf16[128,896]{1,0:T(8,128)(2,1)S(1)}, bf16[128,896]{1,0:T(8,128)(2,1)}, u32[]{:S(2)}) copy-start(bf16[128,896]{1,0:T(8,128)(2,1)} %copy-done.4) | copy-start | bytes 688132
  155.1 6.6 %collective-permute-start.33 = (f32[5,1024]{1,0:T(8,128)S(1)}, f32[5,1024]{1,0:T(8,128)S(1)}, u32[]{:S(2)}, u32[]{:S(2)}) collective-permute-start(f32[5,1024]{1,0:T(8,128)S(1)} %bitcast.20), channel_id=1, source_target_pairs={{0,1},{1,0},{2,3},{3,2},{4,5},{5,4},{6,7},{7,6},{8,9},{9,8},{10,11... | collective-permute-start | bytes 61448 | tf_op jit(solution)/shard_map/ppermute | solution.py:505
  155.2 6.5 %collective-permute-start.34 = (f32[5,1024]{1,0:T(8,128)S(1)}, f32[5,1024]{1,0:T(8,128)S(1)}, u32[]{:S(2)}, u32[]{:S(2)}) collective-permute-start(f32[5,1024]{1,0:T(8,128)S(1)} %bitcast.21), channel_id=1, source_target_pairs={{0,2},{1,3},{2,0},{3,1},{4,6},{5,7},{6,4},{7,5},{8,10},{9,11},{10,... | collective-permute-start | bytes 61448 | tf_op jit(solution)/shard_map/ppermute | solution.py:505
  158.2 5.7 %collective-permute-start.35 = (f32[5,1024]{1,0:T(8,128)S(1)}, f32[5,1024]{1,0:T(8,128)S(1)}, u32[]{:S(2)}, u32[]{:S(2)}) collective-permute-start(f32[5,1024]{1,0:T(8,128)S(1)} %bitcast.22), channel_id=1, source_target_pairs={{0,3},{1,2},{2,1},{3,0},{4,7},{5,6},{6,5},{7,4},{8,11},{9,10},{10,... | collective-permute-start | bytes 61448 | tf_op jit(solution)/shard_map/ppermute | solution.py:505
  161.7 2.9 %collective-permute-start.37 = (bf16[128,896]{1,0:T(8,128)(2,1)S(1)}, bf16[128,896]{1,0:T(8,128)(2,1)S(1)}, u32[]{:S(2)}, u32[]{:S(2)}) collective-permute-start(bf16[128,896]{1,0:T(8,128)(2,1)S(1)} %get-tuple-element.158), channel_id=1, source_target_pairs={{0,4},{4,0},{8,12},{12,8},{16,20},{20,16},{24,28},{28,24},{1,5},{5... | collective-permute-start | bytes 688136 | tf_op jit(solution)/shard_map/ppermute | solution.py:499
  (17 other events, 16.2 us)

commit v2 on v1

v2 whole, which is shorter than its diff:
```python
from functools import partial

import jax
import jax.numpy as jnp
from jax import lax
from jax.experimental import pallas as pl
from jax.experimental.pallas import tpu as pltpu
from jax.sharding import PartitionSpec as P

HD = 64
ROT = 16
EPS = 1e-05
SCALE = HD**-0.5
BF = jnp.bfloat16
F32 = jnp.float32
LN_ROWS = 128
ANY = pl.BlockSpec(memory_space=pl.ANY)
HBM = pl.BlockSpec(memory_space=pltpu.HBM)
VMEM = pl.BlockSpec(memory_space=pltpu.VMEM)
SMEM = pl.BlockSpec(memory_space=pltpu.SMEM)
VMEM_LIMIT = 16 * 1024 * 1024
PEAK = 1.15e9
LITTLE = 0.01


def dot(a, b):
    return jnp.dot(a, b, preferred_element_type=F32)


def dot_nt(a, b):
    return lax.dot_general(a, b, (((1,), (1,)), ((), ())), preferred_element_type=F32)


def dot_tn(a, b):
    return lax.dot_general(a, b, (((0,), (0,)), ((), ())), preferred_element_type=F32)


def shape(dims, dtype):
    return jax.ShapeDtypeStruct(dims, dtype)


def kernel_call(body, name, outs, operands, scratch, micros, fetched=(), placed=False):
    return pl.pallas_call(
        body,
        name=name,
        out_shape=outs,
        in_specs=[SMEM] + [VMEM] * (len(operands) - 1) + [HBM] * len(fetched),
        out_specs=[ANY if placed else VMEM] * len(outs),
        scratch_shapes=scratch,
        cost_estimate=pl.CostEstimate(
            flops=int(micros * PEAK), bytes_accessed=0, transcendentals=0
        ),
        compiler_params=pltpu.CompilerParams(vmem_limit_bytes=VMEM_LIMIT),
    )(*operands, *fetched)


def start_all(pairs, sems, first=0):
    copies = [
        pltpu.make_async_copy(src, dst, sems.at[first + i]) for i, (src, dst) in enumerate(pairs)
    ]
    for one in copies:
        one.start()
    return copies


def wait_all(copies):
    for one in copies:
        one.wait()


def rows_at(start, size):
    return pl.ds(pl.multiple_of(start, size), size)


def shard_rows(place, tz, rows, i):
    return i // tz * tz * rows + (place[1] ^ (i % tz)) * rows


def weight_rows(place, size, i):
    return (i - i % 2 + (place[0] ^ (i % 2))) * size


def rotated(values, cos_table, sine_table):
    lane = lax.broadcasted_iota(jnp.int32, values.shape, 1)
    lanes = values.shape[1]
    turned = jnp.where(
        lane % ROT < ROT // 2,
        pltpu.roll(values, lanes - ROT // 2, 1),
        pltpu.roll(values, ROT // 2, 1),
    )
    return values * cos_table + turned * sine_table


def head_mask(value, head, heads):
    lane = lax.broadcasted_iota(jnp.int32, value.shape, 1)
    return (lane // (value.shape[1] // heads)) == head


def allowed_block(first_row, rows, keys, lower):
    row = lax.broadcasted_iota(jnp.int32, (rows, keys), 0) + first_row
    col = lax.broadcasted_iota(jnp.int32, (rows, keys), 1)
    return (col <= row) & (col >= lower)


def store_shards(place, tz, outs, group, cols, value):
    rows = value.shape[0] // tz
    for b in range(tz):
        outs[group][rows_at((place[1] ^ b) * rows, rows), cols] = value[
            b * rows : (b + 1) * rows
        ].astype(BF)


def forward_body(tz, dp, count, sizes, *refs):
    length, width, nq, nf, nd = sizes
    heads = nd // HD
    place, table, gains, shift_qkv, shift_fc1 = refs[:5]
    at = 5
    shards, pieces_w = refs[at : at + 2 * tz], refs[at + 2 * tz : at + 2 * tz + count]
    at += 2 * tz + count
    out_own, out_sib, x, w, n1, n2, qkv, lse, aa, dgelu, stats = refs[at : at + 11]
    x_sems, w_sems = refs[at + 11 :]
    rows = length // tz
    size = width // dp
    x_in = start_all(
        [
            (one, x.at[rows_at(shard_rows(place, tz, rows, i), rows)])
            for i, one in enumerate(shards)
        ],
        x_sems,
    )
    parts_w = [
        one.at[j * size : (j + 1) * size] for one in pieces_w for j in range(one.shape[0] // size)
    ]
    w_in = start_all(
        [(one, w.at[rows_at(weight_rows(place, size, i), size)]) for i, one in enumerate(parts_w)],
        w_sems,
    )
    for i in range(2 * tz):
        x_in[i].wait()
        start = shard_rows(place, tz, rows, i)

        for j in range(rows // LN_ROWS):
            there = rows_at(start + j * LN_ROWS, LN_ROWS)
            value = x[there, :].astype(F32)
            mean = jnp.mean(value, axis=1, keepdims=True)
            center = value - mean
            spread = lax.rsqrt(jnp.mean(center * center, axis=1, keepdims=True) + EPS)
            scaled = center * spread
            n1[there, :] = (scaled * gains[0:1, :] + gains[1:2, :]).astype(BF)
            n2[there, :] = (scaled * gains[2:3, :] + gains[3:4, :]).astype(BF)
            lane = lax.broadcasted_iota(jnp.int32, (LN_ROWS, 128), 1)
            stats[there, :] = jnp.where(lane == 0, mean, spread)
    wait_all(w_in)
    for g in range(2):
        group = slice(g * length, (g + 1) * length)
        cos_table, sine_table = table[group, 0:nd], table[group, nd : 2 * nd]
        projected = dot(n1[group, :], w[:, 0:nq]) + shift_qkv[...]
        qkv[group, 0:nd] = rotated(projected[:, 0:nd], cos_table, sine_table).astype(BF)
        qkv[group, nd : 2 * nd] = rotated(projected[:, nd : 2 * nd], cos_table, sine_table).astype(
            BF
        )
        qkv[group, 2 * nd : 3 * nd] = projected[:, 2 * nd : 3 * nd].astype(BF)
        for part in range(2):
            cols = slice(part * nf // 2, (part + 1) * nf // 2)
            h = dot(n2[group, :], w[:, nq + cols.start : nq + cols.stop]) + shift_fc1[:, cols]
            phi = 0.5 * (1.0 + lax.erf(h * 0.7071067811865476))
            aa[group, nd + cols.start : nd + cols.stop] = (h * phi).astype(BF)
            dgelu[group, cols] = (phi + h * (0.3989422804014327 * jnp.exp(-0.5 * h * h))).astype(BF)

        half = length // 2
        for block in range(2):
            keys = (block + 1) * half
            q_rows = slice(g * length + block * half, g * length + (block + 1) * half)
            k_rows = slice(g * length, g * length + keys)
            q = qkv[q_rows, 0:nd] * SCALE
            k = qkv[k_rows, nd : 2 * nd]
            v = qkv[k_rows, 2 * nd : 3 * nd]
            lower = table[q_rows, 2 * nd : 2 * nd + 1].astype(jnp.int32)
            allowed = allowed_block(block * half, half, keys, lower)
            gathered = jnp.zeros((half, nd), F32)
            kept = jnp.zeros((half, 128), F32)
            lane = lax.broadcasted_iota(jnp.int32, (half, 128), 1)
            for h in range(heads):
                mine = head_mask(q, h, heads)
                scores = dot_nt(jnp.where(mine, q, jnp.zeros_like(q)), k)
                scores = jnp.where(allowed, scores, -jnp.inf)
                top = jnp.max(scores, axis=1, keepdims=True)
                raised = jnp.exp(scores - top)
                total = jnp.sum(raised, axis=1, keepdims=True)
                soft = (raised * (1.0 / total)).astype(BF)
                gathered = jnp.where(mine, dot(soft, v), gathered)
                kept = jnp.where(lane == h, top + jnp.log(total), kept)
            valid = table[q_rows, 2 * nd + 64 : 2 * nd + 65]
            aa[q_rows, 0:nd] = (gathered * valid).astype(BF)
            lse[q_rows, :] = kept

        quarter = width // 4
        for part in range(4):
            cols = slice(part * quarter, (part + 1) * quarter)
            value = dot_nt(aa[group, :], w[cols, nq + nf :])
            store_shards(place, tz, (out_own, out_sib), g, cols, value)


def second_grads_body(tz, dp, packets, place, aa, *refs):
    shards, cot, outs, sems = refs[: 2 * tz], refs[2 * tz], refs[2 * tz + 1 : -1], refs[-1]
    rows = shards[0].shape[0]
    wait_all(
        start_all(
            [
                (one, cot.at[rows_at(shard_rows(place, tz, rows, i), rows)])
                for i, one in enumerate(shards)
            ],
            sems,
        )
    )
    grads_out(dp, packets, place, outs, lambda cols: dot_tn(cot[:, cols], aa[...]))


def first_grads_body(dp, packets, nq, place, n1, n2, gg, *outs):
    grads_out(
        dp,
        packets,
        place,
        outs,
        lambda cols: jnp.concatenate(
            [dot_tn(n1[:, cols], gg[:, 0:nq]), dot_tn(n2[:, cols], gg[:, nq:])], axis=1
        ),
    )


def grads_out(dp, packets, place, outs, product):
    size = outs[0].shape[0]
    slots = {i: (out, slot) for out, packet in zip(outs, packets) for slot, i in enumerate(packet)}
    for r in range(dp // 2):
        value = product(slice(2 * r * size, (2 * r + 2) * size)).astype(BF)
        low, high = value[0:size], value[size : 2 * size]
        first = place[0] == 0
        for i, (one, two) in ((2 * r, (low, high)), (2 * r + 1, (high, low))):
            out, slot = slots[i]
            out[slot * size : (slot + 1) * size, :] = jnp.where(first, one, two)


def eight_rows(value):
    rows, columns = value.shape
    return jnp.sum(value.reshape(rows // 8, 8, columns), axis=0)


def backward_body(tz, chips, sizes, *refs):
    length, width, nq, nf, nd = sizes
    heads = nd // HD
    place, table, gains, cot, w, qkv, lse, dgelu, stats, x = refs[:10]
    out_own, out_sib, gg, sums = refs[10:14]
    acc, dk, dv, bias_sums = refs[14:]
    rows = length // tz
    acc[...] = jnp.zeros_like(acc)
    bias_sums[...] = jnp.zeros_like(bias_sums)
    for g in range(2):
        group = slice(g * length, (g + 1) * length)
        grad_out = dot(cot[group, :], w[:, nq + nf : nq + nf + nd]).astype(BF)
        for part in range(2):
            cols = slice(part * nf // 2, (part + 1) * nf // 2)
            value = dot(cot[group, :], w[:, nq + nf + nd + cols.start : nq + nf + nd + cols.stop])
            value = value * dgelu[group, cols].astype(F32)
            gg[group, nq + cols.start : nq + cols.stop] = value.astype(BF)
            bias_sums[:, nq + cols.start : nq + cols.stop] += eight_rows(value)

        half = length // 2
        dk[...] = jnp.zeros_like(dk)
        dv[...] = jnp.zeros_like(dv)
        for block in range(2):
            keys = (block + 1) * half
            q_rows = slice(g * length + block * half, g * length + (block + 1) * half)
            k_rows = slice(g * length, g * length + keys)
            q = qkv[q_rows, 0:nd] * SCALE
            k = qkv[k_rows, nd : 2 * nd]
            v = qkv[k_rows, 2 * nd : 3 * nd]
            k_scaled = k * SCALE
            go = grad_out[block * half : (block + 1) * half]
            lower = table[q_rows, 2 * nd : 2 * nd + 1].astype(jnp.int32)
            allowed = allowed_block(block * half, half, keys, lower)
            dq = jnp.zeros((half, nd), F32)
            for h in range(heads):
                mine = head_mask(q, h, heads)
                zero = jnp.zeros_like(q)
                q_h = jnp.where(mine, q, zero)
                go_h = jnp.where(mine, go, zero)
                scores = dot_nt(q_h, k)
                probs = jnp.exp(jnp.where(allowed, scores - lse[q_rows, h : h + 1], -jnp.inf))
                grad_soft = dot_nt(go_h, v)
                inner = jnp.sum(probs * grad_soft, axis=1, keepdims=True)
                grad_scores = (probs * (grad_soft - inner)).astype(BF)
                dq = jnp.where(mine, dot(grad_scores, k_scaled), dq)
                dk[0:keys, :] += dot_tn(grad_scores, q_h)
                dv[0:keys, :] += dot_tn(probs.astype(BF), go_h)
            grads_q = rotated(dq, table[q_rows, 0:nd], -table[q_rows, nd : 2 * nd])
            gg[q_rows, 0:nd] = grads_q.astype(BF)
            bias_sums[:, 0:nd] += eight_rows(grads_q)
        grads_k = rotated(dk[...], table[group, 0:nd], -table[group, nd : 2 * nd])
        gg[group, nd : 2 * nd] = grads_k.astype(BF)
        gg[group, 2 * nd : 3 * nd] = dv[...].astype(BF)
        bias_sums[:, nd : 2 * nd] += eight_rows(grads_k)
        bias_sums[:, 2 * nd : 3 * nd] += eight_rows(dv[...])

        mean, spread = stats[group, 0:1], stats[group, 1:2]
        quarter = width // 4
        for part in range(4):
            cols = slice(part * quarter, (part + 1) * quarter)
            one = dot_nt(gg[group, 0:nq], w[cols, 0:nq])
            two = dot_nt(gg[group, nq:], w[cols, nq : nq + nf])
            scaled = (x[group, cols].astype(F32) - mean) * spread
            for slot, value in enumerate((one * scaled, one, two * scaled, two)):
                acc[slot, :, cols] += eight_rows(value)
            value = one * gains[0:1, cols] + two * gains[2:3, cols]
            store_shards(place, tz, (out_own, out_sib), g, cols, value)
    sums[...] = jnp.zeros_like(sums)
    own = cot[rows_at(place[1] * rows, rows), :].astype(F32)
    acc[4] = eight_rows(own)
    step = width // chips
    for i in range(5):
        total = jnp.sum(acc[i], axis=0, keepdims=True)
        if step % 128 == 0:
            for r in range(chips):
                at = pl.ds(pl.multiple_of((place[3] ^ r) * step, step), step)
                sums[i : i + 1, at] = total[:, r * step : (r + 1) * step]
        else:
            sums[i : i + 1, :] = total
    total = jnp.sum(bias_sums[...], axis=0, keepdims=True)
    sums[5:6, pl.ds(pl.multiple_of(place[0] * nq, nq), nq)] = by_head(total[:, :nq], heads)
    sums[6:7, pl.ds(pl.multiple_of(place[0] * nf, nf), nf)] = total[:, nq:]
    put_sums(out_sib, length, sums[...])


def put_sums(out, row, value):
    high = value.astype(BF).astype(F32)
    out[row : row + 16, :] = jnp.concatenate([high, value - high], axis=0).astype(BF)


def get_sums(ref, row):
    return ref[row : row + 8, :].astype(F32) + ref[row + 8 : row + 16, :].astype(F32)


def combine_body(tz, place, own, other, *outs):
    rows = own.shape[0] // tz
    for r, out in enumerate(outs):
        at = slice(r * rows, (r + 1) * rows)
        out[0:rows, :] = (own[at, :].astype(F32) + other[at, :].astype(F32)).astype(out.dtype)


def by_kind(values, heads):
    parts = [
        values[..., (h * 3 + kind) * HD : (h * 3 + kind + 1) * HD]
        for kind in range(3)
        for h in range(heads)
    ]
    return jnp.concatenate(parts, axis=-1)


def by_head(values, heads):
    parts = [
        values[..., (kind * heads + h) * HD : (kind * heads + h + 1) * HD]
        for h in range(heads)
        for kind in range(3)
    ]
    return jnp.concatenate(parts, axis=-1)


def pack_body(sizes, place, qkv_in, fc1_in, dense_in, fc2_in, kept, given, *scratch):
    nq, nf, nd = sizes
    qkv, fc1, dense, fc2, sems = scratch
    wait_all(
        start_all([(qkv_in, qkv), (fc1_in, fc1), (dense_in, dense), (fc2_in, fc2)], sems)
    )
    for out, which in ((given, 1 - place[0]), (kept, place[0])):

        def half(ref, size):
            return ref[:, pl.ds(pl.multiple_of(which * size, size), size)]

        out[:, 0:nq] = by_kind(half(qkv, nq), nd // HD)
        out[:, nq : nq + nf] = half(fc1, nf)
        out[:, nq + nf : nq + nf + nd] = half(dense, nd)
        out[:, nq + nf + nd :] = half(fc2, nf)


def messages_body(place, to_x, to_y, from_y, from_x, out_x, out_y):
    size = to_x.shape[0]
    out_x[...] = to_x[...] + from_y[size : 2 * size, :]
    out_y[...] = to_y[...] + from_x[size : 2 * size, :]


def split_body(tz, place, own, other, sums, *outs):
    combine_body(tz, place, own, other, *outs[:tz])
    outs[tz][...] = sums[...] + get_sums(other, own.shape[0])


def shard_sum(mine, first, second, out):
    size = out.shape[0]
    out[...] = (
        mine[...].astype(F32) + first[0:size, :].astype(F32) + second[...].astype(F32)
    ).astype(BF)


def pass_body(place, shard, passed, out):
    rows = shard.shape[0]
    keep = (place[2] == 1).astype(F32)
    out[0:rows, :] = (shard[...].astype(F32) + keep * passed[...].astype(F32)).astype(BF)


def relay_body(place, near, shard, passed, to_x, to_y, from_y, from_x, *refs):
    sums, (out_near, out_shard, out_x, out_y, out_sums) = refs[:-5], refs[-5:]
    rows = near.shape[0]
    total = sums[0][...]
    for one in sums[1:]:
        total = total + one[...]
    out_sums[...] = total
    out_near[0:rows, :] = near[...]
    pass_body(place, shard, passed, out_shard)
    for out in (out_near, out_shard):
        put_sums(out, rows, total)
    messages_body(place, to_x, to_y, from_y, from_x, out_x, out_y)


def other_body(place, mine, first, second, out):
    shard_sum(mine, first, second, out)


def finish_body(place, own, first, second, across, x, cot, sums, third, out_rows, out_sums):
    rows = own.shape[0]
    keep = (place[2] == 1).astype(F32)
    back = (
        own[...]
        + first[0:rows, :].astype(F32)
        + second[0:rows, :].astype(F32)
        + keep * across[...].astype(F32)
    )
    value = x[...].astype(F32)
    center = value - jnp.mean(value, axis=1, keepdims=True)
    spread = lax.rsqrt(jnp.mean(center * center, axis=1, keepdims=True) + EPS)
    scaled = center * spread
    out_rows[...] = cot[...].astype(F32) + spread * (
        back
        - jnp.mean(back, axis=1, keepdims=True)
        - scaled * jnp.mean(back * scaled, axis=1, keepdims=True)
    )
    out_sums[...] = sums[...] + get_sums(first, rows) + get_sums(second, rows) + third[...]


def join_body(heads, widths, count, place, *refs):
    parts, other, outs = refs[:count], refs[count], refs[count + 1 :]
    rows = other.shape[0]
    total = parts[0][0:rows, :].astype(F32)
    for one in parts[1:]:
        total = total + one[0:rows, :].astype(F32)
    for half, which in ((total, place[0]), (other[...].astype(F32), 1 - place[0])):
        at = 0
        for i, (out, size) in enumerate(zip(outs, widths)):
            value = half[:, at : at + size]
            if i == 0 and heads:
                value = by_head(value, heads)
            out[:, pl.ds(pl.multiple_of(which * size, size), size)] = value
            at += size


def xor_pairs(size, flip):
    return [(i, i ^ flip) for i in range(size)]


def on_device(
    dp,
    tz,
    inputs,
    segment_ids,
    ln1_gain,
    ln1_bias,
    ln2_gain,
    ln2_bias,
    qkv_weight,
    qkv_bias,
    dense_weight,
    dense_bias,
    fc1_weight,
    fc1_bias,
    fc2_weight,
    fc2_bias,
    cotangent,
):
    rows, width = inputs.shape
    length = segment_ids.shape[0]
    tokens = 2 * length
    chips = dp // 2
    here = lax.axis_index("dp")
    core = here % 2
    chip = here // 2
    tensor = lax.axis_index("tensor")
    step = width // chips
    nq, nf, nd = qkv_weight.shape[1] // 2, fc1_weight.shape[1] // 2, dense_weight.shape[1] // 2
    wide = nq + nf + nd + nf
    heads = nd // HD
    sizes = (length, width, nq, nf, nd)
    middle = (tensor == 1) | (tensor == 2)
    place = jnp.stack([core, tensor, middle, chip]).astype(jnp.int32)

    def turn(values):
        parts = [
            lax.dynamic_slice_in_dim(values, (chip ^ r) * step, step, axis=values.ndim - 1)
            for r in range(chips)
        ]
        return jnp.concatenate(parts, axis=-1)

    def sibling(values):
        return lax.ppermute(values, "dp", xor_pairs(dp, 1))

    def over_chip(values, flip):
        return lax.ppermute(values, "dp", xor_pairs(dp, 2 * flip))

    def over_tensor(values, flip):
        return lax.ppermute(values, "tensor", xor_pairs(tz, flip))

    def together(*values):
        return lax.optimization_barrier(values)

    def after(values, event):
        return lax.optimization_barrier((values, event))[0]

    def over_middle(values):
        return lax.ppermute(values, "tensor", [(0, 0), (1, 2), (2, 1), (3, 3)])

    def add_sibling(place, own, other):
        dtypes = [F32] + [BF] * (tz - 1)
        return kernel_call(
            partial(combine_body, tz),
            "add_sibling",
            [shape((rows, width), d) for d in dtypes],
            (place, own, other),
            [],
            LITTLE,
        )

    def added(parts):
        total = parts[0]
        for one in parts[1:]:
            total = total + one.astype(F32)
        return total

    def row_tables(arrived):
        both_ids = jnp.stack([segment_ids, sibling(after(segment_ids, arrived))])
        earlier = (both_ids[:, None, :] >= 0) & (both_ids[:, None, :] < both_ids[:, :, None])
        begins = jnp.sum(earlier.astype(jnp.int32), axis=2).reshape(tokens)
        flat_ids = both_ids.reshape(tokens)
        index = jnp.arange(tokens, dtype=jnp.int32) % length
        position = (index - begins).astype(F32)
        lane = jnp.arange(nd, dtype=jnp.int32) % HD
        half_rot = ROT // 2
        frequency = jnp.where(
            lane < ROT, 10000.0 ** (-2.0 * (lane % half_rot).astype(F32) / ROT), 0.0
        )
        angles = position[:, None] * frequency[None, :]
        sign = jnp.where(lane < half_rot, -1.0, 1.0)
        lower = jnp.where(flat_ids >= 0, begins, index).astype(F32)
        valid = (flat_ids >= 0).astype(F32)
        last = jnp.where(jnp.arange(128)[None, :] < 64, lower[:, None], valid[:, None])
        return jnp.concatenate([jnp.cos(angles), jnp.sin(angles) * sign, last], axis=1)

    def gather(kept, given, own_rows, later):
        if chips != 4 or tz != 4:
            blocks = [(kept, sibling(given))]
            flip = 1
            while flip < chips:
                blocks = blocks + [(over_chip(a, flip), over_chip(b, flip)) for a, b in blocks]
                flip *= 2
            shards = [own_rows] + [over_tensor(own_rows, r) for r in range(1, tz)]
            return (
                [one for block in blocks for one in block],
                shards + [sibling(one) for one in shards],
                later,
                row_tables(given),
            )
        moved = [over_tensor(own_rows, r) for r in range(1, tz)]
        kept_x, kept_y, given = together(over_chip(kept, 1), over_chip(kept, 2), sibling(given))
        table = row_tables(kept_x)
        given_x, given_y = over_chip(given, 1), over_chip(given, 2)
        moved, kept_x, given_x, given_y, table = together(moved, kept_x, given_x, given_y, table)
        later = after(later, moved)
        pieces = [kept, given, kept_x, given_x, kept_y, given_y]
        pieces += [over_chip(kept_x, 2), over_chip(given_y, 1)]
        shards = [own_rows] + moved
        return pieces, shards + [sibling(one) for one in shards], later, table

    rounds = chips == 4 and tz == 4
    packets = [[0], [1], [4, 6], [3, 7], [2], [5]] if rounds else [[i] for i in range(dp)]

    def first_round(parts):
        if rounds:
            return [over_chip(parts[2], 2), over_chip(parts[3], 1)]
        return []

    def chip_sums(parts):
        blocks = [(parts[2 * r], parts[2 * r + 1]) for r in range(chips)]
        flip = chips // 2
        while flip:
            blocks = [
                tuple(
                    (a.astype(F32) + over_chip(b, flip).astype(F32)).astype(BF)
                    for a, b in zip(blocks[r], blocks[r + flip])
                )
                for r in range(flip)
            ]
            flip //= 2
        return blocks[0]

    def join(terms, other, widths, own_heads):
        return kernel_call(
            partial(join_body, own_heads, widths, len(terms)),
            "join_halves",
            [shape((width // dp, 2 * one), F32) for one in widths],
            (place, *terms, other),
            [],
            LITTLE,
        )

    def half_of(values, which):
        size = values.shape[-1] // 2
        return lax.dynamic_slice_in_dim(values, which * size, size, axis=values.ndim - 1)


    kept, given = kernel_call(
        partial(pack_body, (nq, nf, nd)),
        "pack_weights",
        [shape((width // dp, wide), BF)] * 2,
        (place,),
        [
            pltpu.VMEM(one.shape, BF) for one in (qkv_weight, fc1_weight, dense_weight, fc2_weight)
        ]
        + [pltpu.SemaphoreType.DMA((4,))],
        LITTLE,
        [
            pltpu.with_memory_space_constraint(one, pltpu.HBM)
            for one in (qkv_weight, fc1_weight, dense_weight, fc2_weight)
        ],
    )

    own_rows = turn(after(inputs, kept))
    own_validity = lax.dynamic_slice_in_dim(segment_ids, tensor * rows, rows) >= 0
    masked = jnp.where(own_validity[:, None], turn(cotangent), jnp.zeros((), BF))
    weights, x_shards, masked, table = gather(kept, given, own_rows, masked)
    c_moved = [over_tensor(masked, r) for r in range(1, tz)]
    masked_sib = sibling(masked)

    gains = turn(jnp.stack([ln1_gain, ln1_bias, ln2_gain, ln2_bias]))
    shift_qkv = by_kind(half_of(qkv_bias, core), heads)[None, :]
    shift_fc1 = half_of(fc1_bias, core)[None, :]

    part_own, part_sib, x, w, n1, n2, qkv, lse, aa, dgelu, stats = kernel_call(
        partial(forward_body, tz, dp, len(weights), sizes),
        "forward",
        [
            shape((length, width), BF),
            shape((length, width), BF),
            shape((tokens, width), BF),
            shape((width, wide), BF),
            shape((tokens, width), BF),
            shape((tokens, width), BF),
            shape((tokens, nq), BF),
            shape((tokens, 128), F32),
            shape((tokens, nd + nf), BF),
            shape((tokens, nf), BF),
            shape((tokens, 128), F32),
        ],
        (after(place, masked_sib), table, gains, shift_qkv, shift_fc1),
        [pltpu.SemaphoreType.DMA((2 * tz,)), pltpu.SemaphoreType.DMA((dp,))],
        LITTLE,
        (*x_shards, *weights),
    )

    c_moved, part_sib = together(c_moved, part_sib)
    branch_shards = add_sibling(place, part_own, sibling(part_sib))
    c_shards = [masked] + c_moved + [masked_sib] + [sibling(one) for one in c_moved]
    if rounds:
        passed, across = over_tensor(branch_shards[3], 1), over_middle(branch_shards[3])
    cot, *second_parts = kernel_call(
        partial(second_grads_body, tz, dp, packets),
        "second_grads",
        [shape((tokens, width), BF)]
        + [shape((width // dp * len(packet), nd + nf), BF) for packet in packets],
        (after(place, branch_shards[1]), aa),
        [pltpu.SemaphoreType.DMA((2 * tz,))],
        LITTLE,
        c_shards,
    )

    if rounds:
        shard = kernel_call(
            pass_body,
            "branch_relay",
            [shape((rows, width), BF)],
            (after(place, second_parts[0]), branch_shards[2], passed),
            [],
            LITTLE,
        )[0]
        branch_moved = [over_tensor(branch_shards[1], 1), over_tensor(shard, 2)]
        branch_moved += [across]
    else:
        shard = branch_shards[1]
        branch_moved = [over_tensor(branch_shards[r], r) for r in range(1, tz)]
    second_first = first_round(second_parts)
    back_own, back_sib, gg, sums = kernel_call(
        partial(backward_body, tz, chips, sizes),
        "backward",
        [
            shape((length, width), BF),
            shape((length + 16, width), BF),
            shape((tokens, nq + nf), BF),
            shape((8, width), F32),
        ],
        (
            after(place, shard),
            table,
            gains,
            cot,
            w,
            qkv,
            lse,
            dgelu,
            stats,
            x,
        ),
        [
            pltpu.VMEM((5, 8, width), F32),
            pltpu.VMEM((length, nd), F32),
            pltpu.VMEM((length, nd), F32),
            pltpu.VMEM((8, nq + nf), F32),
        ],
        14,
    )
    first_parts = kernel_call(
        partial(first_grads_body, dp, packets, nq),
        "first_grads",
        [shape((width // dp * len(packet), nq + nf), BF) for packet in packets],
        (place, n1, n2, gg),
        [],
        LITTLE,
    )
    branch_moved, second_first, back_sib = together(
        branch_moved, second_first, after(back_sib, first_parts[0])
    )
    if rounds:
        branch_moved[2] = jnp.where(middle, branch_moved[2], jnp.zeros((), BF))
    output = (
        inputs.astype(F32)
        + turn(added([branch_shards[0]] + branch_moved))
        + dense_bias
        + fc2_bias
    ).astype(BF)

    if rounds:
        back_other = sibling(back_sib)
        first_first = first_round(first_parts)
        *back_shards, sums = kernel_call(
            partial(split_body, tz),
            "split_back",
            [shape((rows, width), F32)]
            + [shape((rows, width), BF)] * 3
            + [shape(sums.shape, F32)],
            (place, back_own, back_other, sums),
            [],
            LITTLE,
        )
        passed, across = over_tensor(back_shards[3], 1), over_middle(back_shards[3])
        second_messages = kernel_call(
            messages_body,
            "second_messages",
            [shape(second_parts[4].shape, BF)] * 2,
            (after(place, back_other), second_parts[4], second_parts[5], *second_first),
            [],
            LITTLE,
        )
        second_x, second_y = over_chip(second_messages[0], 1), over_chip(second_messages[1], 2)
        near, shard, first_x, first_y, sums = kernel_call(
            relay_body,
            "second_round",
            [
                shape((rows + 16, width), BF),
                shape((rows + 16, width), BF),
                shape(first_parts[4].shape, BF),
                shape(first_parts[5].shape, BF),
                shape(sums.shape, F32),
            ],
            (
                after(place, across),
                back_shards[1],
                back_shards[2],
                passed,
                first_parts[4],
                first_parts[5],
                *first_first,
                sums,
                *[over_chip(sums, flip) for flip in range(1, chips)],
            ),
            [],
            LITTLE,
        )
        biases = sums
        back_second, back_first = over_tensor(shard, 2), over_tensor(near, 1)
        third = over_tensor(sums, 3)
        first_x, first_y = over_chip(first_x, 1), over_chip(first_y, 2)

        def other_sum(parts, first, second, where):
            return kernel_call(
                other_body,
                "other_sum",
                [shape(parts[1].shape, BF)],
                (where, parts[1], first[1], second),
                [],
                LITTLE,
            )[0]

        second_sib = sibling(
            other_sum(second_parts, second_first, second_y, after(place, first_parts[0]))
        )
        first_sib = sibling(other_sum(first_parts, first_first, first_y, place))
        first_terms = [first_parts[0], first_first[0], first_x]
        second_terms = [second_parts[0], second_first[0], second_x]
        dense_grad, fc2_grad = join(second_terms, second_sib, (nd, nf), 0)
        qkv_grad, fc1_grad = join(first_terms, first_sib, (nq, nf), heads)
        input_grad, sums = kernel_call(
            finish_body,
            "finish_rows",
            [shape((rows, width), F32), shape(sums.shape, F32)],
            (
                place,
                back_shards[0],
                back_first,
                back_second,
                across,
                own_rows,
                masked,
                sums,
                third,
            ),
            [],
            6,
        )
    else:
        back_other = sibling(back_sib)
        back_shards = add_sibling(place, back_own, back_other)
        back = added([back_shards[0]] + [over_tensor(back_shards[r], r) for r in range(1, tz)])
        sums = added([sums, back_other[length : length + 8], back_other[length + 8 :]])
        if step % 128:
            sums = jnp.concatenate([turn(sums[:5]), sums[5:]], axis=0)
        value = own_rows.astype(F32)
        center = value - jnp.mean(value, axis=1, keepdims=True)
        spread = lax.rsqrt(jnp.mean(center * center, axis=1, keepdims=True) + EPS)
        scaled = center * spread
        input_grad = masked.astype(F32) + spread * (
            back
            - jnp.mean(back, axis=1, keepdims=True)
            - scaled * jnp.mean(back * scaled, axis=1, keepdims=True)
        )
        (second_own, second_other), (first_own, first_other) = (
            chip_sums(second_parts),
            chip_sums(first_parts),
        )
        second_sib, first_sib = sibling(second_other), sibling(first_other)
        flip = 1
        while flip < chips:
            sums = sums + over_chip(sums, flip)
            flip *= 2
        biases = sums
        sums = added([sums] + [over_tensor(sums, r) for r in range(1, tz)])
        dense_grad, fc2_grad = join([second_own], second_sib, (nd, nf), 0)
        qkv_grad, fc1_grad = join([first_own], first_sib, (nq, nf), heads)
    input_grad = turn(input_grad)

    return (
        output,
        input_grad,
        sums[0],
        sums[1],
        sums[2],
        sums[3],
        qkv_grad,
        biases[5, : 2 * nq],
        dense_grad,
        sums[4],
        fc1_grad,
        biases[6, : 2 * nf],
        fc2_grad,
        sums[4],
    )


def solution(mesh):
    return jax.shard_map(
        partial(on_device, mesh.shape["dp"], mesh.shape["tensor"]),
        mesh=mesh,
        in_specs=(
            P(("dp", "tensor"), None),
            P("dp"),
            P(),
            P(),
            P(),
            P(),
            P("dp", "tensor"),
            P("tensor"),
            P("dp", "tensor"),
            P(),
            P("dp", "tensor"),
            P("tensor"),
            P("dp", "tensor"),
            P(),
            P(("dp", "tensor"), None),
        ),
        out_specs=(
            P(("dp", "tensor"), None),
            P(("dp", "tensor"), None),
            P(),
            P(),
            P(),
            P(),
            P("dp", "tensor"),
            P("tensor"),
            P("dp", "tensor"),
            P(),
            P("dp", "tensor"),
            P("tensor"),
            P("dp", "tensor"),
            P(),
        ),
        check_vma=False,
    )
```

time: 167 us -> 140 us (0.84)
  local copies, waits for them, and re-layouts: 21.2 us -> 7.31 us
  waiting for transfers between devices: 42.9 us -> 33.1 us
  starting transfers between devices: 46.1 us -> 53.1 us
  Pallas kernels: 45 us -> 39.1 us
  other arithmetic: 10.3 us -> 6.29 us
    ppermute x12 -> x13, waiting for transfers between devices: 31.3 us -> 14.9 us  [over_tensor(): return lax.ppermute(values, 'tensor', xor_pairs(tz, flip))]
    unnamed x87 -> x18, local copies, waits for them, and re-layouts: 11.7 us -> 0.64 us
    pallas_call x13 -> x15, Pallas kernels: 45 us -> 39.1 us  [kernel_call(): pl.pallas_call(body, name=name, out_shape=outs, in_specs=[SMEM] + [VMEM]...]
    ppermute x14 -> x17, starting transfers between devices: 15.5 us -> 20.9 us  [over_chip(): return lax.ppermute(values, 'dp', xor_pairs(dp, 2 * flip))]
    ppermute x11 -> x14, waiting for transfers between devices: 0.03 us -> 4.38 us  [sibling(): return lax.ppermute(values, 'dp', xor_pairs(dp, 1))]
    dynamic_update_slice x2 -> x0, local copies, waits for them, and re-layouts: 2.81 us -> none  [the longest x1 1.44 us: on_device(): lax.dynamic_update_slice_in_dim(biases, by_head(bias_part[:nq], heads), c...]
    ppermute x12 -> x13, starting transfers between devices: 26.2 us -> 28.6 us  [over_tensor(): return lax.ppermute(values, 'tensor', xor_pairs(tz, flip))]
    ppermute x14 -> x17, waiting for transfers between devices: 11.5 us -> 13.8 us  [over_chip(): return lax.ppermute(values, 'dp', xor_pairs(dp, 2 * flip))]
  transfers between devices with their start and end apart: 39 -> 46, of which waited for: 8 -> 12; matrix products, arithmetic and copies ran while one was open for 12% -> 9% of each run, Pallas kernels for 16% -> 25%
where the time goes in v2:
time: 140 us
  starting transfers between devices  53.1 us (38%)
  Pallas kernels  39.1 us (28%)
  waiting for transfers between devices  33.1 us (24%)
  local copies, waits for them, and re-layouts  7.31 us (5%)
  other arithmetic  6.29 us (4%)
    pallas_call x15, Pallas kernels, kernel_call(): pl.pallas_call(body, name=name, out_shape=outs, in_specs=[SMEM] + [VMEM]...  39.1 us
    ppermute x13, starting transfers between devices, over_tensor(): return lax.ppermute(values, 'tensor', xor_pairs(tz, flip))  28.6 us
    ppermute x17, starting transfers between devices, over_chip(): return lax.ppermute(values, 'dp', xor_pairs(dp, 2 * flip))  20.9 us
    ppermute x13, waiting for transfers between devices, over_tensor(): return lax.ppermute(values, 'tensor', xor_pairs(tz, flip))  14.9 us
    ppermute x17, waiting for transfers between devices, over_chip(): return lax.ppermute(values, 'dp', xor_pairs(dp, 2 * flip))  13.8 us
    ppermute x14, waiting for transfers between devices, sibling(): return lax.ppermute(values, 'dp', xor_pairs(dp, 1))  4.38 us
  transfers between devices with their start and end apart: 46, of which 12 were waited for; matrix products, arithmetic and copies ran while one was open for 9% of the time, Pallas kernels for 25%

profile of v2, /device:TPU:0, one launch (start us, length us, event | category | flops | bytes accessed | tf_op | source)
XLA Modules:
  0.0 139.9 jit_solution(10793242798024924097)
XLA Ops:
  0.8 1.9 %pack_weights.1 = (bf16[128,1536]{1,0:T(8,128)(2,1)S(1)}, bf16[128,1536]{1,0:T(8,128)(2,1)S(1)}) custom-call(s32[4]{0:T(128)S(1)} %pad_add_fusion.1.place.refs_0_, bf16[128,768]{1,0:T(8,128)(2,1)} %qkv_in.1, bf16[128,1024]{1,0:T(8,128)(2,1)} %fc1_in.1, bf16[128,256]{1,0:T(8,128)(2,1)} %dense_in.1, bf16[128,1024]{1,0:T(8,128)(2,1)} %fc2_in.1), custom_call_target="tpu_custom_call" | custom-call | flops 11500000 | tf_op jit(solution)/shard_map/pack_weights/pallas_call | solution.py:43
  2.7 3.0 %collective-permute-start.3 = (bf16[128,1536]{1,0:T(8,128)(2,1)S(1)}, bf16[128,1536]{1,0:T(8,128)(2,1)S(1)}, u32[]{:S(2)}, u32[]{:S(2)}) collective-permute-start(bf16[128,1536]{1,0:T(8,128)(2,1)S(1)} %get-tuple-element.97.refs_13_), channel_id=1, source_target_pairs={{0,8},{4,12},{8,0},{12,4},{16,24},{20,28},{24,16},{28,20},{1,9},{5... | collective-permute-start | bytes 1179656 | tf_op jit(solution)/shard_map/ppermute | solution.py:513
  5.7 1.5 %collective-permute-start.4 = (bf16[128,1536]{1,0:T(8,128)(2,1)S(1)}, bf16[128,1536]{1,0:T(8,128)(2,1)S(1)}, u32[]{:S(2)}, u32[]{:S(2)}) collective-permute-start(bf16[128,1536]{1,0:T(8,128)(2,1)S(1)} %get-tuple-element.97.refs_13_), channel_id=1, source_target_pairs={{0,16},{4,20},{8,24},{12,28},{16,0},{20,4},{24,8},{28,12},{1,17},{... | collective-permute-start | bytes 1179656 | tf_op jit(solution)/shard_map/ppermute | solution.py:513
  7.2 1.1 constant_dynamic-slice_fusion.15
  8.3 1.6 %collective-permute-start = (bf16[128,1024]{1,0:T(8,128)(2,1)S(1)}, bf16[128,1024]{1,0:T(8,128)(2,1)S(1)}, u32[]{:S(2)}, u32[]{:S(2)}) collective-permute-start(bf16[128,1024]{1,0:T(8,128)(2,1)S(1)} %pad_maximum_fusion.2.refs_5_.x), channel_id=1, source_target_pairs={{0,1},{1,0},{2,3},{3,2},{4,5},{5,4},{6,7},{7,6},{8,9},{9,8},{10,11... | collective-permute-start | bytes 786440 | tf_op jit(solution)/shard_map/ppermute | solution.py:516
  10.0 2.6 %collective-permute-start.1 = (bf16[128,1024]{1,0:T(8,128)(2,1)S(1)}, bf16[128,1024]{1,0:T(8,128)(2,1)}, u32[]{:S(2)}, u32[]{:S(2)}) collective-permute-start(bf16[128,1024]{1,0:T(8,128)(2,1)S(1)} %pad_maximum_fusion.2.refs_5_.x), channel_id=1, source_target_pairs={{0,2},{1,3},{2,0},{3,1},{4,6},{5,7},{6,4},{7,5},{8,10},{9,11},{10,... | collective-permute-start | bytes 786440 | tf_op jit(solution)/shard_map/ppermute | solution.py:516
  12.8 2.0 %collective-permute-done.3.refs_15_ = bf16[128,1536]{1,0:T(8,128)(2,1)S(1)} collective-permute-done((bf16[128,1536]{1,0:T(8,128)(2,1)S(1)}, bf16[128,1536]{1,0:T(8,128)(2,1)S(1)}, u32[]{:S(2)}, u32[]{:S(2)}) %collective-permute-start.3) | collective-permute-done | bytes 393248 | tf_op jit(solution)/shard_map/ppermute | solution.py:513
  14.8 3.9 %collective-permute-start.2 = (bf16[128,1024]{1,0:T(8,128)(2,1)S(1)}, bf16[128,1024]{1,0:T(8,128)(2,1)}, u32[]{:S(2)}, u32[]{:S(2)}) collective-permute-start(bf16[128,1024]{1,0:T(8,128)(2,1)S(1)} %pad_maximum_fusion.2.refs_5_.x), channel_id=1, source_target_pairs={{0,3},{1,2},{2,1},{3,0},{4,7},{5,6},{6,5},{7,4},{8,11},{9,10},{10,... | collective-permute-start | bytes 786440 | tf_op jit(solution)/shard_map/ppermute | solution.py:516
  18.7 1.6 %collective-permute-start.6 = (bf16[128,1536]{1,0:T(8,128)(2,1)}, bf16[128,1536]{1,0:T(8,128)(2,1)}, u32[]{:S(2)}, u32[]{:S(2)}) collective-permute-start(bf16[128,1536]{1,0:T(8,128)(2,1)} %collective-permute-done.5.refs_14_), channel_id=1, source_target_pairs={{0,8},{4,12},{8,0},{12,4},{16,24},{20,28},{24,16},{28,20},{1,9},{5... | collective-permute-start | bytes 1179656 | tf_op jit(solution)/shard_map/ppermute | solution.py:513
  20.2 1.5 %collective-permute-start.7 = (bf16[128,1536]{1,0:T(8,128)(2,1)}, bf16[128,1536]{1,0:T(8,128)(2,1)}, u32[]{:S(2)}, u32[]{:S(2)}) collective-permute-start(bf16[128,1536]{1,0:T(8,128)(2,1)} %collective-permute-done.5.refs_14_), channel_id=1, source_target_pairs={{0,16},{4,20},{8,24},{12,28},{16,0},{20,4},{24,8},{28,12},{1,17},{... | collective-permute-start | bytes 1179656 | tf_op jit(solution)/shard_map/ppermute | solution.py:513
  22.3 1.9 %multiply_cosine_fusion = (f32[1024,128]{1,0:T(8,128)S(1)}, f32[1024,128]{1,0:T(8,128)S(1)}) fusion(f32[128]{0:T(128)S(1)} %get-tuple-element.216, f32[1024]{0:T(1024)S(1)} %get-tuple-element.207, f32[128]{0:T(128)S(1)} %get-tuple-element.215), kind=kLoop, calls=%fused_computation.3 | loop fusion | flops 262144 | bytes 1053696 | tf_op jit(solution)/shard_map/cos | solution.py:561
  24.8 5.8 %collective-permute-done.1.refs_7_ = bf16[128,1024]{1,0:T(8,128)(2,1)} collective-permute-done((bf16[128,1024]{1,0:T(8,128)(2,1)S(1)}, bf16[128,1024]{1,0:T(8,128)(2,1)}, u32[]{:S(2)}, u32[]{:S(2)}) %collective-permute-start.1) | collective-permute-done | bytes 262176 | tf_op jit(solution)/shard_map/ppermute | solution.py:516
  30.6 1.1 collective-permute-done.7.refs_18_
  32.7 0.8 dynamic_slice.82
  33.5 1.5 %collective-permute-start.14 = (bf16[128,1536]{1,0:T(8,128)(2,1)S(1)}, bf16[128,1536]{1,0:T(8,128)(2,1)}, u32[]{:S(2)}, u32[]{:S(2)}) collective-permute-start(bf16[128,1536]{1,0:T(8,128)(2,1)S(1)} %collective-permute-done.3.refs_15_), channel_id=1, source_target_pairs={{0,16},{4,20},{8,24},{12,28},{16,0},{20,4},{24,8},{28,12},{1,17},{... | collective-permute-start | bytes 1179656 | tf_op jit(solution)/shard_map/ppermute | solution.py:513
  35.0 1.1 collective-permute-start.15
  36.1 0.6 fusion.12
  36.7 2.4 %collective-permute-start.16 = (bf16[128,1024]{1,0:T(8,128)(2,1)S(1)}, bf16[128,1024]{1,0:T(8,128)(2,1)}, u32[]{:S(2)}, u32[]{:S(2)}) collective-permute-start(bf16[128,1024]{1,0:T(8,128)(2,1)S(1)} %maximum_select_fusion.refs_0_.cot), channel_id=1, source_target_pairs={{0,1},{1,0},{2,3},{3,2},{4,5},{5,4},{6,7},{7,6},{8,9},{9,8},{10,11... | collective-permute-start | bytes 786440 | tf_op jit(solution)/shard_map/ppermute | solution.py:516
  39.1 1.1 collective-permute-start.17
  40.2 1.4 %collective-permute-start.18 = (bf16[128,1024]{1,0:T(8,128)(2,1)S(1)}, bf16[128,1024]{1,0:T(8,128)(2,1)}, u32[]{:S(2)}, u32[]{:S(2)}) collective-permute-start(bf16[128,1024]{1,0:T(8,128)(2,1)S(1)} %maximum_select_fusion.refs_0_.cot), channel_id=1, source_target_pairs={{0,3},{1,2},{2,1},{3,0},{4,7},{5,6},{6,5},{7,4},{8,11},{9,10},{10,... | collective-permute-start | bytes 786440 | tf_op jit(solution)/shard_map/ppermute | solution.py:516
  41.7 1.3 pad_maximum_fusion.3
  43.0 0.8 concatenate.29
  43.8 0.8 dynamic_slice.83
  44.6 0.7 constant_dynamic-slice_fusion.11
  45.3 0.8 collective-permute-done.15.refs_20_
  46.1 11.9 %forward.1 = (bf16[512,1024]{1,0:T(8,128)(2,1)S(1)}, bf16[512,1024]{1,0:T(8,128)(2,1)S(1)}, bf16[1024,1024]{1,0:T(8,128)(2,1)S(1)}, bf16[1024,1536]{1,0:T(8,128)...) custom-call(s32[4]{0:T(128)S(1)} %pad_add_fusion.1.place.refs_0_, ...), custom_call_target="tpu_custom_call" | custom-call | flops 11500000 | tf_op jit(solution)/shard_map/forward/pallas_call | solution.py:43
  58.0 2.6 %collective-permute-done.17.refs_2_ = bf16[128,1024]{1,0:T(8,128)(2,1)} collective-permute-done((bf16[128,1024]{1,0:T(8,128)(2,1)S(1)}, bf16[128,1024]{1,0:T(8,128)(2,1)}, u32[]{:S(2)}, u32[]{:S(2)}) %collective-permute-start.17) | collective-permute-done | bytes 262176 | tf_op jit(solution)/shard_map/ppermute | solution.py:516
  61.6 2.8 %collective-permute-done.19.other = bf16[512,1024]{1,0:T(8,128)(2,1)S(1)} collective-permute-done((bf16[512,1024]{1,0:T(8,128)(2,1)S(1)}, bf16[512,1024]{1,0:T(8,128)(2,1)S(1)}, u32[]{:S(2)}, u32[]{:S(2)}) %collective-permute-start.19) | collective-permute-done | bytes 1048608 | tf_op jit(solution)/shard_map/ppermute | solution.py:510
  64.4 0.8 add_sibling.1
  65.2 4.5 %collective-permute-start.24 = (bf16[128,1024]{1,0:T(8,128)(2,1)S(1)}, bf16[128,1024]{1,0:T(8,128)(2,1)S(1)}, u32[]{:S(2)}, u32[]{:S(2)}) collective-permute-start(bf16[128,1024]{1,0:T(8,128)(2,1)S(1)} %get-tuple-element.126), channel_id=1, source_target_pairs={{0,1},{1,0},{2,3},{3,2},{4,5},{5,4},{6,7},{7,6},{8,9},{9,8},{10,11... | collective-permute-start | bytes 786440 | tf_op jit(solution)/shard_map/ppermute | solution.py:516
  69.8 0.7 collective-permute-start.26
  70.4 3.7 %second_grads.1 = (bf16[1024,1024]{1,0:T(8,128)(2,1)S(1)}, bf16[128,640]{1,0:T(8,128)(2,1)S(1)}, bf16[128,640]{1,0:T(8,128)(2,1)S(1)}, bf16[256,640]{1,0:T(8,128...) custom-call(s32[4]{0:T(128)S(1)} %pad_add_fusion.1.place.refs_0_, ...), custom_call_target="tpu_custom_call" | custom-call | flops 11500000 | tf_op jit(solution)/shard_map/second_grads/pallas_call | solution.py:43
  74.2 1.6 %collective-permute-start.27 = (bf16[256,640]{1,0:T(8,128)(2,1)S(1)}, bf16[256,640]{1,0:T(8,128)(2,1)S(1)}, u32[]{:S(2)}, u32[]{:S(2)}) collective-permute-start(bf16[256,640]{1,0:T(8,128)(2,1)S(1)} %get-tuple-element.127), channel_id=1, source_target_pairs={{0,16},{4,20},{8,24},{12,28},{16,0},{20,4},{24,8},{28,12},{1,17},{... | collective-permute-start | bytes 983048 | tf_op jit(solution)/shard_map/ppermute | solution.py:513
  75.8 1.5 %collective-permute-start.28 = (bf16[256,640]{1,0:T(8,128)(2,1)S(1)}, bf16[256,640]{1,0:T(8,128)(2,1)S(1)}, u32[]{:S(2)}, u32[]{:S(2)}) collective-permute-start(bf16[256,640]{1,0:T(8,128)(2,1)S(1)} %get-tuple-element.128), channel_id=1, source_target_pairs={{0,8},{4,12},{8,0},{12,4},{16,24},{20,28},{24,16},{28,20},{1,9},{5... | collective-permute-start | bytes 983048 | tf_op jit(solution)/shard_map/ppermute | solution.py:513
  77.2 0.6 branch_relay.1
  77.9 4.7 %collective-permute-start.25 = (bf16[128,1024]{1,0:T(8,128)(2,1)S(1)}, bf16[128,1024]{1,0:T(8,128)(2,1)S(1)}, u32[]{:S(2)}, u32[]{:S(2)}) collective-permute-start(bf16[128,1024]{1,0:T(8,128)(2,1)S(1)} %branch_relay.1), channel_id=1, source_target_pairs={{0,2},{1,3},{2,0},{3,1},{4,6},{5,7},{6,4},{7,5},{8,10},{9,11},{10,... | collective-permute-start | bytes 786440 | tf_op jit(solution)/shard_map/ppermute | solution.py:516
  82.6 9.7 %backward.1 = (bf16[512,1024]{1,0:T(8,128)(2,1)S(1)}, bf16[528,1024]{1,0:T(8,128)(2,1)S(1)}, bf16[1024,896]{1,0:T(8,128)(2,1)S(1)}, f32[8,1024]{1,0:T(8,128)S(1)}) custom-call(s32[4]{0:T(128)S(1)} %pad_add_fusion.1.place.refs_0_, f32[1024,384]{1,0:T(8,128)S(1)} %pad_maximum_fusion.refs_1_, f32[4,1024]{1,0:T(4,128)S(1)} %pad_maximum_fusion.4.refs_2_, ...), custom_call_target="tpu_custom_call" | custom-call | flops 16099999744 | tf_op jit(solution)/shard_map/backward/pallas_call | solution.py:43
  92.3 3.2 %first_grads.1 = (bf16[128,896]{1,0:T(8,128)(2,1)S(1)}, bf16[128,896]{1,0:T(8,128)(2,1)S(1)}, bf16[256,896]{1,0:T(8,128)(2,1)S(1)}, bf16[256,896]{1,0:T(8,128)(2...) custom-call(s32[4]{0:T(128)S(1)} %pad_add_fusion.1.place.refs_0_, ...), custom_call_target="tpu_custom_call" | custom-call | flops 11500000 | tf_op jit(solution)/shard_map/first_grads/pallas_call | solution.py:43
  96.7 1.6 %collective-permute-done.29.other = bf16[528,1024]{1,0:T(8,128)(2,1)S(1)} collective-permute-done((bf16[528,1024]{1,0:T(8,128)(2,1)S(1)}, bf16[528,1024]{1,0:T(8,128)(2,1)S(1)}, u32[]{:S(2)}, u32[]{:S(2)}) %collective-permute-start.29) | collective-permute-done | bytes 1081376 | tf_op jit(solution)/shard_map/ppermute | solution.py:510
  98.3 0.8 split_back.1
  99.1 0.7 collective-permute-start.30
  99.8 1.9 %collective-permute-start.31 = (bf16[128,1024]{1,0:T(8,128)(2,1)S(1)}, bf16[128,1024]{1,0:T(8,128)(2,1)S(1)}, u32[]{:S(2)}, u32[]{:S(2)}) collective-permute-start(bf16[128,1024]{1,0:T(8,128)(2,1)S(1)} %get-tuple-element.150), channel_id=1, source_target_pairs={{0,1},{1,0},{2,3},{3,2},{4,5},{5,4},{6,7},{7,6},{8,9},{9,8},{10,11... | collective-permute-start | bytes 786440 | tf_op jit(solution)/shard_map/ppermute | solution.py:516
  102.2 0.6 collective-permute-start.44
  103.0 6.0 %collective-permute-done.32.from_y.refs_1_ = bf16[256,896]{1,0:T(8,128)(2,1)S(1)} collective-permute-done((bf16[256,896]{1,0:T(8,128)(2,1)S(1)}, bf16[256,896]{1,0:T(8,128)(2,1)S(1)}, u32[]{:S(2)}, u32[]{:S(2)}) %collective-permute-start.32) | collective-permute-done | bytes 458784 | tf_op jit(solution)/shard_map/ppermute | solution.py:513
  109.5 2.5 %collective-permute-done.44.second = bf16[128,640]{1,0:T(8,128)(2,1)S(1)} collective-permute-done((bf16[128,640]{1,0:T(8,128)(2,1)S(1)}, bf16[128,640]{1,0:T(8,128)(2,1)S(1)}, u32[]{:S(2)}, u32[]{:S(2)}) %collective-permute-start.44) | collective-permute-done | bytes 163872 | tf_op jit(solution)/shard_map/ppermute | solution.py:513
  112.6 1.5 %collective-permute-start.36 = (f32[8,1024]{1,0:T(8,128)S(1)}, f32[8,1024]{1,0:T(8,128)S(1)}, u32[]{:S(2)}, u32[]{:S(2)}) collective-permute-start(f32[8,1024]{1,0:T(8,128)S(1)} %get-tuple-element.158.refs_0_), channel_id=1, source_target_pairs={{0,24},{4,28},{8,16},{12,20},{16,8},{20,12},{24,0},{28,4},{1,25},{... | collective-permute-start | bytes 98312 | tf_op jit(solution)/shard_map/ppermute | solution.py:513
  114.1 0.6 other_sum.3
  114.7 1.6 %collective-permute-start.43 = (bf16[128,640]{1,0:T(8,128)(2,1)S(1)}, bf16[128,640]{1,0:T(8,128)(2,1)S(1)}, u32[]{:S(2)}, u32[]{:S(2)}) collective-permute-start(bf16[128,640]{1,0:T(8,128)(2,1)S(1)} %get-tuple-element.173), channel_id=1, source_target_pairs={{0,8},{4,12},{8,0},{12,4},{16,24},{20,28},{24,16},{28,20},{1,9},{5... | collective-permute-start | bytes 491528 | tf_op jit(solution)/shard_map/ppermute | solution.py:513
  116.3 1.4 collective-permute-done.36.refs_3_
  117.7 0.7 second_round.1
  118.4 1.6 %collective-permute-start.41 = (bf16[128,896]{1,0:T(8,128)(2,1)S(1)}, bf16[128,896]{1,0:T(8,128)(2,1)S(1)}, u32[]{:S(2)}, u32[]{:S(2)}) collective-permute-start(bf16[128,896]{1,0:T(8,128)(2,1)S(1)} %get-tuple-element.166), channel_id=1, source_target_pairs={{0,16},{4,20},{8,24},{12,28},{16,0},{20,4},{24,8},{28,12},{1,17},{... | collective-permute-start | bytes 688136 | tf_op jit(solution)/shard_map/ppermute | solution.py:513
  120.1 2.9 %collective-permute-start.38 = (bf16[144,1024]{1,0:T(8,128)(2,1)S(1)}, bf16[144,1024]{1,0:T(8,128)(2,1)S(1)}, u32[]{:S(2)}, u32[]{:S(2)}) collective-permute-start(bf16[144,1024]{1,0:T(8,128)(2,1)S(1)} %get-tuple-element.160), channel_id=1, source_target_pairs={{0,2},{1,3},{2,0},{3,1},{4,6},{5,7},{6,4},{7,5},{8,10},{9,11},{10,... | collective-permute-start | bytes 884744 | tf_op jit(solution)/shard_map/ppermute | solution.py:516
  123.0 0.8 fusion.3
  123.8 1.3 collective-permute-start.39
  125.2 0.6 slice_reduce_fusion
  125.8 0.6 slice.52
  126.6 1.4 %join_halves.3 = (f32[128,256]{1,0:T(8,128)}, f32[128,1024]{1,0:T(8,128)}) custom-call(s32[4]{0:T(128)S(1)} %pad_add_fusion.1.place.refs_0_, bf16[128,640]{1,0:T(8,128)(2,1)S(1)} %get-tuple-element.123.refs_0_, bf16[256,640]{1,0:T(8,128)(2,1)S(1)} %collective-permute-done.27.from_y.refs_1_, bf16[128,640]{1,0:T(8,128)(2,1)S(1)} %collective-permute-done.43.refs_2_, ...), custom_call_target="tpu_custom_call" | custom-call | flops 11500000 | tf_op jit(solution)/shard_map/join_halves/pallas_call | solution.py:43
  128.1 0.6 other_sum.2
  128.8 5.8 %collective-permute-done.39.third = f32[8,1024]{1,0:T(8,128)S(1)} collective-permute-done((f32[8,1024]{1,0:T(8,128)S(1)}, f32[8,1024]{1,0:T(8,128)S(1)}, u32[]{:S(2)}, u32[]{:S(2)}) %collective-permute-start.39) | collective-permute-done | bytes 32800 | tf_op jit(solution)/shard_map/ppermute | solution.py:516
  135.2 1.1 finish_rows.1
  136.2 0.6 fusion.11
  136.9 0.9 pad_maximum_fusion.1
  137.7 1.6 %join_halves.2 = (f32[128,768]{1,0:T(8,128)}, f32[128,1024]{1,0:T(8,128)}) custom-call(s32[4]{0:T(128)S(1)} %pad_add_fusion.1.place.refs_0_, bf16[128,896]{1,0:T(8,128)(2,1)S(1)} %get-tuple-element.141.refs_0_, bf16[256,896]{1,0:T(8,128)(2,1)S(1)} %collective-permute-done.32.from_y.refs_1_, bf16[128,896]{1,0:T(8,128)(2,1)S(1)} %collective-permute-done.40.refs_2_, ...), custom_call_target="tpu_custom_call" | custom-call | flops 11500000 | tf_op jit(solution)/shard_map/join_halves/pallas_call | solution.py:43
  139.3 0.6 copy.31
  (93 shorter events, 7.7 us)
Async XLA Ops:
  0.6 11.9 %copy-start.2 = (s32[512]{0:T(512)S(1)}, s32[512]{0:T(512)}, u32[]{:S(2)}) copy-start(s32[512]{0:T(512)} %param.16) | copy-start | bytes 6148
  2.7 12.1 %collective-permute-start.3 = (bf16[128,1536]{1,0:T(8,128)(2,1)S(1)}, bf16[128,1536]{1,0:T(8,128)(2,1)S(1)}, u32[]{:S(2)}, u32[]{:S(2)}) collective-permute-start(bf16[128,1536]{1,0:T(8,128)(2,1)S(1)} %get-tuple-element.97.refs_13_), channel_id=1, source_target_pairs={{0,8},{4,12},{8,0},{12,4},{16,24},{20,28},{24,16},{28,20},{1,9},{5... | collective-permute-start | bytes 1179656 | tf_op jit(solution)/shard_map/ppermute | solution.py:513
  5.7 13.0 %collective-permute-start.4 = (bf16[128,1536]{1,0:T(8,128)(2,1)S(1)}, bf16[128,1536]{1,0:T(8,128)(2,1)S(1)}, u32[]{:S(2)}, u32[]{:S(2)}) collective-permute-start(bf16[128,1536]{1,0:T(8,128)(2,1)S(1)} %get-tuple-element.97.refs_13_), channel_id=1, source_target_pairs={{0,16},{4,20},{8,24},{12,28},{16,0},{20,4},{24,8},{28,12},{1,17},{... | collective-permute-start | bytes 1179656 | tf_op jit(solution)/shard_map/ppermute | solution.py:513
  8.3 16.4 %collective-permute-start = (bf16[128,1024]{1,0:T(8,128)(2,1)S(1)}, bf16[128,1024]{1,0:T(8,128)(2,1)S(1)}, u32[]{:S(2)}, u32[]{:S(2)}) collective-permute-start(bf16[128,1024]{1,0:T(8,128)(2,1)S(1)} %pad_maximum_fusion.2.refs_5_.x), channel_id=1, source_target_pairs={{0,1},{1,0},{2,3},{3,2},{4,5},{5,4},{6,7},{7,6},{8,9},{9,8},{10,11... | collective-permute-start | bytes 786440 | tf_op jit(solution)/shard_map/ppermute | solution.py:516
  10.0 20.7 %collective-permute-start.1 = (bf16[128,1024]{1,0:T(8,128)(2,1)S(1)}, bf16[128,1024]{1,0:T(8,128)(2,1)}, u32[]{:S(2)}, u32[]{:S(2)}) collective-permute-start(bf16[128,1024]{1,0:T(8,128)(2,1)S(1)} %pad_maximum_fusion.2.refs_5_.x), channel_id=1, source_target_pairs={{0,2},{1,3},{2,0},{3,1},{4,6},{5,7},{6,4},{7,5},{8,10},{9,11},{10,... | collective-permute-start | bytes 786440 | tf_op jit(solution)/shard_map/ppermute | solution.py:516
  12.5 6.1 %collective-permute-start.5 = (bf16[128,1536]{1,0:T(8,128)(2,1)S(1)}, bf16[128,1536]{1,0:T(8,128)(2,1)}, u32[]{:S(2)}, u32[]{:S(2)}) collective-permute-start(bf16[128,1536]{1,0:T(8,128)(2,1)S(1)} %get-tuple-element.99), channel_id=1, source_target_pairs={{0,4},{4,0},{8,12},{12,8},{16,20},{20,16},{24,28},{28,24},{1,5},{5... | collective-permute-start | bytes 1179656 | tf_op jit(solution)/shard_map/ppermute | solution.py:510
  14.8 15.9 %collective-permute-start.2 = (bf16[128,1024]{1,0:T(8,128)(2,1)S(1)}, bf16[128,1024]{1,0:T(8,128)(2,1)}, u32[]{:S(2)}, u32[]{:S(2)}) collective-permute-start(bf16[128,1024]{1,0:T(8,128)(2,1)S(1)} %pad_maximum_fusion.2.refs_5_.x), channel_id=1, source_target_pairs={{0,3},{1,2},{2,1},{3,0},{4,7},{5,6},{6,5},{7,4},{8,11},{9,10},{10,... | collective-permute-start | bytes 786440 | tf_op jit(solution)/shard_map/ppermute | solution.py:516
  18.6 1.6 %collective-permute-start.8 = (s32[512]{0:T(512)S(1)}, s32[512]{0:T(512)S(1)}, u32[]{:S(2)}, u32[]{:S(2)}) collective-permute-start(s32[512]{0:T(512)S(1)} %copy-done.2), channel_id=1, source_target_pairs={{0,4},{4,0},{8,12},{12,8},{16,20},{20,16},{24,28},{28,24},{1,5},{5... | collective-permute-start | bytes 6152 | tf_op jit(solution)/shard_map/ppermute | solution.py:510
  18.7 12.0 %collective-permute-start.6 = (bf16[128,1536]{1,0:T(8,128)(2,1)}, bf16[128,1536]{1,0:T(8,128)(2,1)}, u32[]{:S(2)}, u32[]{:S(2)}) collective-permute-start(bf16[128,1536]{1,0:T(8,128)(2,1)} %collective-permute-done.5.refs_14_), channel_id=1, source_target_pairs={{0,8},{4,12},{8,0},{12,4},{16,24},{20,28},{24,16},{28,20},{1,9},{5... | collective-permute-start | bytes 1179656 | tf_op jit(solution)/shard_map/ppermute | solution.py:513
  20.2 11.5 %collective-permute-start.7 = (bf16[128,1536]{1,0:T(8,128)(2,1)}, bf16[128,1536]{1,0:T(8,128)(2,1)}, u32[]{:S(2)}, u32[]{:S(2)}) collective-permute-start(bf16[128,1536]{1,0:T(8,128)(2,1)} %collective-permute-done.5.refs_14_), channel_id=1, source_target_pairs={{0,16},{4,20},{8,24},{12,28},{16,0},{20,4},{24,8},{28,12},{1,17},{... | collective-permute-start | bytes 1179656 | tf_op jit(solution)/shard_map/ppermute | solution.py:513
  24.2 17.4 %copy-start.5 = (f32[1024]{0:T(1024)S(1)}, f32[1024]{0:T(1024)}, u32[]{:S(2)}) copy-start(f32[1024]{0:T(1024)} %param.20) | copy-start | bytes 12292
  24.2 17.4 %copy-start.6 = (f32[1024]{0:T(1024)S(1)}, f32[1024]{0:T(1024)}, u32[]{:S(2)}) copy-start(f32[1024]{0:T(1024)} %param.19) | copy-start | bytes 12292
  24.3 17.4 %copy-start.7 = (f32[1024]{0:T(1024)S(1)}, f32[1024]{0:T(1024)}, u32[]{:S(2)}) copy-start(f32[1024]{0:T(1024)} %param.18) | copy-start | bytes 12292
  24.7 8.8 %collective-permute-start.10 = (bf16[128,1024]{1,0:T(8,128)(2,1)S(1)}, bf16[128,1024]{1,0:T(8,128)(2,1)}, u32[]{:S(2)}, u32[]{:S(2)}) collective-permute-start(bf16[128,1024]{1,0:T(8,128)(2,1)S(1)} %pad_maximum_fusion.2.refs_5_.x), channel_id=1, source_target_pairs={{0,4},{4,0},{8,12},{12,8},{16,20},{20,16},{24,28},{28,24},{1,5},{5... | collective-permute-start | bytes 786440 | tf_op jit(solution)/shard_map/ppermute | solution.py:510
  31.7 3.3 %collective-permute-start.9 = (bf16[128,1024]{1,0:T(8,128)(2,1)S(1)}, bf16[128,1024]{1,0:T(8,128)(2,1)}, u32[]{:S(2)}, u32[]{:S(2)}) collective-permute-start(bf16[128,1024]{1,0:T(8,128)(2,1)S(1)} %maximum_select_fusion.refs_0_.cot), channel_id=1, source_target_pairs={{0,4},{4,0},{8,12},{12,8},{16,20},{20,16},{24,28},{28,24},{1,5},{5... | collective-permute-start | bytes 786440 | tf_op jit(solution)/shard_map/ppermute | solution.py:510
  31.7 5.0 %collective-permute-start.11 = (bf16[128,1024]{1,0:T(8,128)(2,1)S(1)}, bf16[128,1024]{1,0:T(8,128)(2,1)}, u32[]{:S(2)}, u32[]{:S(2)}) collective-permute-start(bf16[128,1024]{1,0:T(8,128)(2,1)S(1)} %collective-permute-done.refs_6_), channel_id=1, source_target_pairs={{0,4},{4,0},{8,12},{12,8},{16,20},{20,16},{24,28},{28,24},{1,5},{5... | collective-permute-start | bytes 786440 | tf_op jit(solution)/shard_map/ppermute | solution.py:510
  32.2 6.9 %collective-permute-start.12 = (bf16[128,1024]{1,0:T(8,128)(2,1)}, bf16[128,1024]{1,0:T(8,128)(2,1)}, u32[]{:S(2)}, u32[]{:S(2)}) collective-permute-start(bf16[128,1024]{1,0:T(8,128)(2,1)} %collective-permute-done.1.refs_7_), channel_id=1, source_target_pairs={{0,4},{4,0},{8,12},{12,8},{16,20},{20,16},{24,28},{28,24},{1,5},{5... | collective-permute-start | bytes 786440 | tf_op jit(solution)/shard_map/ppermute | solution.py:510
  32.2 8.0 %collective-permute-start.13 = (bf16[128,1024]{1,0:T(8,128)(2,1)}, bf16[128,1024]{1,0:T(8,128)(2,1)}, u32[]{:S(2)}, u32[]{:S(2)}) collective-permute-start(bf16[128,1024]{1,0:T(8,128)(2,1)} %collective-permute-done.2.refs_8_), channel_id=1, source_target_pairs={{0,4},{4,0},{8,12},{12,8},{16,20},{20,16},{24,28},{28,24},{1,5},{5... | collective-permute-start | bytes 786440 | tf_op jit(solution)/shard_map/ppermute | solution.py:510
  33.5 11.8 %collective-permute-start.14 = (bf16[128,1536]{1,0:T(8,128)(2,1)S(1)}, bf16[128,1536]{1,0:T(8,128)(2,1)}, u32[]{:S(2)}, u32[]{:S(2)}) collective-permute-start(bf16[128,1536]{1,0:T(8,128)(2,1)S(1)} %collective-permute-done.3.refs_15_), channel_id=1, source_target_pairs={{0,16},{4,20},{8,24},{12,28},{16,0},{20,4},{24,8},{28,12},{1,17},{... | collective-permute-start | bytes 1179656 | tf_op jit(solution)/shard_map/ppermute | solution.py:513
  35.0 11.1 %collective-permute-start.15 = (bf16[128,1536]{1,0:T(8,128)(2,1)}, bf16[128,1536]{1,0:T(8,128)(2,1)}, u32[]{:S(2)}, u32[]{:S(2)}) collective-permute-start(bf16[128,1536]{1,0:T(8,128)(2,1)} %collective-permute-done.7.refs_18_), channel_id=1, source_target_pairs={{0,8},{4,12},{8,0},{12,4},{16,24},{20,28},{24,16},{28,20},{1,9},{5... | collective-permute-start | bytes 1179656 | tf_op jit(solution)/shard_map/ppermute | solution.py:513
  36.7 21.3 %collective-permute-start.16 = (bf16[128,1024]{1,0:T(8,128)(2,1)S(1)}, bf16[128,1024]{1,0:T(8,128)(2,1)}, u32[]{:S(2)}, u32[]{:S(2)}) collective-permute-start(bf16[128,1024]{1,0:T(8,128)(2,1)S(1)} %maximum_select_fusion.refs_0_.cot), channel_id=1, source_target_pairs={{0,1},{1,0},{2,3},{3,2},{4,5},{5,4},{6,7},{7,6},{8,9},{9,8},{10,11... | collective-permute-start | bytes 786440 | tf_op jit(solution)/shard_map/ppermute | solution.py:516
  39.1 21.5 %collective-permute-start.17 = (bf16[128,1024]{1,0:T(8,128)(2,1)S(1)}, bf16[128,1024]{1,0:T(8,128)(2,1)}, u32[]{:S(2)}, u32[]{:S(2)}) collective-permute-start(bf16[128,1024]{1,0:T(8,128)(2,1)S(1)} %maximum_select_fusion.refs_0_.cot), channel_id=1, source_target_pairs={{0,2},{1,3},{2,0},{3,1},{4,6},{5,7},{6,4},{7,5},{8,10},{9,11},{10,... | collective-permute-start | bytes 786440 | tf_op jit(solution)/shard_map/ppermute | solution.py:516
  40.2 20.4 %collective-permute-start.18 = (bf16[128,1024]{1,0:T(8,128)(2,1)S(1)}, bf16[128,1024]{1,0:T(8,128)(2,1)}, u32[]{:S(2)}, u32[]{:S(2)}) collective-permute-start(bf16[128,1024]{1,0:T(8,128)(2,1)S(1)} %maximum_select_fusion.refs_0_.cot), channel_id=1, source_target_pairs={{0,3},{1,2},{2,1},{3,0},{4,7},{5,6},{6,5},{7,4},{8,11},{9,10},{10,... | collective-permute-start | bytes 786440 | tf_op jit(solution)/shard_map/ppermute | solution.py:516
  60.6 3.8 %collective-permute-start.19 = (bf16[512,1024]{1,0:T(8,128)(2,1)S(1)}, bf16[512,1024]{1,0:T(8,128)(2,1)S(1)}, u32[]{:S(2)}, u32[]{:S(2)}) collective-permute-start(bf16[512,1024]{1,0:T(8,128)(2,1)S(1)} %get-tuple-element.115), channel_id=1, source_target_pairs={{0,4},{4,0},{8,12},{12,8},{16,20},{20,16},{24,28},{28,24},{1,5},{5... | collective-permute-start | bytes 3145736 | tf_op jit(solution)/shard_map/ppermute | solution.py:510
  60.6 9.1 %collective-permute-start.21 = (bf16[128,1024]{1,0:T(8,128)(2,1)}, bf16[128,1024]{1,0:T(8,128)(2,1)S(1)}, u32[]{:S(2)}, u32[]{:S(2)}) collective-permute-start(bf16[128,1024]{1,0:T(8,128)(2,1)} %collective-permute-done.16.refs_1_), channel_id=1, source_target_pairs={{0,4},{4,0},{8,12},{12,8},{16,20},{20,16},{24,28},{28,24},{1,5},{5... | collective-permute-start | bytes 786440 | tf_op jit(solution)/shard_map/ppermute | solution.py:510
  61.1 9.3 %collective-permute-start.22 = (bf16[128,1024]{1,0:T(8,128)(2,1)}, bf16[128,1024]{1,0:T(8,128)(2,1)S(1)}, u32[]{:S(2)}, u32[]{:S(2)}) collective-permute-start(bf16[128,1024]{1,0:T(8,128)(2,1)} %collective-permute-done.17.refs_2_), channel_id=1, source_target_pairs={{0,4},{4,0},{8,12},{12,8},{16,20},{20,16},{24,28},{28,24},{1,5},{5... | collective-permute-start | bytes 786440 | tf_op jit(solution)/shard_map/ppermute | solution.py:510
  61.1 9.3 %collective-permute-start.23 = (bf16[128,1024]{1,0:T(8,128)(2,1)}, bf16[128,1024]{1,0:T(8,128)(2,1)S(1)}, u32[]{:S(2)}, u32[]{:S(2)}) collective-permute-start(bf16[128,1024]{1,0:T(8,128)(2,1)} %collective-permute-done.18.refs_3_), channel_id=1, source_target_pairs={{0,4},{4,0},{8,12},{12,8},{16,20},{20,16},{24,28},{28,24},{1,5},{5... | collective-permute-start | bytes 786440 | tf_op jit(solution)/shard_map/ppermute | solution.py:510
  65.2 12.1 %collective-permute-start.24 = (bf16[128,1024]{1,0:T(8,128)(2,1)S(1)}, bf16[128,1024]{1,0:T(8,128)(2,1)S(1)}, u32[]{:S(2)}, u32[]{:S(2)}) collective-permute-start(bf16[128,1024]{1,0:T(8,128)(2,1)S(1)} %get-tuple-element.126), channel_id=1, source_target_pairs={{0,1},{1,0},{2,3},{3,2},{4,5},{5,4},{6,7},{7,6},{8,9},{9,8},{10,11... | collective-permute-start | bytes 786440 | tf_op jit(solution)/shard_map/ppermute | solution.py:516
  69.7 25.8 %collective-permute-start.20 = (bf16[128,1024]{1,0:T(8,128)(2,1)S(1)}, bf16[128,1024]{1,0:T(8,128)(2,1)S(1)}, u32[]{:S(2)}, u32[]{:S(2)}) collective-permute-start(bf16[128,1024]{1,0:T(8,128)(2,1)S(1)} %get-tuple-element.117), channel_id=1, source_target_pairs={{0,1},{1,0},{2,3},{3,2},{4,5},{5,4},{6,7},{7,6},{8,9},{9,8},{10,11... | collective-permute-start | bytes 786440 | tf_op jit(solution)/shard_map/ppermute | solution.py:516
  69.8 25.7 %collective-permute-start.26 = (bf16[128,1024]{1,0:T(8,128)(2,1)S(1)}, bf16[128,1024]{1,0:T(8,128)(2,1)S(1)}, u32[]{:S(2)}, u32[]{:S(2)}) collective-permute-start(bf16[128,1024]{1,0:T(8,128)(2,1)S(1)} %get-tuple-element.126), channel_id=1, source_target_pairs={{0,0},{1,2},{2,1},{3,3},{4,4},{5,6},{6,5},{7,7},{8,8},{9,10},{10,9... | collective-permute-start | bytes 786440 | tf_op jit(solution)/shard_map/ppermute | solution.py:525
  74.2 21.3 %collective-permute-start.27 = (bf16[256,640]{1,0:T(8,128)(2,1)S(1)}, bf16[256,640]{1,0:T(8,128)(2,1)S(1)}, u32[]{:S(2)}, u32[]{:S(2)}) collective-permute-start(bf16[256,640]{1,0:T(8,128)(2,1)S(1)} %get-tuple-element.127), channel_id=1, source_target_pairs={{0,16},{4,20},{8,24},{12,28},{16,0},{20,4},{24,8},{28,12},{1,17},{... | collective-permute-start | bytes 983048 | tf_op jit(solution)/shard_map/ppermute | solution.py:513
  75.8 19.8 %collective-permute-start.28 = (bf16[256,640]{1,0:T(8,128)(2,1)S(1)}, bf16[256,640]{1,0:T(8,128)(2,1)S(1)}, u32[]{:S(2)}, u32[]{:S(2)}) collective-permute-start(bf16[256,640]{1,0:T(8,128)(2,1)S(1)} %get-tuple-element.128), channel_id=1, source_target_pairs={{0,8},{4,12},{8,0},{12,4},{16,24},{20,28},{24,16},{28,20},{1,9},{5... | collective-permute-start | bytes 983048 | tf_op jit(solution)/shard_map/ppermute | solution.py:513
  77.9 17.6 %collective-permute-start.25 = (bf16[128,1024]{1,0:T(8,128)(2,1)S(1)}, bf16[128,1024]{1,0:T(8,128)(2,1)S(1)}, u32[]{:S(2)}, u32[]{:S(2)}) collective-permute-start(bf16[128,1024]{1,0:T(8,128)(2,1)S(1)} %branch_relay.1), channel_id=1, source_target_pairs={{0,2},{1,3},{2,0},{3,1},{4,6},{5,7},{6,4},{7,5},{8,10},{9,11},{10,... | collective-permute-start | bytes 786440 | tf_op jit(solution)/shard_map/ppermute | solution.py:516
  95.5 2.8 %collective-permute-start.29 = (bf16[528,1024]{1,0:T(8,128)(2,1)S(1)}, bf16[528,1024]{1,0:T(8,128)(2,1)S(1)}, u32[]{:S(2)}, u32[]{:S(2)}) collective-permute-start(bf16[528,1024]{1,0:T(8,128)(2,1)S(1)} %get-tuple-element.147), channel_id=1, source_target_pairs={{0,4},{4,0},{8,12},{12,8},{16,20},{20,16},{24,28},{28,24},{1,5},{5... | collective-permute-start | bytes 3244040 | tf_op jit(solution)/shard_map/ppermute | solution.py:510
  95.6 13.4 %collective-permute-start.32 = (bf16[256,896]{1,0:T(8,128)(2,1)S(1)}, bf16[256,896]{1,0:T(8,128)(2,1)S(1)}, u32[]{:S(2)}, u32[]{:S(2)}) collective-permute-start(bf16[256,896]{1,0:T(8,128)(2,1)S(1)} %get-tuple-element.156), channel_id=1, source_target_pairs={{0,16},{4,20},{8,24},{12,28},{16,0},{20,4},{24,8},{28,12},{1,17},{... | collective-permute-start | bytes 1376264 | tf_op jit(solution)/shard_map/ppermute | solution.py:513
  96.2 18.5 %collective-permute-start.33 = (bf16[256,896]{1,0:T(8,128)(2,1)S(1)}, bf16[256,896]{1,0:T(8,128)(2,1)S(1)}, u32[]{:S(2)}, u32[]{:S(2)}) collective-permute-start(bf16[256,896]{1,0:T(8,128)(2,1)S(1)} %get-tuple-element.157), channel_id=1, source_target_pairs={{0,8},{4,12},{8,0},{12,4},{16,24},{20,28},{24,16},{28,20},{1,9},{5... | collective-permute-start | bytes 1376264 | tf_op jit(solution)/shard_map/ppermute | solution.py:513
  99.1 13.5 %collective-permute-start.30 = (bf16[128,1024]{1,0:T(8,128)(2,1)S(1)}, bf16[128,1024]{1,0:T(8,128)(2,1)S(1)}, u32[]{:S(2)}, u32[]{:S(2)}) collective-permute-start(bf16[128,1024]{1,0:T(8,128)(2,1)S(1)} %get-tuple-element.150), channel_id=1, source_target_pairs={{0,0},{1,2},{2,1},{3,3},{4,4},{5,6},{6,5},{7,7},{8,8},{9,10},{10,9... | collective-permute-start | bytes 786440 | tf_op jit(solution)/shard_map/ppermute | solution.py:525
  99.8 17.9 %collective-permute-start.31 = (bf16[128,1024]{1,0:T(8,128)(2,1)S(1)}, bf16[128,1024]{1,0:T(8,128)(2,1)S(1)}, u32[]{:S(2)}, u32[]{:S(2)}) collective-permute-start(bf16[128,1024]{1,0:T(8,128)(2,1)S(1)} %get-tuple-element.150), channel_id=1, source_target_pairs={{0,1},{1,0},{2,3},{3,2},{4,5},{5,4},{6,7},{7,6},{8,9},{9,8},{10,11... | collective-permute-start | bytes 786440 | tf_op jit(solution)/shard_map/ppermute | solution.py:516
  102.2 9.8 %collective-permute-start.44 = (bf16[128,640]{1,0:T(8,128)(2,1)S(1)}, bf16[128,640]{1,0:T(8,128)(2,1)S(1)}, u32[]{:S(2)}, u32[]{:S(2)}) collective-permute-start(bf16[128,640]{1,0:T(8,128)(2,1)S(1)} %get-tuple-element.176), channel_id=1, source_target_pairs={{0,16},{4,20},{8,24},{12,28},{16,0},{20,4},{24,8},{28,12},{1,17},{... | collective-permute-start | bytes 491528 | tf_op jit(solution)/shard_map/ppermute | solution.py:513
  109.0 14.0 %copy-start = (bf16[128,1024]{1,0:T(8,128)(2,1)S(1)}, bf16[128,1024]{1,0:T(8,128)(2,1)}, u32[]{:S(2)}) copy-start(bf16[128,1024]{1,0:T(8,128)(2,1)} %param.15) | copy-start | bytes 786436
  109.0 14.0 %copy-start.3 = (f32[1024]{0:T(1024)S(1)}, f32[1024]{0:T(1024)}, u32[]{:S(2)}) copy-start(f32[1024]{0:T(1024)} %param.28) | copy-start | bytes 12292
  109.0 14.0 %copy-start.4 = (f32[1024]{0:T(1024)S(1)}, f32[1024]{0:T(1024)}, u32[]{:S(2)}) copy-start(f32[1024]{0:T(1024)} %param.24) | copy-start | bytes 12292
  109.0 7.3 %collective-permute-start.34 = (f32[8,1024]{1,0:T(8,128)S(1)}, f32[8,1024]{1,0:T(8,128)S(1)}, u32[]{:S(2)}, u32[]{:S(2)}) collective-permute-start(f32[8,1024]{1,0:T(8,128)S(1)} %get-tuple-element.158.refs_0_), channel_id=1, source_target_pairs={{0,8},{4,12},{8,0},{12,4},{16,24},{20,28},{24,16},{28,20},{1,9},{5... | collective-permute-start | bytes 98312 | tf_op jit(solution)/shard_map/ppermute | solution.py:513
  112.1 4.2 %collective-permute-start.35 = (f32[8,1024]{1,0:T(8,128)S(1)}, f32[8,1024]{1,0:T(8,128)S(1)}, u32[]{:S(2)}, u32[]{:S(2)}) collective-permute-start(f32[8,1024]{1,0:T(8,128)S(1)} %get-tuple-element.158.refs_0_), channel_id=1, source_target_pairs={{0,16},{4,20},{8,24},{12,28},{16,0},{20,4},{24,8},{28,12},{1,17},{... | collective-permute-start | bytes 98312 | tf_op jit(solution)/shard_map/ppermute | solution.py:513
  112.6 5.1 %collective-permute-start.36 = (f32[8,1024]{1,0:T(8,128)S(1)}, f32[8,1024]{1,0:T(8,128)S(1)}, u32[]{:S(2)}, u32[]{:S(2)}) collective-permute-start(f32[8,1024]{1,0:T(8,128)S(1)} %get-tuple-element.158.refs_0_), channel_id=1, source_target_pairs={{0,24},{4,28},{8,16},{12,20},{16,8},{20,12},{24,0},{28,4},{1,25},{... | collective-permute-start | bytes 98312 | tf_op jit(solution)/shard_map/ppermute | solution.py:513
  114.7 9.1 %collective-permute-start.43 = (bf16[128,640]{1,0:T(8,128)(2,1)S(1)}, bf16[128,640]{1,0:T(8,128)(2,1)S(1)}, u32[]{:S(2)}, u32[]{:S(2)}) collective-permute-start(bf16[128,640]{1,0:T(8,128)(2,1)S(1)} %get-tuple-element.173), channel_id=1, source_target_pairs={{0,8},{4,12},{8,0},{12,4},{16,24},{20,28},{24,16},{28,20},{1,9},{5... | collective-permute-start | bytes 491528 | tf_op jit(solution)/shard_map/ppermute | solution.py:513
  116.3 10.1 %collective-permute-start.45 = (bf16[128,640]{1,0:T(8,128)(2,1)S(1)}, bf16[128,640]{1,0:T(8,128)(2,1)S(1)}, u32[]{:S(2)}, u32[]{:S(2)}) collective-permute-start(bf16[128,640]{1,0:T(8,128)(2,1)S(1)} %other_sum.3), channel_id=1, source_target_pairs={{0,4},{4,0},{8,12},{12,8},{16,20},{20,16},{24,28},{28,24},{1,5},{5... | collective-permute-start | bytes 491528 | tf_op jit(solution)/shard_map/ppermute | solution.py:510
  118.4 9.7 %collective-permute-start.41 = (bf16[128,896]{1,0:T(8,128)(2,1)S(1)}, bf16[128,896]{1,0:T(8,128)(2,1)S(1)}, u32[]{:S(2)}, u32[]{:S(2)}) collective-permute-start(bf16[128,896]{1,0:T(8,128)(2,1)S(1)} %get-tuple-element.166), channel_id=1, source_target_pairs={{0,16},{4,20},{8,24},{12,28},{16,0},{20,4},{24,8},{28,12},{1,17},{... | collective-permute-start | bytes 688136 | tf_op jit(solution)/shard_map/ppermute | solution.py:513
  120.0 14.6 %collective-permute-start.37 = (bf16[144,1024]{1,0:T(8,128)(2,1)S(1)}, bf16[144,1024]{1,0:T(8,128)(2,1)S(1)}, u32[]{:S(2)}, u32[]{:S(2)}) collective-permute-start(bf16[144,1024]{1,0:T(8,128)(2,1)S(1)} %get-tuple-element.159), channel_id=1, source_target_pairs={{0,1},{1,0},{2,3},{3,2},{4,5},{5,4},{6,7},{7,6},{8,9},{9,8},{10,11... | collective-permute-start | bytes 884744 | tf_op jit(solution)/shard_map/ppermute | solution.py:516
  120.1 15.1 %collective-permute-start.38 = (bf16[144,1024]{1,0:T(8,128)(2,1)S(1)}, bf16[144,1024]{1,0:T(8,128)(2,1)S(1)}, u32[]{:S(2)}, u32[]{:S(2)}) collective-permute-start(bf16[144,1024]{1,0:T(8,128)(2,1)S(1)} %get-tuple-element.160), channel_id=1, source_target_pairs={{0,2},{1,3},{2,0},{3,1},{4,6},{5,7},{6,4},{7,5},{8,10},{9,11},{10,... | collective-permute-start | bytes 884744 | tf_op jit(solution)/shard_map/ppermute | solution.py:516
  123.8 10.8 %collective-permute-start.39 = (f32[8,1024]{1,0:T(8,128)S(1)}, f32[8,1024]{1,0:T(8,128)S(1)}, u32[]{:S(2)}, u32[]{:S(2)}) collective-permute-start(f32[8,1024]{1,0:T(8,128)S(1)} %get-tuple-element.161.sums), channel_id=1, source_target_pairs={{0,3},{1,2},{2,1},{3,0},{4,7},{5,6},{6,5},{7,4},{8,11},{9,10},{10,... | collective-permute-start | bytes 98312 | tf_op jit(solution)/shard_map/ppermute | solution.py:516
  126.4 11.4 %collective-permute-start.40 = (bf16[128,896]{1,0:T(8,128)(2,1)S(1)}, bf16[128,896]{1,0:T(8,128)(2,1)S(1)}, u32[]{:S(2)}, u32[]{:S(2)}) collective-permute-start(bf16[128,896]{1,0:T(8,128)(2,1)S(1)} %get-tuple-element.164), channel_id=1, source_target_pairs={{0,8},{4,12},{8,0},{12,4},{16,24},{20,28},{24,16},{28,20},{1,9},{5... | collective-permute-start | bytes 688136 | tf_op jit(solution)/shard_map/ppermute | solution.py:513
  128.7 9.1 %collective-permute-start.42 = (bf16[128,896]{1,0:T(8,128)(2,1)S(1)}, bf16[128,896]{1,0:T(8,128)(2,1)S(1)}, u32[]{:S(2)}, u32[]{:S(2)}) collective-permute-start(bf16[128,896]{1,0:T(8,128)(2,1)S(1)} %other_sum.2), channel_id=1, source_target_pairs={{0,4},{4,0},{8,12},{12,8},{16,20},{20,16},{24,28},{28,24},{1,5},{5... | collective-permute-start | bytes 688136 | tf_op jit(solution)/shard_map/ppermute | solution.py:510
  136.8 3.1 %copy-start.1 = (f32[1,1024]{1,0:T(1,128)}, f32[1,1024]{1,0:T(1,128)S(1)}, u32[]{:S(2)}) copy-start(f32[1,1024]{1,0:T(1,128)S(1)} %get-tuple-element.196) | copy-start | bytes 12292

commit v3 on v2

--- a/solution.py
+++ b/solution.py
@@ -381,22 +381,17 @@
         out[:, nq + nf + nd :] = half(fc2, nf)
 
 
-def messages_body(place, to_x, to_y, from_y, from_x, out_x, out_y):
-    size = to_x.shape[0]
-    out_x[...] = to_x[...] + from_y[size : 2 * size, :]
-    out_y[...] = to_y[...] + from_x[size : 2 * size, :]
-
-
-def split_body(tz, place, own, other, sums, *outs):
+def split_body(tz, place, own, other, *refs):
+    sums, outs = refs[: -tz - 1], refs[-tz - 1 :]
     combine_body(tz, place, own, other, *outs[:tz])
-    outs[tz][...] = sums[...] + get_sums(other, own.shape[0])
-
-
-def shard_sum(mine, first, second, out):
-    size = out.shape[0]
-    out[...] = (
-        mine[...].astype(F32) + first[0:size, :].astype(F32) + second[...].astype(F32)
-    ).astype(BF)
+    add_sums(sums, outs[tz])
+
+
+def add_sums(refs, out):
+    total = refs[0][...]
+    for one in refs[1:]:
+        total = total + one[...]
+    out[...] = total
 
 
 def pass_body(place, shard, passed, out):
@@ -405,22 +400,33 @@
     out[0:rows, :] = (shard[...].astype(F32) + keep * passed[...].astype(F32)).astype(BF)
 
 
-def relay_body(place, near, shard, passed, to_x, to_y, from_y, from_x, *refs):
-    sums, (out_near, out_shard, out_x, out_y, out_sums) = refs[:-5], refs[-5:]
+def relay_body(place, near, shard, passed, *refs):
+    first, second, sums = refs[:4], refs[4:8], refs[8:-5]
+    out_near, out_shard, out_x, out_y, out_sums = refs[-5:]
     rows = near.shape[0]
-    total = sums[0][...]
-    for one in sums[1:]:
-        total = total + one[...]
-    out_sums[...] = total
+    add_sums(sums, out_sums)
+    total = out_sums[...]
     out_near[0:rows, :] = near[...]
     pass_body(place, shard, passed, out_shard)
     for out in (out_near, out_shard):
         put_sums(out, rows, total)
-    messages_body(place, to_x, to_y, from_y, from_x, out_x, out_y)
-
-
-def other_body(place, mine, first, second, out):
-    shard_sum(mine, first, second, out)
+    at = 0
+    for to_x, to_y, from_y, from_x in (first, second):
+        size, columns = to_x.shape
+        cols = slice(at, at + columns)
+        out_x[:, cols] = to_x[...] + from_y[size : 2 * size, :]
+        out_y[:, cols] = to_y[...] + from_x[size : 2 * size, :]
+        at += columns
+
+
+def other_body(place, first, first_x, second, second_x, from_y, out):
+    size, at = out.shape[0], 0
+    for mine, from_x in ((first, first_x), (second, second_x)):
+        cols = slice(at, at + mine.shape[1])
+        out[:, cols] = (
+            mine[...].astype(F32) + from_x[0:size, :].astype(F32) + from_y[:, cols].astype(F32)
+        ).astype(BF)
+        at += mine.shape[1]
 
 
 def finish_body(place, own, first, second, across, x, cot, sums, third, out_rows, out_sums):
@@ -447,10 +453,17 @@
 def join_body(heads, widths, count, place, *refs):
     parts, other, outs = refs[:count], refs[count], refs[count + 1 :]
     rows = other.shape[0]
-    total = parts[0][0:rows, :].astype(F32)
-    for one in parts[1:]:
-        total = total + one[0:rows, :].astype(F32)
-    for half, which in ((total, place[0]), (other[...].astype(F32), 1 - place[0])):
+    sums, at = [], 0
+    while at < count:
+        total, columns = parts[at][0:rows, :].astype(F32), parts[at].shape[1]
+        at += 1
+        while at < count and parts[at].shape[1] == columns:
+            total = total + parts[at][0:rows, :].astype(F32)
+            at += 1
+        sums.append(total)
+    if len(sums) == 3:
+        sums = [jnp.concatenate(sums[:2], axis=1) + sums[2]]
+    for half, which in ((sums[0], place[0]), (other[...].astype(F32), 1 - place[0])):
         at = 0
         for i, (out, size) in enumerate(zip(outs, widths)):
             value = half[:, at : at + size]
@@ -672,8 +685,10 @@
     )
 
     c_moved, part_sib = together(c_moved, part_sib)
-    branch_shards = add_sibling(place, part_own, sibling(part_sib))
-    c_shards = [masked] + c_moved + [masked_sib] + [sibling(one) for one in c_moved]
+    part_other = sibling(part_sib)
+    branch_shards = add_sibling(place, part_own, part_other)
+    c_shards = [masked] + c_moved + [masked_sib]
+    c_shards += [sibling(one) for one in after(c_moved, part_other)]
     if rounds:
         passed, across = over_tensor(branch_shards[3], 1), over_middle(branch_shards[3])
     cot, *second_parts = kernel_call(
@@ -753,6 +768,11 @@
 
     if rounds:
         back_other = sibling(back_sib)
+        first_parts = list(first_parts)
+        sums_chips = [over_chip(sums, flip) for flip in range(1, chips)]
+        first_parts[2], first_parts[3], sums_chips = together(
+            first_parts[2], first_parts[3], sums_chips
+        )
         first_first = first_round(first_parts)
         *back_shards, sums = kernel_call(
             partial(split_body, tz),
@@ -760,28 +780,19 @@
             [shape((rows, width), F32)]
             + [shape((rows, width), BF)] * 3
             + [shape(sums.shape, F32)],
-            (place, back_own, back_other, sums),
+            (place, back_own, back_other, sums, *sums_chips),
             [],
             LITTLE,
         )
         passed, across = over_tensor(back_shards[3], 1), over_middle(back_shards[3])
-        second_messages = kernel_call(
-            messages_body,
-            "second_messages",
-            [shape(second_parts[4].shape, BF)] * 2,
-            (after(place, back_other), second_parts[4], second_parts[5], *second_first),
-            [],
-            LITTLE,
-        )
-        second_x, second_y = over_chip(second_messages[0], 1), over_chip(second_messages[1], 2)
-        near, shard, first_x, first_y, sums = kernel_call(
+        near, shard, from_x, from_y, sums = kernel_call(
             relay_body,
             "second_round",
             [
                 shape((rows + 16, width), BF),
                 shape((rows + 16, width), BF),
-                shape(first_parts[4].shape, BF),
-                shape(first_parts[5].shape, BF),
+                shape((width // dp, wide), BF),
+                shape((width // dp, wide), BF),
                 shape(sums.shape, F32),
             ],
             (
@@ -792,8 +803,11 @@
                 first_parts[4],
                 first_parts[5],
                 *first_first,
+                second_parts[4],
+                second_parts[5],
+                *second_first,
                 sums,
-                *[over_chip(sums, flip) for flip in range(1, chips)],
+                sibling(sums),
             ),
             [],
             LITTLE,
@@ -801,32 +815,25 @@
         biases = sums
         back_second, back_first = over_tensor(shard, 2), over_tensor(near, 1)
         third = over_tensor(sums, 3)
-        first_x, first_y = over_chip(first_x, 1), over_chip(first_y, 2)
-
-        def other_sum(parts, first, second, where):
-            return kernel_call(
-                other_body,
-                "other_sum",
-                [shape(parts[1].shape, BF)],
-                (where, parts[1], first[1], second),
-                [],
-                LITTLE,
-            )[0]
-
-        second_sib = sibling(
-            other_sum(second_parts, second_first, second_y, after(place, first_parts[0]))
-        )
-        first_sib = sibling(other_sum(first_parts, first_first, first_y, place))
-        first_terms = [first_parts[0], first_first[0], first_x]
-        second_terms = [second_parts[0], second_first[0], second_x]
-        dense_grad, fc2_grad = join(second_terms, second_sib, (nd, nf), 0)
-        qkv_grad, fc1_grad = join(first_terms, first_sib, (nq, nf), heads)
+        from_x, from_y = over_chip(from_x, 1), over_chip(from_y, 2)
+        other = kernel_call(
+            other_body,
+            "other_sums",
+            [shape((width // dp, wide), BF)],
+            (place, first_parts[1], first_first[1], second_parts[1], second_first[1], from_y),
+            [],
+            LITTLE,
+        )[0]
+        own_parts = [first_parts[0], first_first[0], second_parts[0], second_first[0], from_x]
+        qkv_grad, fc1_grad, dense_grad, fc2_grad = join(
+            own_parts, sibling(other), (nq, nf, nd, nf), heads
+        )
         input_grad, sums = kernel_call(
             finish_body,
             "finish_rows",
             [shape((rows, width), F32), shape(sums.shape, F32)],
             (
-                place,
+                after(place, other),
                 back_shards[0],
                 back_first,
                 back_second,

time: 140 us -> 137 us (0.979)
  Pallas kernels: 39.1 us -> 36.9 us
    ppermute x13, waiting for transfers between devices: 14.9 us -> 17.9 us  [over_tensor(): return lax.ppermute(values, 'tensor', xor_pairs(tz, flip))]
    pallas_call x15 -> x12, Pallas kernels: 39.1 us -> 36.9 us  [kernel_call(): pl.pallas_call(body, name=name, out_shape=outs, in_specs=[SMEM] + [VMEM]...]
    ppermute x17 -> x15, waiting for transfers between devices: 13.8 us -> 12.1 us  [over_chip(): return lax.ppermute(values, 'dp', xor_pairs(dp, 2 * flip))]
    ppermute x14, waiting for transfers between devices: 4.38 us -> 2.69 us  [sibling(): return lax.ppermute(values, 'dp', xor_pairs(dp, 1))]
    ppermute x13, starting transfers between devices: 28.6 us -> 27.1 us  [over_tensor(): return lax.ppermute(values, 'tensor', xor_pairs(tz, flip))]
    ppermute x17 -> x15, starting transfers between devices: 20.9 us -> 21.9 us  [over_chip(): return lax.ppermute(values, 'dp', xor_pairs(dp, 2 * flip))]
  transfers between devices with their start and end apart: 46 -> 44, of which waited for: 12 -> 14; matrix products, arithmetic and copies ran while one was open for 9% -> 9% of each run, Pallas kernels for 25% -> 24%
where the time goes in v3:
time: 137 us; the launch traced here: 136 us
  starting transfers between devices  52.2 us (38%)
  Pallas kernels  36.9 us (27%)
  waiting for transfers between devices  32.7 us (24%)
  local copies, waits for them, and re-layouts  7.32 us (5%)
  other arithmetic  6.29 us (5%)
    pallas_call x12, Pallas kernels, kernel_call(): pl.pallas_call(body, name=name, out_shape=outs, in_specs=[SMEM] + [VMEM]...  36.9 us
    ppermute x13, starting transfers between devices, over_tensor(): return lax.ppermute(values, 'tensor', xor_pairs(tz, flip))  27.1 us
    ppermute x15, starting transfers between devices, over_chip(): return lax.ppermute(values, 'dp', xor_pairs(dp, 2 * flip))  21.9 us
    ppermute x13, waiting for transfers between devices, over_tensor(): return lax.ppermute(values, 'tensor', xor_pairs(tz, flip))  17.9 us
    ppermute x15, waiting for transfers between devices, over_chip(): return lax.ppermute(values, 'dp', xor_pairs(dp, 2 * flip))  12.1 us
  transfers between devices with their start and end apart: 44, of which 14 were waited for; matrix products, arithmetic and copies ran while one was open for 9% of the time, Pallas kernels for 24%

profile of v3, /device:TPU:0, one launch (start us, length us, event | category | flops | bytes accessed | tf_op | source)
XLA Modules:
  0.0 136.4 jit_solution(3778804812293593241)
XLA Ops:
  0.8 1.9 %pack_weights.1 = (bf16[128,1536]{1,0:T(8,128)(2,1)S(1)}, bf16[128,1536]{1,0:T(8,128)(2,1)S(1)}) custom-call(s32[4]{0:T(128)S(1)} %pad_add_fusion.1.place.refs_0_, bf16[128,768]{1,0:T(8,128)(2,1)} %qkv_in.1, bf16[128,1024]{1,0:T(8,128)(2,1)} %fc1_in.1, bf16[128,256]{1,0:T(8,128)(2,1)} %dense_in.1, bf16[128,1024]{1,0:T(8,128)(2,1)} %fc2_in.1), custom_call_target="tpu_custom_call" | custom-call | flops 11500000 | tf_op jit(solution)/shard_map/pack_weights/pallas_call | solution.py:43
  2.7 3.0 %collective-permute-start.3 = (bf16[128,1536]{1,0:T(8,128)(2,1)S(1)}, bf16[128,1536]{1,0:T(8,128)(2,1)S(1)}, u32[]{:S(2)}, u32[]{:S(2)}) collective-permute-start(bf16[128,1536]{1,0:T(8,128)(2,1)S(1)} %get-tuple-element.102.refs_13_), channel_id=1, source_target_pairs={{0,8},{4,12},{8,0},{12,4},{16,24},{20,28},{24,16},{28,20},{1,9},{5... | collective-permute-start | bytes 1179656 | tf_op jit(solution)/shard_map/ppermute | solution.py:526
  5.7 1.5 %collective-permute-start.4 = (bf16[128,1536]{1,0:T(8,128)(2,1)S(1)}, bf16[128,1536]{1,0:T(8,128)(2,1)S(1)}, u32[]{:S(2)}, u32[]{:S(2)}) collective-permute-start(bf16[128,1536]{1,0:T(8,128)(2,1)S(1)} %get-tuple-element.102.refs_13_), channel_id=1, source_target_pairs={{0,16},{4,20},{8,24},{12,28},{16,0},{20,4},{24,8},{28,12},{1,17},{... | collective-permute-start | bytes 1179656 | tf_op jit(solution)/shard_map/ppermute | solution.py:526
  7.2 1.1 constant_dynamic-slice_fusion.15
  8.3 1.6 %collective-permute-start = (bf16[128,1024]{1,0:T(8,128)(2,1)S(1)}, bf16[128,1024]{1,0:T(8,128)(2,1)S(1)}, u32[]{:S(2)}, u32[]{:S(2)}) collective-permute-start(bf16[128,1024]{1,0:T(8,128)(2,1)S(1)} %pad_maximum_fusion.2.refs_5_.x), channel_id=1, source_target_pairs={{0,1},{1,0},{2,3},{3,2},{4,5},{5,4},{6,7},{7,6},{8,9},{9,8},{10,11... | collective-permute-start | bytes 786440 | tf_op jit(solution)/shard_map/ppermute | solution.py:529
  10.0 2.6 %collective-permute-start.1 = (bf16[128,1024]{1,0:T(8,128)(2,1)S(1)}, bf16[128,1024]{1,0:T(8,128)(2,1)}, u32[]{:S(2)}, u32[]{:S(2)}) collective-permute-start(bf16[128,1024]{1,0:T(8,128)(2,1)S(1)} %pad_maximum_fusion.2.refs_5_.x), channel_id=1, source_target_pairs={{0,2},{1,3},{2,0},{3,1},{4,6},{5,7},{6,4},{7,5},{8,10},{9,11},{10,... | collective-permute-start | bytes 786440 | tf_op jit(solution)/shard_map/ppermute | solution.py:529
  12.8 2.0 %collective-permute-done.3.refs_15_ = bf16[128,1536]{1,0:T(8,128)(2,1)S(1)} collective-permute-done((bf16[128,1536]{1,0:T(8,128)(2,1)S(1)}, bf16[128,1536]{1,0:T(8,128)(2,1)S(1)}, u32[]{:S(2)}, u32[]{:S(2)}) %collective-permute-start.3) | collective-permute-done | bytes 393248 | tf_op jit(solution)/shard_map/ppermute | solution.py:526
  14.8 3.9 %collective-permute-start.2 = (bf16[128,1024]{1,0:T(8,128)(2,1)S(1)}, bf16[128,1024]{1,0:T(8,128)(2,1)}, u32[]{:S(2)}, u32[]{:S(2)}) collective-permute-start(bf16[128,1024]{1,0:T(8,128)(2,1)S(1)} %pad_maximum_fusion.2.refs_5_.x), channel_id=1, source_target_pairs={{0,3},{1,2},{2,1},{3,0},{4,7},{5,6},{6,5},{7,4},{8,11},{9,10},{10,... | collective-permute-start | bytes 786440 | tf_op jit(solution)/shard_map/ppermute | solution.py:529
  18.7 1.6 %collective-permute-start.6 = (bf16[128,1536]{1,0:T(8,128)(2,1)}, bf16[128,1536]{1,0:T(8,128)(2,1)}, u32[]{:S(2)}, u32[]{:S(2)}) collective-permute-start(bf16[128,1536]{1,0:T(8,128)(2,1)} %collective-permute-done.5.refs_14_), channel_id=1, source_target_pairs={{0,8},{4,12},{8,0},{12,4},{16,24},{20,28},{24,16},{28,20},{1,9},{5... | collective-permute-start | bytes 1179656 | tf_op jit(solution)/shard_map/ppermute | solution.py:526
  20.2 1.5 %collective-permute-start.7 = (bf16[128,1536]{1,0:T(8,128)(2,1)}, bf16[128,1536]{1,0:T(8,128)(2,1)}, u32[]{:S(2)}, u32[]{:S(2)}) collective-permute-start(bf16[128,1536]{1,0:T(8,128)(2,1)} %collective-permute-done.5.refs_14_), channel_id=1, source_target_pairs={{0,16},{4,20},{8,24},{12,28},{16,0},{20,4},{24,8},{28,12},{1,17},{... | collective-permute-start | bytes 1179656 | tf_op jit(solution)/shard_map/ppermute | solution.py:526
  22.3 1.9 %multiply_cosine_fusion = (f32[1024,128]{1,0:T(8,128)S(1)}, f32[1024,128]{1,0:T(8,128)S(1)}) fusion(f32[128]{0:T(128)S(1)} %get-tuple-element.226, f32[1024]{0:T(1024)S(1)} %get-tuple-element.217, f32[128]{0:T(128)S(1)} %get-tuple-element.225), kind=kLoop, calls=%fused_computation.3 | loop fusion | flops 262144 | bytes 1053696 | tf_op jit(solution)/shard_map/cos | solution.py:574
  24.8 5.8 %collective-permute-done.1.refs_7_ = bf16[128,1024]{1,0:T(8,128)(2,1)} collective-permute-done((bf16[128,1024]{1,0:T(8,128)(2,1)S(1)}, bf16[128,1024]{1,0:T(8,128)(2,1)}, u32[]{:S(2)}, u32[]{:S(2)}) %collective-permute-start.1) | collective-permute-done | bytes 262176 | tf_op jit(solution)/shard_map/ppermute | solution.py:529
  30.6 1.1 collective-permute-done.7.refs_18_
  32.7 0.8 dynamic_slice.82
  33.5 1.5 %collective-permute-start.14 = (bf16[128,1536]{1,0:T(8,128)(2,1)S(1)}, bf16[128,1536]{1,0:T(8,128)(2,1)}, u32[]{:S(2)}, u32[]{:S(2)}) collective-permute-start(bf16[128,1536]{1,0:T(8,128)(2,1)S(1)} %collective-permute-done.3.refs_15_), channel_id=1, source_target_pairs={{0,16},{4,20},{8,24},{12,28},{16,0},{20,4},{24,8},{28,12},{1,17},{... | collective-permute-start | bytes 1179656 | tf_op jit(solution)/shard_map/ppermute | solution.py:526
  35.0 1.1 collective-permute-start.15
  36.1 0.6 fusion.12
  36.7 2.4 %collective-permute-start.16 = (bf16[128,1024]{1,0:T(8,128)(2,1)S(1)}, bf16[128,1024]{1,0:T(8,128)(2,1)}, u32[]{:S(2)}, u32[]{:S(2)}) collective-permute-start(bf16[128,1024]{1,0:T(8,128)(2,1)S(1)} %maximum_select_fusion.refs_0_.cot), channel_id=1, source_target_pairs={{0,1},{1,0},{2,3},{3,2},{4,5},{5,4},{6,7},{7,6},{8,9},{9,8},{10,11... | collective-permute-start | bytes 786440 | tf_op jit(solution)/shard_map/ppermute | solution.py:529
  39.1 1.1 collective-permute-start.17
  40.2 1.4 %collective-permute-start.18 = (bf16[128,1024]{1,0:T(8,128)(2,1)S(1)}, bf16[128,1024]{1,0:T(8,128)(2,1)}, u32[]{:S(2)}, u32[]{:S(2)}) collective-permute-start(bf16[128,1024]{1,0:T(8,128)(2,1)S(1)} %maximum_select_fusion.refs_0_.cot), channel_id=1, source_target_pairs={{0,3},{1,2},{2,1},{3,0},{4,7},{5,6},{6,5},{7,4},{8,11},{9,10},{10,... | collective-permute-start | bytes 786440 | tf_op jit(solution)/shard_map/ppermute | solution.py:529
  41.7 1.3 pad_maximum_fusion.3
  43.0 0.8 concatenate.29
  43.8 0.8 dynamic_slice.83
  44.6 0.7 constant_dynamic-slice_fusion.11
  45.3 0.8 collective-permute-done.15.refs_20_
  46.1 11.9 %forward.1 = (bf16[512,1024]{1,0:T(8,128)(2,1)S(1)}, bf16[512,1024]{1,0:T(8,128)(2,1)S(1)}, bf16[1024,1024]{1,0:T(8,128)(2,1)S(1)}, bf16[1024,1536]{1,0:T(8,128)...) custom-call(s32[4]{0:T(128)S(1)} %pad_add_fusion.1.place.refs_0_, ...), custom_call_target="tpu_custom_call" | custom-call | flops 11500000 | tf_op jit(solution)/shard_map/forward/pallas_call | solution.py:43
  58.0 2.6 %collective-permute-done.17.refs_2_ = bf16[128,1024]{1,0:T(8,128)(2,1)} collective-permute-done((bf16[128,1024]{1,0:T(8,128)(2,1)S(1)}, bf16[128,1024]{1,0:T(8,128)(2,1)}, u32[]{:S(2)}, u32[]{:S(2)}) %collective-permute-start.17) | collective-permute-done | bytes 262176 | tf_op jit(solution)/shard_map/ppermute | solution.py:529
  60.6 2.7 %collective-permute-done.19.other = bf16[512,1024]{1,0:T(8,128)(2,1)S(1)} collective-permute-done((bf16[512,1024]{1,0:T(8,128)(2,1)S(1)}, bf16[512,1024]{1,0:T(8,128)(2,1)S(1)}, u32[]{:S(2)}, u32[]{:S(2)}) %collective-permute-start.19) | collective-permute-done | bytes 1048608 | tf_op jit(solution)/shard_map/ppermute | solution.py:523
  63.9 0.8 add_sibling.1
  64.7 4.5 %collective-permute-start.24 = (bf16[128,1024]{1,0:T(8,128)(2,1)S(1)}, bf16[128,1024]{1,0:T(8,128)(2,1)S(1)}, u32[]{:S(2)}, u32[]{:S(2)}) collective-permute-start(bf16[128,1024]{1,0:T(8,128)(2,1)S(1)} %get-tuple-element.134), channel_id=1, source_target_pairs={{0,1},{1,0},{2,3},{3,2},{4,5},{5,4},{6,7},{7,6},{8,9},{9,8},{10,11... | collective-permute-start | bytes 786440 | tf_op jit(solution)/shard_map/ppermute | solution.py:529
  69.3 0.7 collective-permute-start.26
  70.0 3.7 %second_grads.1 = (bf16[1024,1024]{1,0:T(8,128)(2,1)S(1)}, bf16[128,640]{1,0:T(8,128)(2,1)S(1)}, bf16[128,640]{1,0:T(8,128)(2,1)S(1)}, bf16[256,640]{1,0:T(8,128...) custom-call(s32[4]{0:T(128)S(1)} %pad_add_fusion.1.place.refs_0_, ...), custom_call_target="tpu_custom_call" | custom-call | flops 11500000 | tf_op jit(solution)/shard_map/second_grads/pallas_call | solution.py:43
  73.7 2.6 %collective-permute-done.24.passed = bf16[128,1024]{1,0:T(8,128)(2,1)S(1)} collective-permute-done((bf16[128,1024]{1,0:T(8,128)(2,1)S(1)}, bf16[128,1024]{1,0:T(8,128)(2,1)S(1)}, u32[]{:S(2)}, u32[]{:S(2)}) %collective-permute-start.24) | collective-permute-done | bytes 262176 | tf_op jit(solution)/shard_map/ppermute | solution.py:529
  76.4 0.6 branch_relay.1
  77.0 3.1 %collective-permute-start.25 = (bf16[128,1024]{1,0:T(8,128)(2,1)S(1)}, bf16[128,1024]{1,0:T(8,128)(2,1)S(1)}, u32[]{:S(2)}, u32[]{:S(2)}) collective-permute-start(bf16[128,1024]{1,0:T(8,128)(2,1)S(1)} %branch_relay.1), channel_id=1, source_target_pairs={{0,2},{1,3},{2,0},{3,1},{4,6},{5,7},{6,4},{7,5},{8,10},{9,11},{10,... | collective-permute-start | bytes 786440 | tf_op jit(solution)/shard_map/ppermute | solution.py:529
  80.0 1.5 %collective-permute-start.27 = (bf16[256,640]{1,0:T(8,128)(2,1)S(1)}, bf16[256,640]{1,0:T(8,128)(2,1)S(1)}, u32[]{:S(2)}, u32[]{:S(2)}) collective-permute-start(bf16[256,640]{1,0:T(8,128)(2,1)S(1)} %get-tuple-element.135), channel_id=1, source_target_pairs={{0,16},{4,20},{8,24},{12,28},{16,0},{20,4},{24,8},{28,12},{1,17},{... | collective-permute-start | bytes 983048 | tf_op jit(solution)/shard_map/ppermute | solution.py:526
  81.6 1.5 %collective-permute-start.28 = (bf16[256,640]{1,0:T(8,128)(2,1)S(1)}, bf16[256,640]{1,0:T(8,128)(2,1)S(1)}, u32[]{:S(2)}, u32[]{:S(2)}) collective-permute-start(bf16[256,640]{1,0:T(8,128)(2,1)S(1)} %get-tuple-element.136), channel_id=1, source_target_pairs={{0,8},{4,12},{8,0},{12,4},{16,24},{20,28},{24,16},{28,20},{1,9},{5... | collective-permute-start | bytes 983048 | tf_op jit(solution)/shard_map/ppermute | solution.py:526
  83.0 9.7 %backward.1 = (bf16[512,1024]{1,0:T(8,128)(2,1)S(1)}, bf16[528,1024]{1,0:T(8,128)(2,1)S(1)}, bf16[1024,896]{1,0:T(8,128)(2,1)S(1)}, f32[8,1024]{1,0:T(8,128)S(1)}) custom-call(s32[4]{0:T(128)S(1)} %pad_add_fusion.1.place.refs_0_, f32[1024,384]{1,0:T(8,128)S(1)} %pad_maximum_fusion.refs_1_, f32[4,1024]{1,0:T(4,128)S(1)} %pad_maximum_fusion.4.refs_2_, ...), custom_call_target="tpu_custom_call" | custom-call | flops 16099999744 | tf_op jit(solution)/shard_map/backward/pallas_call | solution.py:43
  92.7 3.2 %first_grads.1 = (bf16[128,896]{1,0:T(8,128)(2,1)S(1)}, bf16[128,896]{1,0:T(8,128)(2,1)S(1)}, bf16[256,896]{1,0:T(8,128)(2,1)S(1)}, bf16[256,896]{1,0:T(8,128)(2...) custom-call(s32[4]{0:T(128)S(1)} %pad_add_fusion.1.place.refs_0_, ...), custom_call_target="tpu_custom_call" | custom-call | flops 11500000 | tf_op jit(solution)/shard_map/first_grads/pallas_call | solution.py:43
  96.1 0.6 collective-permute-start.29
  97.2 2.4 %collective-permute-start.31 = (f32[8,1024]{1,0:T(8,128)S(1)}, f32[8,1024]{1,0:T(8,128)S(1)}, u32[]{:S(2)}, u32[]{:S(2)}) collective-permute-start(f32[8,1024]{1,0:T(8,128)S(1)} %get-tuple-element.157.refs_0_), channel_id=1, source_target_pairs={{0,24},{4,28},{8,16},{12,20},{16,8},{20,12},{24,0},{28,4},{1,25},{... | collective-permute-start | bytes 98312 | tf_op jit(solution)/shard_map/ppermute | solution.py:526
  100.6 1.4 %collective-permute-done.31.refs_3_ = f32[8,1024]{1,0:T(8,128)S(1)} collective-permute-done((f32[8,1024]{1,0:T(8,128)S(1)}, f32[8,1024]{1,0:T(8,128)S(1)}, u32[]{:S(2)}, u32[]{:S(2)}) %collective-permute-start.31) | collective-permute-done | bytes 32800 | tf_op jit(solution)/shard_map/ppermute | solution.py:526
  102.0 1.5 %collective-permute-start.32 = (bf16[256,896]{1,0:T(8,128)(2,1)S(1)}, bf16[256,896]{1,0:T(8,128)(2,1)S(1)}, u32[]{:S(2)}, u32[]{:S(2)}) collective-permute-start(bf16[256,896]{1,0:T(8,128)(2,1)S(1)} %get-tuple-element.158), channel_id=1, source_target_pairs={{0,8},{4,12},{8,0},{12,4},{16,24},{20,28},{24,16},{28,20},{1,9},{5... | collective-permute-start | bytes 1376264 | tf_op jit(solution)/shard_map/ppermute | solution.py:526
  103.5 1.5 %collective-permute-start.36 = (bf16[256,896]{1,0:T(8,128)(2,1)S(1)}, bf16[256,896]{1,0:T(8,128)(2,1)S(1)}, u32[]{:S(2)}, u32[]{:S(2)}) collective-permute-start(bf16[256,896]{1,0:T(8,128)(2,1)S(1)} %get-tuple-element.172), channel_id=1, source_target_pairs={{0,16},{4,20},{8,24},{12,28},{16,0},{20,4},{24,8},{28,12},{1,17},{... | collective-permute-start | bytes 1376264 | tf_op jit(solution)/shard_map/ppermute | solution.py:526
  105.0 0.8 split_back.1
  105.8 0.7 collective-permute-start.34
  106.5 1.9 %collective-permute-start.35 = (bf16[128,1024]{1,0:T(8,128)(2,1)S(1)}, bf16[128,1024]{1,0:T(8,128)(2,1)S(1)}, u32[]{:S(2)}, u32[]{:S(2)}) collective-permute-start(bf16[128,1024]{1,0:T(8,128)(2,1)S(1)} %get-tuple-element.166), channel_id=1, source_target_pairs={{0,1},{1,0},{2,3},{3,2},{4,5},{5,4},{6,7},{7,6},{8,9},{9,8},{10,11... | collective-permute-start | bytes 786440 | tf_op jit(solution)/shard_map/ppermute | solution.py:529
  108.6 4.6 %collective-permute-done.32.refs_3_.first_x = bf16[256,896]{1,0:T(8,128)(2,1)S(1)} collective-permute-done((bf16[256,896]{1,0:T(8,128)(2,1)S(1)}, bf16[256,896]{1,0:T(8,128)(2,1)S(1)}, u32[]{:S(2)}, u32[]{:S(2)}) %collective-permute-start.32) | collective-permute-done | bytes 458784 | tf_op jit(solution)/shard_map/ppermute | solution.py:526
  113.2 1.2 collective-permute-done.36.refs_2_.refs_1_
  114.4 0.8 second_round.1
  115.2 1.6 %collective-permute-start.38 = (bf16[128,1536]{1,0:T(8,128)(2,1)S(1)}, bf16[128,1536]{1,0:T(8,128)(2,1)S(1)}, u32[]{:S(2)}, u32[]{:S(2)}) collective-permute-start(bf16[128,1536]{1,0:T(8,128)(2,1)S(1)} %get-tuple-element.177), channel_id=1, source_target_pairs={{0,16},{4,20},{8,24},{12,28},{16,0},{20,4},{24,8},{28,12},{1,17},{... | collective-permute-start | bytes 1179656 | tf_op jit(solution)/shard_map/ppermute | solution.py:526
  116.9 2.0 %collective-permute-start.40 = (bf16[144,1024]{1,0:T(8,128)(2,1)S(1)}, bf16[144,1024]{1,0:T(8,128)(2,1)S(1)}, u32[]{:S(2)}, u32[]{:S(2)}) collective-permute-start(bf16[144,1024]{1,0:T(8,128)(2,1)S(1)} %get-tuple-element.181), channel_id=1, source_target_pairs={{0,2},{1,3},{2,0},{3,1},{4,6},{5,7},{6,4},{7,5},{8,10},{9,11},{10,... | collective-permute-start | bytes 884744 | tf_op jit(solution)/shard_map/ppermute | solution.py:529
  118.9 0.8 fusion.3
  119.7 2.3 %collective-permute-start.41 = (f32[8,1024]{1,0:T(8,128)S(1)}, f32[8,1024]{1,0:T(8,128)S(1)}, u32[]{:S(2)}, u32[]{:S(2)}) collective-permute-start(f32[8,1024]{1,0:T(8,128)S(1)} %get-tuple-element.182.sums), channel_id=1, source_target_pairs={{0,3},{1,2},{2,1},{3,0},{4,7},{5,6},{6,5},{7,4},{8,11},{9,10},{10,... | collective-permute-start | bytes 98312 | tf_op jit(solution)/shard_map/ppermute | solution.py:529
  122.1 0.6 slice_reduce_fusion
  122.7 0.6 slice.52
  123.9 0.7 other_sums.1
  124.6 5.2 %collective-permute-done.41.third = f32[8,1024]{1,0:T(8,128)S(1)} collective-permute-done((f32[8,1024]{1,0:T(8,128)S(1)}, f32[8,1024]{1,0:T(8,128)S(1)}, u32[]{:S(2)}, u32[]{:S(2)}) %collective-permute-start.41) | collective-permute-done | bytes 32800 | tf_op jit(solution)/shard_map/ppermute | solution.py:529
  129.8 1.6 %collective-permute-done.40.second = bf16[144,1024]{1,0:T(8,128)(2,1)S(1)} collective-permute-done((bf16[144,1024]{1,0:T(8,128)(2,1)S(1)}, bf16[144,1024]{1,0:T(8,128)(2,1)S(1)}, u32[]{:S(2)}, u32[]{:S(2)}) %collective-permute-start.40) | collective-permute-done | bytes 294944 | tf_op jit(solution)/shard_map/ppermute | solution.py:529
  131.5 1.0 finish_rows.1
  132.5 0.6 fusion.11
  133.2 0.8 pad_maximum_fusion.1
  134.0 1.8 %join_halves.1 = (f32[128,768]{1,0:T(8,128)}, f32[128,1024]{1,0:T(8,128)}, f32[128,256]{1,0:T(8,128)}, f32[128,1024]{1,0:T(8,128)}) custom-call(s32[4]{0:T(128)S(1)} %pad_add_fusion.1.place.refs_0_, bf16[128,896]{1,0:T(8,128)(2,1)S(1)} %get-tuple-element.149.refs_0_, bf16[256,896]{1,0:T(8,128)(2,1)S(1)} %collective-permute-done.36.refs_2_.refs_1_, ...), custom_call_target="tpu_custom_call" | custom-call | flops 11500000 | tf_op jit(solution)/shard_map/join_halves/pallas_call | solution.py:43
  135.8 0.6 copy.31
  (86 shorter events, 5.8 us)
Async XLA Ops:
  0.6 11.9 %copy-start.2 = (s32[512]{0:T(512)S(1)}, s32[512]{0:T(512)}, u32[]{:S(2)}) copy-start(s32[512]{0:T(512)} %param.16) | copy-start | bytes 6148
  2.7 12.1 %collective-permute-start.3 = (bf16[128,1536]{1,0:T(8,128)(2,1)S(1)}, bf16[128,1536]{1,0:T(8,128)(2,1)S(1)}, u32[]{:S(2)}, u32[]{:S(2)}) collective-permute-start(bf16[128,1536]{1,0:T(8,128)(2,1)S(1)} %get-tuple-element.102.refs_13_), channel_id=1, source_target_pairs={{0,8},{4,12},{8,0},{12,4},{16,24},{20,28},{24,16},{28,20},{1,9},{5... | collective-permute-start | bytes 1179656 | tf_op jit(solution)/shard_map/ppermute | solution.py:526
  5.7 13.0 %collective-permute-start.4 = (bf16[128,1536]{1,0:T(8,128)(2,1)S(1)}, bf16[128,1536]{1,0:T(8,128)(2,1)S(1)}, u32[]{:S(2)}, u32[]{:S(2)}) collective-permute-start(bf16[128,1536]{1,0:T(8,128)(2,1)S(1)} %get-tuple-element.102.refs_13_), channel_id=1, source_target_pairs={{0,16},{4,20},{8,24},{12,28},{16,0},{20,4},{24,8},{28,12},{1,17},{... | collective-permute-start | bytes 1179656 | tf_op jit(solution)/shard_map/ppermute | solution.py:526
  8.3 16.4 %collective-permute-start = (bf16[128,1024]{1,0:T(8,128)(2,1)S(1)}, bf16[128,1024]{1,0:T(8,128)(2,1)S(1)}, u32[]{:S(2)}, u32[]{:S(2)}) collective-permute-start(bf16[128,1024]{1,0:T(8,128)(2,1)S(1)} %pad_maximum_fusion.2.refs_5_.x), channel_id=1, source_target_pairs={{0,1},{1,0},{2,3},{3,2},{4,5},{5,4},{6,7},{7,6},{8,9},{9,8},{10,11... | collective-permute-start | bytes 786440 | tf_op jit(solution)/shard_map/ppermute | solution.py:529
  10.0 20.7 %collective-permute-start.1 = (bf16[128,1024]{1,0:T(8,128)(2,1)S(1)}, bf16[128,1024]{1,0:T(8,128)(2,1)}, u32[]{:S(2)}, u32[]{:S(2)}) collective-permute-start(bf16[128,1024]{1,0:T(8,128)(2,1)S(1)} %pad_maximum_fusion.2.refs_5_.x), channel_id=1, source_target_pairs={{0,2},{1,3},{2,0},{3,1},{4,6},{5,7},{6,4},{7,5},{8,10},{9,11},{10,... | collective-permute-start | bytes 786440 | tf_op jit(solution)/shard_map/ppermute | solution.py:529
  12.5 6.1 %collective-permute-start.5 = (bf16[128,1536]{1,0:T(8,128)(2,1)S(1)}, bf16[128,1536]{1,0:T(8,128)(2,1)}, u32[]{:S(2)}, u32[]{:S(2)}) collective-permute-start(bf16[128,1536]{1,0:T(8,128)(2,1)S(1)} %get-tuple-element.104), channel_id=1, source_target_pairs={{0,4},{4,0},{8,12},{12,8},{16,20},{20,16},{24,28},{28,24},{1,5},{5... | collective-permute-start | bytes 1179656 | tf_op jit(solution)/shard_map/ppermute | solution.py:523
  14.8 15.9 %collective-permute-start.2 = (bf16[128,1024]{1,0:T(8,128)(2,1)S(1)}, bf16[128,1024]{1,0:T(8,128)(2,1)}, u32[]{:S(2)}, u32[]{:S(2)}) collective-permute-start(bf16[128,1024]{1,0:T(8,128)(2,1)S(1)} %pad_maximum_fusion.2.refs_5_.x), channel_id=1, source_target_pairs={{0,3},{1,2},{2,1},{3,0},{4,7},{5,6},{6,5},{7,4},{8,11},{9,10},{10,... | collective-permute-start | bytes 786440 | tf_op jit(solution)/shard_map/ppermute | solution.py:529
  18.6 1.6 %collective-permute-start.8 = (s32[512]{0:T(512)S(1)}, s32[512]{0:T(512)S(1)}, u32[]{:S(2)}, u32[]{:S(2)}) collective-permute-start(s32[512]{0:T(512)S(1)} %copy-done.2), channel_id=1, source_target_pairs={{0,4},{4,0},{8,12},{12,8},{16,20},{20,16},{24,28},{28,24},{1,5},{5... | collective-permute-start | bytes 6152 | tf_op jit(solution)/shard_map/ppermute | solution.py:523
  18.7 12.0 %collective-permute-start.6 = (bf16[128,1536]{1,0:T(8,128)(2,1)}, bf16[128,1536]{1,0:T(8,128)(2,1)}, u32[]{:S(2)}, u32[]{:S(2)}) collective-permute-start(bf16[128,1536]{1,0:T(8,128)(2,1)} %collective-permute-done.5.refs_14_), channel_id=1, source_target_pairs={{0,8},{4,12},{8,0},{12,4},{16,24},{20,28},{24,16},{28,20},{1,9},{5... | collective-permute-start | bytes 1179656 | tf_op jit(solution)/shard_map/ppermute | solution.py:526
  20.2 11.5 %collective-permute-start.7 = (bf16[128,1536]{1,0:T(8,128)(2,1)}, bf16[128,1536]{1,0:T(8,128)(2,1)}, u32[]{:S(2)}, u32[]{:S(2)}) collective-permute-start(bf16[128,1536]{1,0:T(8,128)(2,1)} %collective-permute-done.5.refs_14_), channel_id=1, source_target_pairs={{0,16},{4,20},{8,24},{12,28},{16,0},{20,4},{24,8},{28,12},{1,17},{... | collective-permute-start | bytes 1179656 | tf_op jit(solution)/shard_map/ppermute | solution.py:526
  24.2 17.4 %copy-start.5 = (f32[1024]{0:T(1024)S(1)}, f32[1024]{0:T(1024)}, u32[]{:S(2)}) copy-start(f32[1024]{0:T(1024)} %param.20) | copy-start | bytes 12292
  24.2 17.4 %copy-start.6 = (f32[1024]{0:T(1024)S(1)}, f32[1024]{0:T(1024)}, u32[]{:S(2)}) copy-start(f32[1024]{0:T(1024)} %param.19) | copy-start | bytes 12292
  24.3 17.4 %copy-start.7 = (f32[1024]{0:T(1024)S(1)}, f32[1024]{0:T(1024)}, u32[]{:S(2)}) copy-start(f32[1024]{0:T(1024)} %param.18) | copy-start | bytes 12292
  24.7 8.8 %collective-permute-start.10 = (bf16[128,1024]{1,0:T(8,128)(2,1)S(1)}, bf16[128,1024]{1,0:T(8,128)(2,1)}, u32[]{:S(2)}, u32[]{:S(2)}) collective-permute-start(bf16[128,1024]{1,0:T(8,128)(2,1)S(1)} %pad_maximum_fusion.2.refs_5_.x), channel_id=1, source_target_pairs={{0,4},{4,0},{8,12},{12,8},{16,20},{20,16},{24,28},{28,24},{1,5},{5... | collective-permute-start | bytes 786440 | tf_op jit(solution)/shard_map/ppermute | solution.py:523
  31.7 3.3 %collective-permute-start.9 = (bf16[128,1024]{1,0:T(8,128)(2,1)S(1)}, bf16[128,1024]{1,0:T(8,128)(2,1)}, u32[]{:S(2)}, u32[]{:S(2)}) collective-permute-start(bf16[128,1024]{1,0:T(8,128)(2,1)S(1)} %maximum_select_fusion.refs_0_.cot), channel_id=1, source_target_pairs={{0,4},{4,0},{8,12},{12,8},{16,20},{20,16},{24,28},{28,24},{1,5},{5... | collective-permute-start | bytes 786440 | tf_op jit(solution)/shard_map/ppermute | solution.py:523
  31.7 5.0 %collective-permute-start.11 = (bf16[128,1024]{1,0:T(8,128)(2,1)S(1)}, bf16[128,1024]{1,0:T(8,128)(2,1)}, u32[]{:S(2)}, u32[]{:S(2)}) collective-permute-start(bf16[128,1024]{1,0:T(8,128)(2,1)S(1)} %collective-permute-done.refs_6_), channel_id=1, source_target_pairs={{0,4},{4,0},{8,12},{12,8},{16,20},{20,16},{24,28},{28,24},{1,5},{5... | collective-permute-start | bytes 786440 | tf_op jit(solution)/shard_map/ppermute | solution.py:523
  32.2 6.9 %collective-permute-start.12 = (bf16[128,1024]{1,0:T(8,128)(2,1)}, bf16[128,1024]{1,0:T(8,128)(2,1)}, u32[]{:S(2)}, u32[]{:S(2)}) collective-permute-start(bf16[128,1024]{1,0:T(8,128)(2,1)} %collective-permute-done.1.refs_7_), channel_id=1, source_target_pairs={{0,4},{4,0},{8,12},{12,8},{16,20},{20,16},{24,28},{28,24},{1,5},{5... | collective-permute-start | bytes 786440 | tf_op jit(solution)/shard_map/ppermute | solution.py:523
  32.2 8.0 %collective-permute-start.13 = (bf16[128,1024]{1,0:T(8,128)(2,1)}, bf16[128,1024]{1,0:T(8,128)(2,1)}, u32[]{:S(2)}, u32[]{:S(2)}) collective-permute-start(bf16[128,1024]{1,0:T(8,128)(2,1)} %collective-permute-done.2.refs_8_), channel_id=1, source_target_pairs={{0,4},{4,0},{8,12},{12,8},{16,20},{20,16},{24,28},{28,24},{1,5},{5... | collective-permute-start | bytes 786440 | tf_op jit(solution)/shard_map/ppermute | solution.py:523
  33.5 11.8 %collective-permute-start.14 = (bf16[128,1536]{1,0:T(8,128)(2,1)S(1)}, bf16[128,1536]{1,0:T(8,128)(2,1)}, u32[]{:S(2)}, u32[]{:S(2)}) collective-permute-start(bf16[128,1536]{1,0:T(8,128)(2,1)S(1)} %collective-permute-done.3.refs_15_), channel_id=1, source_target_pairs={{0,16},{4,20},{8,24},{12,28},{16,0},{20,4},{24,8},{28,12},{1,17},{... | collective-permute-start | bytes 1179656 | tf_op jit(solution)/shard_map/ppermute | solution.py:526
  35.0 11.1 %collective-permute-start.15 = (bf16[128,1536]{1,0:T(8,128)(2,1)}, bf16[128,1536]{1,0:T(8,128)(2,1)}, u32[]{:S(2)}, u32[]{:S(2)}) collective-permute-start(bf16[128,1536]{1,0:T(8,128)(2,1)} %collective-permute-done.7.refs_18_), channel_id=1, source_target_pairs={{0,8},{4,12},{8,0},{12,4},{16,24},{20,28},{24,16},{28,20},{1,9},{5... | collective-permute-start | bytes 1179656 | tf_op jit(solution)/shard_map/ppermute | solution.py:526
  36.7 21.3 %collective-permute-start.16 = (bf16[128,1024]{1,0:T(8,128)(2,1)S(1)}, bf16[128,1024]{1,0:T(8,128)(2,1)}, u32[]{:S(2)}, u32[]{:S(2)}) collective-permute-start(bf16[128,1024]{1,0:T(8,128)(2,1)S(1)} %maximum_select_fusion.refs_0_.cot), channel_id=1, source_target_pairs={{0,1},{1,0},{2,3},{3,2},{4,5},{5,4},{6,7},{7,6},{8,9},{9,8},{10,11... | collective-permute-start | bytes 786440 | tf_op jit(solution)/shard_map/ppermute | solution.py:529
  39.1 21.5 %collective-permute-start.17 = (bf16[128,1024]{1,0:T(8,128)(2,1)S(1)}, bf16[128,1024]{1,0:T(8,128)(2,1)}, u32[]{:S(2)}, u32[]{:S(2)}) collective-permute-start(bf16[128,1024]{1,0:T(8,128)(2,1)S(1)} %maximum_select_fusion.refs_0_.cot), channel_id=1, source_target_pairs={{0,2},{1,3},{2,0},{3,1},{4,6},{5,7},{6,4},{7,5},{8,10},{9,11},{10,... | collective-permute-start | bytes 786440 | tf_op jit(solution)/shard_map/ppermute | solution.py:529
  40.2 20.4 %collective-permute-start.18 = (bf16[128,1024]{1,0:T(8,128)(2,1)S(1)}, bf16[128,1024]{1,0:T(8,128)(2,1)}, u32[]{:S(2)}, u32[]{:S(2)}) collective-permute-start(bf16[128,1024]{1,0:T(8,128)(2,1)S(1)} %maximum_select_fusion.refs_0_.cot), channel_id=1, source_target_pairs={{0,3},{1,2},{2,1},{3,0},{4,7},{5,6},{6,5},{7,4},{8,11},{9,10},{10,... | collective-permute-start | bytes 786440 | tf_op jit(solution)/shard_map/ppermute | solution.py:529
  60.6 2.7 %collective-permute-start.19 = (bf16[512,1024]{1,0:T(8,128)(2,1)S(1)}, bf16[512,1024]{1,0:T(8,128)(2,1)S(1)}, u32[]{:S(2)}, u32[]{:S(2)}) collective-permute-start(bf16[512,1024]{1,0:T(8,128)(2,1)S(1)} %get-tuple-element.120), channel_id=1, source_target_pairs={{0,4},{4,0},{8,12},{12,8},{16,20},{20,16},{24,28},{28,24},{1,5},{5... | collective-permute-start | bytes 3145736 | tf_op jit(solution)/shard_map/ppermute | solution.py:523
  63.3 6.0 %collective-permute-start.21 = (bf16[128,1024]{1,0:T(8,128)(2,1)}, bf16[128,1024]{1,0:T(8,128)(2,1)S(1)}, u32[]{:S(2)}, u32[]{:S(2)}) collective-permute-start(bf16[128,1024]{1,0:T(8,128)(2,1)} %collective-permute-done.16.refs_1_), channel_id=1, source_target_pairs={{0,4},{4,0},{8,12},{12,8},{16,20},{20,16},{24,28},{28,24},{1,5},{5... | collective-permute-start | bytes 786440 | tf_op jit(solution)/shard_map/ppermute | solution.py:523
  63.4 6.5 %collective-permute-start.22 = (bf16[128,1024]{1,0:T(8,128)(2,1)}, bf16[128,1024]{1,0:T(8,128)(2,1)S(1)}, u32[]{:S(2)}, u32[]{:S(2)}) collective-permute-start(bf16[128,1024]{1,0:T(8,128)(2,1)} %collective-permute-done.17.refs_2_), channel_id=1, source_target_pairs={{0,4},{4,0},{8,12},{12,8},{16,20},{20,16},{24,28},{28,24},{1,5},{5... | collective-permute-start | bytes 786440 | tf_op jit(solution)/shard_map/ppermute | solution.py:523
  63.8 6.2 %collective-permute-start.23 = (bf16[128,1024]{1,0:T(8,128)(2,1)}, bf16[128,1024]{1,0:T(8,128)(2,1)S(1)}, u32[]{:S(2)}, u32[]{:S(2)}) collective-permute-start(bf16[128,1024]{1,0:T(8,128)(2,1)} %collective-permute-done.18.refs_3_), channel_id=1, source_target_pairs={{0,4},{4,0},{8,12},{12,8},{16,20},{20,16},{24,28},{28,24},{1,5},{5... | collective-permute-start | bytes 786440 | tf_op jit(solution)/shard_map/ppermute | solution.py:523
  64.7 11.6 %collective-permute-start.24 = (bf16[128,1024]{1,0:T(8,128)(2,1)S(1)}, bf16[128,1024]{1,0:T(8,128)(2,1)S(1)}, u32[]{:S(2)}, u32[]{:S(2)}) collective-permute-start(bf16[128,1024]{1,0:T(8,128)(2,1)S(1)} %get-tuple-element.134), channel_id=1, source_target_pairs={{0,1},{1,0},{2,3},{3,2},{4,5},{5,4},{6,7},{7,6},{8,9},{9,8},{10,11... | collective-permute-start | bytes 786440 | tf_op jit(solution)/shard_map/ppermute | solution.py:529
  69.2 26.7 %collective-permute-start.20 = (bf16[128,1024]{1,0:T(8,128)(2,1)S(1)}, bf16[128,1024]{1,0:T(8,128)(2,1)S(1)}, u32[]{:S(2)}, u32[]{:S(2)}) collective-permute-start(bf16[128,1024]{1,0:T(8,128)(2,1)S(1)} %get-tuple-element.122), channel_id=1, source_target_pairs={{0,1},{1,0},{2,3},{3,2},{4,5},{5,4},{6,7},{7,6},{8,9},{9,8},{10,11... | collective-permute-start | bytes 786440 | tf_op jit(solution)/shard_map/ppermute | solution.py:529
  69.3 26.7 %collective-permute-start.26 = (bf16[128,1024]{1,0:T(8,128)(2,1)S(1)}, bf16[128,1024]{1,0:T(8,128)(2,1)S(1)}, u32[]{:S(2)}, u32[]{:S(2)}) collective-permute-start(bf16[128,1024]{1,0:T(8,128)(2,1)S(1)} %get-tuple-element.134), channel_id=1, source_target_pairs={{0,0},{1,2},{2,1},{3,3},{4,4},{5,6},{6,5},{7,7},{8,8},{9,10},{10,9... | collective-permute-start | bytes 786440 | tf_op jit(solution)/shard_map/ppermute | solution.py:538
  77.0 19.0 %collective-permute-start.25 = (bf16[128,1024]{1,0:T(8,128)(2,1)S(1)}, bf16[128,1024]{1,0:T(8,128)(2,1)S(1)}, u32[]{:S(2)}, u32[]{:S(2)}) collective-permute-start(bf16[128,1024]{1,0:T(8,128)(2,1)S(1)} %branch_relay.1), channel_id=1, source_target_pairs={{0,2},{1,3},{2,0},{3,1},{4,6},{5,7},{6,4},{7,5},{8,10},{9,11},{10,... | collective-permute-start | bytes 786440 | tf_op jit(solution)/shard_map/ppermute | solution.py:529
  80.0 15.9 %collective-permute-start.27 = (bf16[256,640]{1,0:T(8,128)(2,1)S(1)}, bf16[256,640]{1,0:T(8,128)(2,1)S(1)}, u32[]{:S(2)}, u32[]{:S(2)}) collective-permute-start(bf16[256,640]{1,0:T(8,128)(2,1)S(1)} %get-tuple-element.135), channel_id=1, source_target_pairs={{0,16},{4,20},{8,24},{12,28},{16,0},{20,4},{24,8},{28,12},{1,17},{... | collective-permute-start | bytes 983048 | tf_op jit(solution)/shard_map/ppermute | solution.py:526
  81.6 14.4 %collective-permute-start.28 = (bf16[256,640]{1,0:T(8,128)(2,1)S(1)}, bf16[256,640]{1,0:T(8,128)(2,1)S(1)}, u32[]{:S(2)}, u32[]{:S(2)}) collective-permute-start(bf16[256,640]{1,0:T(8,128)(2,1)S(1)} %get-tuple-element.136), channel_id=1, source_target_pairs={{0,8},{4,12},{8,0},{12,4},{16,24},{20,28},{24,16},{28,20},{1,9},{5... | collective-permute-start | bytes 983048 | tf_op jit(solution)/shard_map/ppermute | solution.py:526
  96.0 9.0 %collective-permute-start.33 = (bf16[528,1024]{1,0:T(8,128)(2,1)S(1)}, bf16[528,1024]{1,0:T(8,128)(2,1)S(1)}, u32[]{:S(2)}, u32[]{:S(2)}) collective-permute-start(bf16[528,1024]{1,0:T(8,128)(2,1)S(1)} %get-tuple-element.162), channel_id=1, source_target_pairs={{0,4},{4,0},{8,12},{12,8},{16,20},{20,16},{24,28},{28,24},{1,5},{5... | collective-permute-start | bytes 3244040 | tf_op jit(solution)/shard_map/ppermute | solution.py:523
  96.1 4.0 %collective-permute-start.29 = (f32[8,1024]{1,0:T(8,128)S(1)}, f32[8,1024]{1,0:T(8,128)S(1)}, u32[]{:S(2)}, u32[]{:S(2)}) collective-permute-start(f32[8,1024]{1,0:T(8,128)S(1)} %get-tuple-element.157.refs_0_), channel_id=1, source_target_pairs={{0,8},{4,12},{8,0},{12,4},{16,24},{20,28},{24,16},{28,20},{1,9},{5... | collective-permute-start | bytes 98312 | tf_op jit(solution)/shard_map/ppermute | solution.py:526
  96.7 3.9 %collective-permute-start.30 = (f32[8,1024]{1,0:T(8,128)S(1)}, f32[8,1024]{1,0:T(8,128)S(1)}, u32[]{:S(2)}, u32[]{:S(2)}) collective-permute-start(f32[8,1024]{1,0:T(8,128)S(1)} %get-tuple-element.157.refs_0_), channel_id=1, source_target_pairs={{0,16},{4,20},{8,24},{12,28},{16,0},{20,4},{24,8},{28,12},{1,17},{... | collective-permute-start | bytes 98312 | tf_op jit(solution)/shard_map/ppermute | solution.py:526
  97.2 4.8 %collective-permute-start.31 = (f32[8,1024]{1,0:T(8,128)S(1)}, f32[8,1024]{1,0:T(8,128)S(1)}, u32[]{:S(2)}, u32[]{:S(2)}) collective-permute-start(f32[8,1024]{1,0:T(8,128)S(1)} %get-tuple-element.157.refs_0_), channel_id=1, source_target_pairs={{0,24},{4,28},{8,16},{12,20},{16,8},{20,12},{24,0},{28,4},{1,25},{... | collective-permute-start | bytes 98312 | tf_op jit(solution)/shard_map/ppermute | solution.py:526
  102.0 11.2 %collective-permute-start.32 = (bf16[256,896]{1,0:T(8,128)(2,1)S(1)}, bf16[256,896]{1,0:T(8,128)(2,1)S(1)}, u32[]{:S(2)}, u32[]{:S(2)}) collective-permute-start(bf16[256,896]{1,0:T(8,128)(2,1)S(1)} %get-tuple-element.158), channel_id=1, source_target_pairs={{0,8},{4,12},{8,0},{12,4},{16,24},{20,28},{24,16},{28,20},{1,9},{5... | collective-permute-start | bytes 1376264 | tf_op jit(solution)/shard_map/ppermute | solution.py:526
  103.5 10.9 %collective-permute-start.36 = (bf16[256,896]{1,0:T(8,128)(2,1)S(1)}, bf16[256,896]{1,0:T(8,128)(2,1)S(1)}, u32[]{:S(2)}, u32[]{:S(2)}) collective-permute-start(bf16[256,896]{1,0:T(8,128)(2,1)S(1)} %get-tuple-element.172), channel_id=1, source_target_pairs={{0,16},{4,20},{8,24},{12,28},{16,0},{20,4},{24,8},{28,12},{1,17},{... | collective-permute-start | bytes 1376264 | tf_op jit(solution)/shard_map/ppermute | solution.py:526
  105.8 2.8 %collective-permute-start.34 = (bf16[128,1024]{1,0:T(8,128)(2,1)S(1)}, bf16[128,1024]{1,0:T(8,128)(2,1)S(1)}, u32[]{:S(2)}, u32[]{:S(2)}) collective-permute-start(bf16[128,1024]{1,0:T(8,128)(2,1)S(1)} %get-tuple-element.166), channel_id=1, source_target_pairs={{0,0},{1,2},{2,1},{3,3},{4,4},{5,6},{6,5},{7,7},{8,8},{9,10},{10,9... | collective-permute-start | bytes 786440 | tf_op jit(solution)/shard_map/ppermute | solution.py:538
  106.5 7.9 %collective-permute-start.35 = (bf16[128,1024]{1,0:T(8,128)(2,1)S(1)}, bf16[128,1024]{1,0:T(8,128)(2,1)S(1)}, u32[]{:S(2)}, u32[]{:S(2)}) collective-permute-start(bf16[128,1024]{1,0:T(8,128)(2,1)S(1)} %get-tuple-element.166), channel_id=1, source_target_pairs={{0,1},{1,0},{2,3},{3,2},{4,5},{5,4},{6,7},{7,6},{8,9},{9,8},{10,11... | collective-permute-start | bytes 786440 | tf_op jit(solution)/shard_map/ppermute | solution.py:529
  108.4 6.0 %collective-permute-start.37 = (f32[8,1024]{1,0:T(8,128)S(1)}, f32[8,1024]{1,0:T(8,128)S(1)}, u32[]{:S(2)}, u32[]{:S(2)}) collective-permute-start(f32[8,1024]{1,0:T(8,128)S(1)} %get-tuple-element.176.refs_8_), channel_id=1, source_target_pairs={{0,4},{4,0},{8,12},{12,8},{16,20},{20,16},{24,28},{28,24},{1,5},{5... | collective-permute-start | bytes 98312 | tf_op jit(solution)/shard_map/ppermute | solution.py:523
  114.4 4.5 %copy-start = (bf16[128,1024]{1,0:T(8,128)(2,1)S(1)}, bf16[128,1024]{1,0:T(8,128)(2,1)}, u32[]{:S(2)}) copy-start(bf16[128,1024]{1,0:T(8,128)(2,1)} %param.15) | copy-start | bytes 786436
  114.4 4.5 %copy-start.3 = (f32[1024]{0:T(1024)S(1)}, f32[1024]{0:T(1024)}, u32[]{:S(2)}) copy-start(f32[1024]{0:T(1024)} %param.28) | copy-start | bytes 12292
  114.4 4.5 %copy-start.4 = (f32[1024]{0:T(1024)S(1)}, f32[1024]{0:T(1024)}, u32[]{:S(2)}) copy-start(f32[1024]{0:T(1024)} %param.24) | copy-start | bytes 12292
  115.2 8.6 %collective-permute-start.38 = (bf16[128,1536]{1,0:T(8,128)(2,1)S(1)}, bf16[128,1536]{1,0:T(8,128)(2,1)S(1)}, u32[]{:S(2)}, u32[]{:S(2)}) collective-permute-start(bf16[128,1536]{1,0:T(8,128)(2,1)S(1)} %get-tuple-element.177), channel_id=1, source_target_pairs={{0,16},{4,20},{8,24},{12,28},{16,0},{20,4},{24,8},{28,12},{1,17},{... | collective-permute-start | bytes 1179656 | tf_op jit(solution)/shard_map/ppermute | solution.py:526
  116.8 13.0 %collective-permute-start.39 = (bf16[144,1024]{1,0:T(8,128)(2,1)S(1)}, bf16[144,1024]{1,0:T(8,128)(2,1)S(1)}, u32[]{:S(2)}, u32[]{:S(2)}) collective-permute-start(bf16[144,1024]{1,0:T(8,128)(2,1)S(1)} %get-tuple-element.180), channel_id=1, source_target_pairs={{0,1},{1,0},{2,3},{3,2},{4,5},{5,4},{6,7},{7,6},{8,9},{9,8},{10,11... | collective-permute-start | bytes 884744 | tf_op jit(solution)/shard_map/ppermute | solution.py:529
  116.9 14.5 %collective-permute-start.40 = (bf16[144,1024]{1,0:T(8,128)(2,1)S(1)}, bf16[144,1024]{1,0:T(8,128)(2,1)S(1)}, u32[]{:S(2)}, u32[]{:S(2)}) collective-permute-start(bf16[144,1024]{1,0:T(8,128)(2,1)S(1)} %get-tuple-element.181), channel_id=1, source_target_pairs={{0,2},{1,3},{2,0},{3,1},{4,6},{5,7},{6,4},{7,5},{8,10},{9,11},{10,... | collective-permute-start | bytes 884744 | tf_op jit(solution)/shard_map/ppermute | solution.py:529
  119.7 10.1 %collective-permute-start.41 = (f32[8,1024]{1,0:T(8,128)S(1)}, f32[8,1024]{1,0:T(8,128)S(1)}, u32[]{:S(2)}, u32[]{:S(2)}) collective-permute-start(f32[8,1024]{1,0:T(8,128)S(1)} %get-tuple-element.182.sums), channel_id=1, source_target_pairs={{0,3},{1,2},{2,1},{3,0},{4,7},{5,6},{6,5},{7,4},{8,11},{9,10},{10,... | collective-permute-start | bytes 98312 | tf_op jit(solution)/shard_map/ppermute | solution.py:529
  123.3 10.7 %collective-permute-start.42 = (bf16[128,1536]{1,0:T(8,128)(2,1)S(1)}, bf16[128,1536]{1,0:T(8,128)(2,1)S(1)}, u32[]{:S(2)}, u32[]{:S(2)}) collective-permute-start(bf16[128,1536]{1,0:T(8,128)(2,1)S(1)} %get-tuple-element.185), channel_id=1, source_target_pairs={{0,8},{4,12},{8,0},{12,4},{16,24},{20,28},{24,16},{28,20},{1,9},{5... | collective-permute-start | bytes 1179656 | tf_op jit(solution)/shard_map/ppermute | solution.py:526
  124.6 9.5 %collective-permute-start.43 = (bf16[128,1536]{1,0:T(8,128)(2,1)S(1)}, bf16[128,1536]{1,0:T(8,128)(2,1)S(1)}, u32[]{:S(2)}, u32[]{:S(2)}) collective-permute-start(bf16[128,1536]{1,0:T(8,128)(2,1)S(1)} %other_sums.1), channel_id=1, source_target_pairs={{0,4},{4,0},{8,12},{12,8},{16,20},{20,16},{24,28},{28,24},{1,5},{5... | collective-permute-start | bytes 1179656 | tf_op jit(solution)/shard_map/ppermute | solution.py:523
  133.1 2.7 %copy-start.1 = (f32[1,1024]{1,0:T(1,128)}, f32[1,1024]{1,0:T(1,128)S(1)}, u32[]{:S(2)}) copy-start(f32[1,1024]{1,0:T(1,128)S(1)} %get-tuple-element.206) | copy-start | bytes 12292

commit v4 on v3

--- a/solution.py
+++ b/solution.py
@@ -336,7 +336,8 @@
 
 
 def get_sums(ref, row):
-    return ref[row : row + 8, :].astype(F32) + ref[row + 8 : row + 16, :].astype(F32)
+    value = ref[row : row + 16, :].astype(F32)
+    return value[0:8] + value[8:16]
 
 
 def combine_body(tz, place, own, other, *outs):

time: 137 us -> 137 us (level)
  no operation moved by 1% of the time
where the time goes in v4:
time: 137 us; the launch traced here: 136 us
  starting transfers between devices  52.2 us (38%)
  Pallas kernels  36.9 us (27%)
  waiting for transfers between devices  32.7 us (24%)
  local copies, waits for them, and re-layouts  7.32 us (5%)
  other arithmetic  6.29 us (5%)
    pallas_call x12, Pallas kernels, kernel_call(): pl.pallas_call(body, name=name, out_shape=outs, in_specs=[SMEM] + [VMEM]...  36.9 us
    ppermute x13, starting transfers between devices, over_tensor(): return lax.ppermute(values, 'tensor', xor_pairs(tz, flip))  27.1 us
    ppermute x15, starting transfers between devices, over_chip(): return lax.ppermute(values, 'dp', xor_pairs(dp, 2 * flip))  21.9 us
    ppermute x13, waiting for transfers between devices, over_tensor(): return lax.ppermute(values, 'tensor', xor_pairs(tz, flip))  17.9 us
    ppermute x15, waiting for transfers between devices, over_chip(): return lax.ppermute(values, 'dp', xor_pairs(dp, 2 * flip))  12.1 us
  transfers between devices with their start and end apart: 44, of which 14 were waited for; matrix products, arithmetic and copies ran while one was open for 9% of the time, Pallas kernels for 24%

profile of v4, /device:TPU:0, one launch (start us, length us, event | category | flops | bytes accessed | tf_op | source)
XLA Modules:
  0.0 136.4 jit_solution(13399720850812833945)
XLA Ops:
  0.8 1.9 %pack_weights.1 = (bf16[128,1536]{1,0:T(8,128)(2,1)S(1)}, bf16[128,1536]{1,0:T(8,128)(2,1)S(1)}) custom-call(s32[4]{0:T(128)S(1)} %pad_add_fusion.1.place.refs_0_, bf16[128,768]{1,0:T(8,128)(2,1)} %qkv_in.1, bf16[128,1024]{1,0:T(8,128)(2,1)} %fc1_in.1, bf16[128,256]{1,0:T(8,128)(2,1)} %dense_in.1, bf16[128,1024]{1,0:T(8,128)(2,1)} %fc2_in.1), custom_call_target="tpu_custom_call" | custom-call | flops 11500000 | tf_op jit(solution)/shard_map/pack_weights/pallas_call | solution.py:43
  2.7 3.0 %collective-permute-start.3 = (bf16[128,1536]{1,0:T(8,128)(2,1)S(1)}, bf16[128,1536]{1,0:T(8,128)(2,1)S(1)}, u32[]{:S(2)}, u32[]{:S(2)}) collective-permute-start(bf16[128,1536]{1,0:T(8,128)(2,1)S(1)} %get-tuple-element.102.refs_13_), channel_id=1, source_target_pairs={{0,8},{4,12},{8,0},{12,4},{16,24},{20,28},{24,16},{28,20},{1,9},{5... | collective-permute-start | bytes 1179656 | tf_op jit(solution)/shard_map/ppermute | solution.py:527
  5.7 1.5 %collective-permute-start.4 = (bf16[128,1536]{1,0:T(8,128)(2,1)S(1)}, bf16[128,1536]{1,0:T(8,128)(2,1)S(1)}, u32[]{:S(2)}, u32[]{:S(2)}) collective-permute-start(bf16[128,1536]{1,0:T(8,128)(2,1)S(1)} %get-tuple-element.102.refs_13_), channel_id=1, source_target_pairs={{0,16},{4,20},{8,24},{12,28},{16,0},{20,4},{24,8},{28,12},{1,17},{... | collective-permute-start | bytes 1179656 | tf_op jit(solution)/shard_map/ppermute | solution.py:527
  7.2 1.1 constant_dynamic-slice_fusion.15
  8.3 1.6 %collective-permute-start = (bf16[128,1024]{1,0:T(8,128)(2,1)S(1)}, bf16[128,1024]{1,0:T(8,128)(2,1)S(1)}, u32[]{:S(2)}, u32[]{:S(2)}) collective-permute-start(bf16[128,1024]{1,0:T(8,128)(2,1)S(1)} %pad_maximum_fusion.2.refs_5_.x), channel_id=1, source_target_pairs={{0,1},{1,0},{2,3},{3,2},{4,5},{5,4},{6,7},{7,6},{8,9},{9,8},{10,11... | collective-permute-start | bytes 786440 | tf_op jit(solution)/shard_map/ppermute | solution.py:530
  10.0 2.6 %collective-permute-start.1 = (bf16[128,1024]{1,0:T(8,128)(2,1)S(1)}, bf16[128,1024]{1,0:T(8,128)(2,1)}, u32[]{:S(2)}, u32[]{:S(2)}) collective-permute-start(bf16[128,1024]{1,0:T(8,128)(2,1)S(1)} %pad_maximum_fusion.2.refs_5_.x), channel_id=1, source_target_pairs={{0,2},{1,3},{2,0},{3,1},{4,6},{5,7},{6,4},{7,5},{8,10},{9,11},{10,... | collective-permute-start | bytes 786440 | tf_op jit(solution)/shard_map/ppermute | solution.py:530
  12.8 2.0 %collective-permute-done.3.refs_15_ = bf16[128,1536]{1,0:T(8,128)(2,1)S(1)} collective-permute-done((bf16[128,1536]{1,0:T(8,128)(2,1)S(1)}, bf16[128,1536]{1,0:T(8,128)(2,1)S(1)}, u32[]{:S(2)}, u32[]{:S(2)}) %collective-permute-start.3) | collective-permute-done | bytes 393248 | tf_op jit(solution)/shard_map/ppermute | solution.py:527
  14.8 3.9 %collective-permute-start.2 = (bf16[128,1024]{1,0:T(8,128)(2,1)S(1)}, bf16[128,1024]{1,0:T(8,128)(2,1)}, u32[]{:S(2)}, u32[]{:S(2)}) collective-permute-start(bf16[128,1024]{1,0:T(8,128)(2,1)S(1)} %pad_maximum_fusion.2.refs_5_.x), channel_id=1, source_target_pairs={{0,3},{1,2},{2,1},{3,0},{4,7},{5,6},{6,5},{7,4},{8,11},{9,10},{10,... | collective-permute-start | bytes 786440 | tf_op jit(solution)/shard_map/ppermute | solution.py:530
  18.7 1.6 %collective-permute-start.6 = (bf16[128,1536]{1,0:T(8,128)(2,1)}, bf16[128,1536]{1,0:T(8,128)(2,1)}, u32[]{:S(2)}, u32[]{:S(2)}) collective-permute-start(bf16[128,1536]{1,0:T(8,128)(2,1)} %collective-permute-done.5.refs_14_), channel_id=1, source_target_pairs={{0,8},{4,12},{8,0},{12,4},{16,24},{20,28},{24,16},{28,20},{1,9},{5... | collective-permute-start | bytes 1179656 | tf_op jit(solution)/shard_map/ppermute | solution.py:527
  20.2 1.5 %collective-permute-start.7 = (bf16[128,1536]{1,0:T(8,128)(2,1)}, bf16[128,1536]{1,0:T(8,128)(2,1)}, u32[]{:S(2)}, u32[]{:S(2)}) collective-permute-start(bf16[128,1536]{1,0:T(8,128)(2,1)} %collective-permute-done.5.refs_14_), channel_id=1, source_target_pairs={{0,16},{4,20},{8,24},{12,28},{16,0},{20,4},{24,8},{28,12},{1,17},{... | collective-permute-start | bytes 1179656 | tf_op jit(solution)/shard_map/ppermute | solution.py:527
  22.3 1.9 %multiply_cosine_fusion = (f32[1024,128]{1,0:T(8,128)S(1)}, f32[1024,128]{1,0:T(8,128)S(1)}) fusion(f32[128]{0:T(128)S(1)} %get-tuple-element.226, f32[1024]{0:T(1024)S(1)} %get-tuple-element.217, f32[128]{0:T(128)S(1)} %get-tuple-element.225), kind=kLoop, calls=%fused_computation.3 | loop fusion | flops 262144 | bytes 1053696 | tf_op jit(solution)/shard_map/cos | solution.py:575
  24.8 5.8 %collective-permute-done.1.refs_7_ = bf16[128,1024]{1,0:T(8,128)(2,1)} collective-permute-done((bf16[128,1024]{1,0:T(8,128)(2,1)S(1)}, bf16[128,1024]{1,0:T(8,128)(2,1)}, u32[]{:S(2)}, u32[]{:S(2)}) %collective-permute-start.1) | collective-permute-done | bytes 262176 | tf_op jit(solution)/shard_map/ppermute | solution.py:530
  30.6 1.1 collective-permute-done.7.refs_18_
  32.7 0.8 dynamic_slice.82
  33.5 1.5 %collective-permute-start.14 = (bf16[128,1536]{1,0:T(8,128)(2,1)S(1)}, bf16[128,1536]{1,0:T(8,128)(2,1)}, u32[]{:S(2)}, u32[]{:S(2)}) collective-permute-start(bf16[128,1536]{1,0:T(8,128)(2,1)S(1)} %collective-permute-done.3.refs_15_), channel_id=1, source_target_pairs={{0,16},{4,20},{8,24},{12,28},{16,0},{20,4},{24,8},{28,12},{1,17},{... | collective-permute-start | bytes 1179656 | tf_op jit(solution)/shard_map/ppermute | solution.py:527
  35.0 1.1 collective-permute-start.15
  36.1 0.6 fusion.12
  36.7 2.4 %collective-permute-start.16 = (bf16[128,1024]{1,0:T(8,128)(2,1)S(1)}, bf16[128,1024]{1,0:T(8,128)(2,1)}, u32[]{:S(2)}, u32[]{:S(2)}) collective-permute-start(bf16[128,1024]{1,0:T(8,128)(2,1)S(1)} %maximum_select_fusion.refs_0_.cot), channel_id=1, source_target_pairs={{0,1},{1,0},{2,3},{3,2},{4,5},{5,4},{6,7},{7,6},{8,9},{9,8},{10,11... | collective-permute-start | bytes 786440 | tf_op jit(solution)/shard_map/ppermute | solution.py:530
  39.1 1.1 collective-permute-start.17
  40.2 1.4 %collective-permute-start.18 = (bf16[128,1024]{1,0:T(8,128)(2,1)S(1)}, bf16[128,1024]{1,0:T(8,128)(2,1)}, u32[]{:S(2)}, u32[]{:S(2)}) collective-permute-start(bf16[128,1024]{1,0:T(8,128)(2,1)S(1)} %maximum_select_fusion.refs_0_.cot), channel_id=1, source_target_pairs={{0,3},{1,2},{2,1},{3,0},{4,7},{5,6},{6,5},{7,4},{8,11},{9,10},{10,... | collective-permute-start | bytes 786440 | tf_op jit(solution)/shard_map/ppermute | solution.py:530
  41.7 1.3 pad_maximum_fusion.3
  43.0 0.8 concatenate.29
  43.8 0.8 dynamic_slice.83
  44.6 0.7 constant_dynamic-slice_fusion.11
  45.3 0.8 collective-permute-done.15.refs_20_
  46.1 11.9 %forward.1 = (bf16[512,1024]{1,0:T(8,128)(2,1)S(1)}, bf16[512,1024]{1,0:T(8,128)(2,1)S(1)}, bf16[1024,1024]{1,0:T(8,128)(2,1)S(1)}, bf16[1024,1536]{1,0:T(8,128)...) custom-call(s32[4]{0:T(128)S(1)} %pad_add_fusion.1.place.refs_0_, ...), custom_call_target="tpu_custom_call" | custom-call | flops 11500000 | tf_op jit(solution)/shard_map/forward/pallas_call | solution.py:43
  58.0 2.6 %collective-permute-done.17.refs_2_ = bf16[128,1024]{1,0:T(8,128)(2,1)} collective-permute-done((bf16[128,1024]{1,0:T(8,128)(2,1)S(1)}, bf16[128,1024]{1,0:T(8,128)(2,1)}, u32[]{:S(2)}, u32[]{:S(2)}) %collective-permute-start.17) | collective-permute-done | bytes 262176 | tf_op jit(solution)/shard_map/ppermute | solution.py:530
  60.6 2.7 %collective-permute-done.19.other = bf16[512,1024]{1,0:T(8,128)(2,1)S(1)} collective-permute-done((bf16[512,1024]{1,0:T(8,128)(2,1)S(1)}, bf16[512,1024]{1,0:T(8,128)(2,1)S(1)}, u32[]{:S(2)}, u32[]{:S(2)}) %collective-permute-start.19) | collective-permute-done | bytes 1048608 | tf_op jit(solution)/shard_map/ppermute | solution.py:524
  63.9 0.8 add_sibling.1
  64.7 4.5 %collective-permute-start.24 = (bf16[128,1024]{1,0:T(8,128)(2,1)S(1)}, bf16[128,1024]{1,0:T(8,128)(2,1)S(1)}, u32[]{:S(2)}, u32[]{:S(2)}) collective-permute-start(bf16[128,1024]{1,0:T(8,128)(2,1)S(1)} %get-tuple-element.134), channel_id=1, source_target_pairs={{0,1},{1,0},{2,3},{3,2},{4,5},{5,4},{6,7},{7,6},{8,9},{9,8},{10,11... | collective-permute-start | bytes 786440 | tf_op jit(solution)/shard_map/ppermute | solution.py:530
  69.3 0.7 collective-permute-start.26
  70.0 3.7 %second_grads.1 = (bf16[1024,1024]{1,0:T(8,128)(2,1)S(1)}, bf16[128,640]{1,0:T(8,128)(2,1)S(1)}, bf16[128,640]{1,0:T(8,128)(2,1)S(1)}, bf16[256,640]{1,0:T(8,128...) custom-call(s32[4]{0:T(128)S(1)} %pad_add_fusion.1.place.refs_0_, ...), custom_call_target="tpu_custom_call" | custom-call | flops 11500000 | tf_op jit(solution)/shard_map/second_grads/pallas_call | solution.py:43
  73.7 2.6 %collective-permute-done.24.passed = bf16[128,1024]{1,0:T(8,128)(2,1)S(1)} collective-permute-done((bf16[128,1024]{1,0:T(8,128)(2,1)S(1)}, bf16[128,1024]{1,0:T(8,128)(2,1)S(1)}, u32[]{:S(2)}, u32[]{:S(2)}) %collective-permute-start.24) | collective-permute-done | bytes 262176 | tf_op jit(solution)/shard_map/ppermute | solution.py:530
  76.4 0.6 branch_relay.1
  77.0 3.1 %collective-permute-start.25 = (bf16[128,1024]{1,0:T(8,128)(2,1)S(1)}, bf16[128,1024]{1,0:T(8,128)(2,1)S(1)}, u32[]{:S(2)}, u32[]{:S(2)}) collective-permute-start(bf16[128,1024]{1,0:T(8,128)(2,1)S(1)} %branch_relay.1), channel_id=1, source_target_pairs={{0,2},{1,3},{2,0},{3,1},{4,6},{5,7},{6,4},{7,5},{8,10},{9,11},{10,... | collective-permute-start | bytes 786440 | tf_op jit(solution)/shard_map/ppermute | solution.py:530
  80.0 1.5 %collective-permute-start.27 = (bf16[256,640]{1,0:T(8,128)(2,1)S(1)}, bf16[256,640]{1,0:T(8,128)(2,1)S(1)}, u32[]{:S(2)}, u32[]{:S(2)}) collective-permute-start(bf16[256,640]{1,0:T(8,128)(2,1)S(1)} %get-tuple-element.135), channel_id=1, source_target_pairs={{0,16},{4,20},{8,24},{12,28},{16,0},{20,4},{24,8},{28,12},{1,17},{... | collective-permute-start | bytes 983048 | tf_op jit(solution)/shard_map/ppermute | solution.py:527
  81.6 1.5 %collective-permute-start.28 = (bf16[256,640]{1,0:T(8,128)(2,1)S(1)}, bf16[256,640]{1,0:T(8,128)(2,1)S(1)}, u32[]{:S(2)}, u32[]{:S(2)}) collective-permute-start(bf16[256,640]{1,0:T(8,128)(2,1)S(1)} %get-tuple-element.136), channel_id=1, source_target_pairs={{0,8},{4,12},{8,0},{12,4},{16,24},{20,28},{24,16},{28,20},{1,9},{5... | collective-permute-start | bytes 983048 | tf_op jit(solution)/shard_map/ppermute | solution.py:527
  83.0 9.7 %backward.1 = (bf16[512,1024]{1,0:T(8,128)(2,1)S(1)}, bf16[528,1024]{1,0:T(8,128)(2,1)S(1)}, bf16[1024,896]{1,0:T(8,128)(2,1)S(1)}, f32[8,1024]{1,0:T(8,128)S(1)}) custom-call(s32[4]{0:T(128)S(1)} %pad_add_fusion.1.place.refs_0_, f32[1024,384]{1,0:T(8,128)S(1)} %pad_maximum_fusion.refs_1_, f32[4,1024]{1,0:T(4,128)S(1)} %pad_maximum_fusion.4.refs_2_, ...), custom_call_target="tpu_custom_call" | custom-call | flops 16099999744 | tf_op jit(solution)/shard_map/backward/pallas_call | solution.py:43
  92.7 3.2 %first_grads.1 = (bf16[128,896]{1,0:T(8,128)(2,1)S(1)}, bf16[128,896]{1,0:T(8,128)(2,1)S(1)}, bf16[256,896]{1,0:T(8,128)(2,1)S(1)}, bf16[256,896]{1,0:T(8,128)(2...) custom-call(s32[4]{0:T(128)S(1)} %pad_add_fusion.1.place.refs_0_, ...), custom_call_target="tpu_custom_call" | custom-call | flops 11500000 | tf_op jit(solution)/shard_map/first_grads/pallas_call | solution.py:43
  96.1 0.6 collective-permute-start.29
  97.2 2.4 %collective-permute-start.31 = (f32[8,1024]{1,0:T(8,128)S(1)}, f32[8,1024]{1,0:T(8,128)S(1)}, u32[]{:S(2)}, u32[]{:S(2)}) collective-permute-start(f32[8,1024]{1,0:T(8,128)S(1)} %get-tuple-element.157.refs_0_), channel_id=1, source_target_pairs={{0,24},{4,28},{8,16},{12,20},{16,8},{20,12},{24,0},{28,4},{1,25},{... | collective-permute-start | bytes 98312 | tf_op jit(solution)/shard_map/ppermute | solution.py:527
  100.6 1.4 %collective-permute-done.31.refs_3_ = f32[8,1024]{1,0:T(8,128)S(1)} collective-permute-done((f32[8,1024]{1,0:T(8,128)S(1)}, f32[8,1024]{1,0:T(8,128)S(1)}, u32[]{:S(2)}, u32[]{:S(2)}) %collective-permute-start.31) | collective-permute-done | bytes 32800 | tf_op jit(solution)/shard_map/ppermute | solution.py:527
  102.0 1.5 %collective-permute-start.32 = (bf16[256,896]{1,0:T(8,128)(2,1)S(1)}, bf16[256,896]{1,0:T(8,128)(2,1)S(1)}, u32[]{:S(2)}, u32[]{:S(2)}) collective-permute-start(bf16[256,896]{1,0:T(8,128)(2,1)S(1)} %get-tuple-element.158), channel_id=1, source_target_pairs={{0,8},{4,12},{8,0},{12,4},{16,24},{20,28},{24,16},{28,20},{1,9},{5... | collective-permute-start | bytes 1376264 | tf_op jit(solution)/shard_map/ppermute | solution.py:527
  103.5 1.5 %collective-permute-start.36 = (bf16[256,896]{1,0:T(8,128)(2,1)S(1)}, bf16[256,896]{1,0:T(8,128)(2,1)S(1)}, u32[]{:S(2)}, u32[]{:S(2)}) collective-permute-start(bf16[256,896]{1,0:T(8,128)(2,1)S(1)} %get-tuple-element.172), channel_id=1, source_target_pairs={{0,16},{4,20},{8,24},{12,28},{16,0},{20,4},{24,8},{28,12},{1,17},{... | collective-permute-start | bytes 1376264 | tf_op jit(solution)/shard_map/ppermute | solution.py:527
  105.0 0.8 split_back.1
  105.8 0.7 collective-permute-start.34
  106.5 1.9 %collective-permute-start.35 = (bf16[128,1024]{1,0:T(8,128)(2,1)S(1)}, bf16[128,1024]{1,0:T(8,128)(2,1)S(1)}, u32[]{:S(2)}, u32[]{:S(2)}) collective-permute-start(bf16[128,1024]{1,0:T(8,128)(2,1)S(1)} %get-tuple-element.166), channel_id=1, source_target_pairs={{0,1},{1,0},{2,3},{3,2},{4,5},{5,4},{6,7},{7,6},{8,9},{9,8},{10,11... | collective-permute-start | bytes 786440 | tf_op jit(solution)/shard_map/ppermute | solution.py:530
  108.6 4.6 %collective-permute-done.32.refs_3_.first_x = bf16[256,896]{1,0:T(8,128)(2,1)S(1)} collective-permute-done((bf16[256,896]{1,0:T(8,128)(2,1)S(1)}, bf16[256,896]{1,0:T(8,128)(2,1)S(1)}, u32[]{:S(2)}, u32[]{:S(2)}) %collective-permute-start.32) | collective-permute-done | bytes 458784 | tf_op jit(solution)/shard_map/ppermute | solution.py:527
  113.2 1.2 collective-permute-done.36.refs_2_.refs_1_
  114.4 0.8 second_round.1
  115.2 1.6 %collective-permute-start.38 = (bf16[128,1536]{1,0:T(8,128)(2,1)S(1)}, bf16[128,1536]{1,0:T(8,128)(2,1)S(1)}, u32[]{:S(2)}, u32[]{:S(2)}) collective-permute-start(bf16[128,1536]{1,0:T(8,128)(2,1)S(1)} %get-tuple-element.177), channel_id=1, source_target_pairs={{0,16},{4,20},{8,24},{12,28},{16,0},{20,4},{24,8},{28,12},{1,17},{... | collective-permute-start | bytes 1179656 | tf_op jit(solution)/shard_map/ppermute | solution.py:527
  116.9 2.0 %collective-permute-start.40 = (bf16[144,1024]{1,0:T(8,128)(2,1)S(1)}, bf16[144,1024]{1,0:T(8,128)(2,1)S(1)}, u32[]{:S(2)}, u32[]{:S(2)}) collective-permute-start(bf16[144,1024]{1,0:T(8,128)(2,1)S(1)} %get-tuple-element.181), channel_id=1, source_target_pairs={{0,2},{1,3},{2,0},{3,1},{4,6},{5,7},{6,4},{7,5},{8,10},{9,11},{10,... | collective-permute-start | bytes 884744 | tf_op jit(solution)/shard_map/ppermute | solution.py:530
  118.9 0.8 fusion.3
  119.7 2.3 %collective-permute-start.41 = (f32[8,1024]{1,0:T(8,128)S(1)}, f32[8,1024]{1,0:T(8,128)S(1)}, u32[]{:S(2)}, u32[]{:S(2)}) collective-permute-start(f32[8,1024]{1,0:T(8,128)S(1)} %get-tuple-element.182.sums), channel_id=1, source_target_pairs={{0,3},{1,2},{2,1},{3,0},{4,7},{5,6},{6,5},{7,4},{8,11},{9,10},{10,... | collective-permute-start | bytes 98312 | tf_op jit(solution)/shard_map/ppermute | solution.py:530
  122.1 0.6 slice_reduce_fusion
  122.7 0.6 slice.52
  123.9 0.7 other_sums.1
  124.6 5.2 %collective-permute-done.41.third = f32[8,1024]{1,0:T(8,128)S(1)} collective-permute-done((f32[8,1024]{1,0:T(8,128)S(1)}, f32[8,1024]{1,0:T(8,128)S(1)}, u32[]{:S(2)}, u32[]{:S(2)}) %collective-permute-start.41) | collective-permute-done | bytes 32800 | tf_op jit(solution)/shard_map/ppermute | solution.py:530
  129.8 1.6 %collective-permute-done.40.second = bf16[144,1024]{1,0:T(8,128)(2,1)S(1)} collective-permute-done((bf16[144,1024]{1,0:T(8,128)(2,1)S(1)}, bf16[144,1024]{1,0:T(8,128)(2,1)S(1)}, u32[]{:S(2)}, u32[]{:S(2)}) %collective-permute-start.40) | collective-permute-done | bytes 294944 | tf_op jit(solution)/shard_map/ppermute | solution.py:530
  131.5 1.0 finish_rows.1
  132.5 0.6 fusion.11
  133.2 0.8 pad_maximum_fusion.1
  134.0 1.8 %join_halves.1 = (f32[128,768]{1,0:T(8,128)}, f32[128,1024]{1,0:T(8,128)}, f32[128,256]{1,0:T(8,128)}, f32[128,1024]{1,0:T(8,128)}) custom-call(s32[4]{0:T(128)S(1)} %pad_add_fusion.1.place.refs_0_, bf16[128,896]{1,0:T(8,128)(2,1)S(1)} %get-tuple-element.149.refs_0_, bf16[256,896]{1,0:T(8,128)(2,1)S(1)} %collective-permute-done.36.refs_2_.refs_1_, ...), custom_call_target="tpu_custom_call" | custom-call | flops 11500000 | tf_op jit(solution)/shard_map/join_halves/pallas_call | solution.py:43
  135.8 0.6 copy.31
  (86 shorter events, 5.8 us)
Async XLA Ops:
  0.6 11.9 %copy-start.2 = (s32[512]{0:T(512)S(1)}, s32[512]{0:T(512)}, u32[]{:S(2)}) copy-start(s32[512]{0:T(512)} %param.16) | copy-start | bytes 6148
  2.7 12.1 %collective-permute-start.3 = (bf16[128,1536]{1,0:T(8,128)(2,1)S(1)}, bf16[128,1536]{1,0:T(8,128)(2,1)S(1)}, u32[]{:S(2)}, u32[]{:S(2)}) collective-permute-start(bf16[128,1536]{1,0:T(8,128)(2,1)S(1)} %get-tuple-element.102.refs_13_), channel_id=1, source_target_pairs={{0,8},{4,12},{8,0},{12,4},{16,24},{20,28},{24,16},{28,20},{1,9},{5... | collective-permute-start | bytes 1179656 | tf_op jit(solution)/shard_map/ppermute | solution.py:527
  5.7 13.0 %collective-permute-start.4 = (bf16[128,1536]{1,0:T(8,128)(2,1)S(1)}, bf16[128,1536]{1,0:T(8,128)(2,1)S(1)}, u32[]{:S(2)}, u32[]{:S(2)}) collective-permute-start(bf16[128,1536]{1,0:T(8,128)(2,1)S(1)} %get-tuple-element.102.refs_13_), channel_id=1, source_target_pairs={{0,16},{4,20},{8,24},{12,28},{16,0},{20,4},{24,8},{28,12},{1,17},{... | collective-permute-start | bytes 1179656 | tf_op jit(solution)/shard_map/ppermute | solution.py:527
  8.3 16.4 %collective-permute-start = (bf16[128,1024]{1,0:T(8,128)(2,1)S(1)}, bf16[128,1024]{1,0:T(8,128)(2,1)S(1)}, u32[]{:S(2)}, u32[]{:S(2)}) collective-permute-start(bf16[128,1024]{1,0:T(8,128)(2,1)S(1)} %pad_maximum_fusion.2.refs_5_.x), channel_id=1, source_target_pairs={{0,1},{1,0},{2,3},{3,2},{4,5},{5,4},{6,7},{7,6},{8,9},{9,8},{10,11... | collective-permute-start | bytes 786440 | tf_op jit(solution)/shard_map/ppermute | solution.py:530
  10.0 20.7 %collective-permute-start.1 = (bf16[128,1024]{1,0:T(8,128)(2,1)S(1)}, bf16[128,1024]{1,0:T(8,128)(2,1)}, u32[]{:S(2)}, u32[]{:S(2)}) collective-permute-start(bf16[128,1024]{1,0:T(8,128)(2,1)S(1)} %pad_maximum_fusion.2.refs_5_.x), channel_id=1, source_target_pairs={{0,2},{1,3},{2,0},{3,1},{4,6},{5,7},{6,4},{7,5},{8,10},{9,11},{10,... | collective-permute-start | bytes 786440 | tf_op jit(solution)/shard_map/ppermute | solution.py:530
  12.5 6.1 %collective-permute-start.5 = (bf16[128,1536]{1,0:T(8,128)(2,1)S(1)}, bf16[128,1536]{1,0:T(8,128)(2,1)}, u32[]{:S(2)}, u32[]{:S(2)}) collective-permute-start(bf16[128,1536]{1,0:T(8,128)(2,1)S(1)} %get-tuple-element.104), channel_id=1, source_target_pairs={{0,4},{4,0},{8,12},{12,8},{16,20},{20,16},{24,28},{28,24},{1,5},{5... | collective-permute-start | bytes 1179656 | tf_op jit(solution)/shard_map/ppermute | solution.py:524
  14.8 15.9 %collective-permute-start.2 = (bf16[128,1024]{1,0:T(8,128)(2,1)S(1)}, bf16[128,1024]{1,0:T(8,128)(2,1)}, u32[]{:S(2)}, u32[]{:S(2)}) collective-permute-start(bf16[128,1024]{1,0:T(8,128)(2,1)S(1)} %pad_maximum_fusion.2.refs_5_.x), channel_id=1, source_target_pairs={{0,3},{1,2},{2,1},{3,0},{4,7},{5,6},{6,5},{7,4},{8,11},{9,10},{10,... | collective-permute-start | bytes 786440 | tf_op jit(solution)/shard_map/ppermute | solution.py:530
  18.6 1.6 %collective-permute-start.8 = (s32[512]{0:T(512)S(1)}, s32[512]{0:T(512)S(1)}, u32[]{:S(2)}, u32[]{:S(2)}) collective-permute-start(s32[512]{0:T(512)S(1)} %copy-done.2), channel_id=1, source_target_pairs={{0,4},{4,0},{8,12},{12,8},{16,20},{20,16},{24,28},{28,24},{1,5},{5... | collective-permute-start | bytes 6152 | tf_op jit(solution)/shard_map/ppermute | solution.py:524
  18.7 12.0 %collective-permute-start.6 = (bf16[128,1536]{1,0:T(8,128)(2,1)}, bf16[128,1536]{1,0:T(8,128)(2,1)}, u32[]{:S(2)}, u32[]{:S(2)}) collective-permute-start(bf16[128,1536]{1,0:T(8,128)(2,1)} %collective-permute-done.5.refs_14_), channel_id=1, source_target_pairs={{0,8},{4,12},{8,0},{12,4},{16,24},{20,28},{24,16},{28,20},{1,9},{5... | collective-permute-start | bytes 1179656 | tf_op jit(solution)/shard_map/ppermute | solution.py:527
  20.2 11.5 %collective-permute-start.7 = (bf16[128,1536]{1,0:T(8,128)(2,1)}, bf16[128,1536]{1,0:T(8,128)(2,1)}, u32[]{:S(2)}, u32[]{:S(2)}) collective-permute-start(bf16[128,1536]{1,0:T(8,128)(2,1)} %collective-permute-done.5.refs_14_), channel_id=1, source_target_pairs={{0,16},{4,20},{8,24},{12,28},{16,0},{20,4},{24,8},{28,12},{1,17},{... | collective-permute-start | bytes 1179656 | tf_op jit(solution)/shard_map/ppermute | solution.py:527
  24.2 17.4 %copy-start.5 = (f32[1024]{0:T(1024)S(1)}, f32[1024]{0:T(1024)}, u32[]{:S(2)}) copy-start(f32[1024]{0:T(1024)} %param.20) | copy-start | bytes 12292
  24.2 17.4 %copy-start.6 = (f32[1024]{0:T(1024)S(1)}, f32[1024]{0:T(1024)}, u32[]{:S(2)}) copy-start(f32[1024]{0:T(1024)} %param.19) | copy-start | bytes 12292
  24.3 17.4 %copy-start.7 = (f32[1024]{0:T(1024)S(1)}, f32[1024]{0:T(1024)}, u32[]{:S(2)}) copy-start(f32[1024]{0:T(1024)} %param.18) | copy-start | bytes 12292
  24.7 8.8 %collective-permute-start.10 = (bf16[128,1024]{1,0:T(8,128)(2,1)S(1)}, bf16[128,1024]{1,0:T(8,128)(2,1)}, u32[]{:S(2)}, u32[]{:S(2)}) collective-permute-start(bf16[128,1024]{1,0:T(8,128)(2,1)S(1)} %pad_maximum_fusion.2.refs_5_.x), channel_id=1, source_target_pairs={{0,4},{4,0},{8,12},{12,8},{16,20},{20,16},{24,28},{28,24},{1,5},{5... | collective-permute-start | bytes 786440 | tf_op jit(solution)/shard_map/ppermute | solution.py:524
  31.7 3.3 %collective-permute-start.9 = (bf16[128,1024]{1,0:T(8,128)(2,1)S(1)}, bf16[128,1024]{1,0:T(8,128)(2,1)}, u32[]{:S(2)}, u32[]{:S(2)}) collective-permute-start(bf16[128,1024]{1,0:T(8,128)(2,1)S(1)} %maximum_select_fusion.refs_0_.cot), channel_id=1, source_target_pairs={{0,4},{4,0},{8,12},{12,8},{16,20},{20,16},{24,28},{28,24},{1,5},{5... | collective-permute-start | bytes 786440 | tf_op jit(solution)/shard_map/ppermute | solution.py:524
  31.7 5.0 %collective-permute-start.11 = (bf16[128,1024]{1,0:T(8,128)(2,1)S(1)}, bf16[128,1024]{1,0:T(8,128)(2,1)}, u32[]{:S(2)}, u32[]{:S(2)}) collective-permute-start(bf16[128,1024]{1,0:T(8,128)(2,1)S(1)} %collective-permute-done.refs_6_), channel_id=1, source_target_pairs={{0,4},{4,0},{8,12},{12,8},{16,20},{20,16},{24,28},{28,24},{1,5},{5... | collective-permute-start | bytes 786440 | tf_op jit(solution)/shard_map/ppermute | solution.py:524
  32.2 6.9 %collective-permute-start.12 = (bf16[128,1024]{1,0:T(8,128)(2,1)}, bf16[128,1024]{1,0:T(8,128)(2,1)}, u32[]{:S(2)}, u32[]{:S(2)}) collective-permute-start(bf16[128,1024]{1,0:T(8,128)(2,1)} %collective-permute-done.1.refs_7_), channel_id=1, source_target_pairs={{0,4},{4,0},{8,12},{12,8},{16,20},{20,16},{24,28},{28,24},{1,5},{5... | collective-permute-start | bytes 786440 | tf_op jit(solution)/shard_map/ppermute | solution.py:524
  32.2 8.0 %collective-permute-start.13 = (bf16[128,1024]{1,0:T(8,128)(2,1)}, bf16[128,1024]{1,0:T(8,128)(2,1)}, u32[]{:S(2)}, u32[]{:S(2)}) collective-permute-start(bf16[128,1024]{1,0:T(8,128)(2,1)} %collective-permute-done.2.refs_8_), channel_id=1, source_target_pairs={{0,4},{4,0},{8,12},{12,8},{16,20},{20,16},{24,28},{28,24},{1,5},{5... | collective-permute-start | bytes 786440 | tf_op jit(solution)/shard_map/ppermute | solution.py:524
  33.5 11.8 %collective-permute-start.14 = (bf16[128,1536]{1,0:T(8,128)(2,1)S(1)}, bf16[128,1536]{1,0:T(8,128)(2,1)}, u32[]{:S(2)}, u32[]{:S(2)}) collective-permute-start(bf16[128,1536]{1,0:T(8,128)(2,1)S(1)} %collective-permute-done.3.refs_15_), channel_id=1, source_target_pairs={{0,16},{4,20},{8,24},{12,28},{16,0},{20,4},{24,8},{28,12},{1,17},{... | collective-permute-start | bytes 1179656 | tf_op jit(solution)/shard_map/ppermute | solution.py:527
  35.0 11.1 %collective-permute-start.15 = (bf16[128,1536]{1,0:T(8,128)(2,1)}, bf16[128,1536]{1,0:T(8,128)(2,1)}, u32[]{:S(2)}, u32[]{:S(2)}) collective-permute-start(bf16[128,1536]{1,0:T(8,128)(2,1)} %collective-permute-done.7.refs_18_), channel_id=1, source_target_pairs={{0,8},{4,12},{8,0},{12,4},{16,24},{20,28},{24,16},{28,20},{1,9},{5... | collective-permute-start | bytes 1179656 | tf_op jit(solution)/shard_map/ppermute | solution.py:527
  36.7 21.3 %collective-permute-start.16 = (bf16[128,1024]{1,0:T(8,128)(2,1)S(1)}, bf16[128,1024]{1,0:T(8,128)(2,1)}, u32[]{:S(2)}, u32[]{:S(2)}) collective-permute-start(bf16[128,1024]{1,0:T(8,128)(2,1)S(1)} %maximum_select_fusion.refs_0_.cot), channel_id=1, source_target_pairs={{0,1},{1,0},{2,3},{3,2},{4,5},{5,4},{6,7},{7,6},{8,9},{9,8},{10,11... | collective-permute-start | bytes 786440 | tf_op jit(solution)/shard_map/ppermute | solution.py:530
  39.1 21.5 %collective-permute-start.17 = (bf16[128,1024]{1,0:T(8,128)(2,1)S(1)}, bf16[128,1024]{1,0:T(8,128)(2,1)}, u32[]{:S(2)}, u32[]{:S(2)}) collective-permute-start(bf16[128,1024]{1,0:T(8,128)(2,1)S(1)} %maximum_select_fusion.refs_0_.cot), channel_id=1, source_target_pairs={{0,2},{1,3},{2,0},{3,1},{4,6},{5,7},{6,4},{7,5},{8,10},{9,11},{10,... | collective-permute-start | bytes 786440 | tf_op jit(solution)/shard_map/ppermute | solution.py:530
  40.2 20.4 %collective-permute-start.18 = (bf16[128,1024]{1,0:T(8,128)(2,1)S(1)}, bf16[128,1024]{1,0:T(8,128)(2,1)}, u32[]{:S(2)}, u32[]{:S(2)}) collective-permute-start(bf16[128,1024]{1,0:T(8,128)(2,1)S(1)} %maximum_select_fusion.refs_0_.cot), channel_id=1, source_target_pairs={{0,3},{1,2},{2,1},{3,0},{4,7},{5,6},{6,5},{7,4},{8,11},{9,10},{10,... | collective-permute-start | bytes 786440 | tf_op jit(solution)/shard_map/ppermute | solution.py:530
  60.6 2.7 %collective-permute-start.19 = (bf16[512,1024]{1,0:T(8,128)(2,1)S(1)}, bf16[512,1024]{1,0:T(8,128)(2,1)S(1)}, u32[]{:S(2)}, u32[]{:S(2)}) collective-permute-start(bf16[512,1024]{1,0:T(8,128)(2,1)S(1)} %get-tuple-element.120), channel_id=1, source_target_pairs={{0,4},{4,0},{8,12},{12,8},{16,20},{20,16},{24,28},{28,24},{1,5},{5... | collective-permute-start | bytes 3145736 | tf_op jit(solution)/shard_map/ppermute | solution.py:524
  63.3 6.0 %collective-permute-start.21 = (bf16[128,1024]{1,0:T(8,128)(2,1)}, bf16[128,1024]{1,0:T(8,128)(2,1)S(1)}, u32[]{:S(2)}, u32[]{:S(2)}) collective-permute-start(bf16[128,1024]{1,0:T(8,128)(2,1)} %collective-permute-done.16.refs_1_), channel_id=1, source_target_pairs={{0,4},{4,0},{8,12},{12,8},{16,20},{20,16},{24,28},{28,24},{1,5},{5... | collective-permute-start | bytes 786440 | tf_op jit(solution)/shard_map/ppermute | solution.py:524
  63.4 6.5 %collective-permute-start.22 = (bf16[128,1024]{1,0:T(8,128)(2,1)}, bf16[128,1024]{1,0:T(8,128)(2,1)S(1)}, u32[]{:S(2)}, u32[]{:S(2)}) collective-permute-start(bf16[128,1024]{1,0:T(8,128)(2,1)} %collective-permute-done.17.refs_2_), channel_id=1, source_target_pairs={{0,4},{4,0},{8,12},{12,8},{16,20},{20,16},{24,28},{28,24},{1,5},{5... | collective-permute-start | bytes 786440 | tf_op jit(solution)/shard_map/ppermute | solution.py:524
  63.8 6.2 %collective-permute-start.23 = (bf16[128,1024]{1,0:T(8,128)(2,1)}, bf16[128,1024]{1,0:T(8,128)(2,1)S(1)}, u32[]{:S(2)}, u32[]{:S(2)}) collective-permute-start(bf16[128,1024]{1,0:T(8,128)(2,1)} %collective-permute-done.18.refs_3_), channel_id=1, source_target_pairs={{0,4},{4,0},{8,12},{12,8},{16,20},{20,16},{24,28},{28,24},{1,5},{5... | collective-permute-start | bytes 786440 | tf_op jit(solution)/shard_map/ppermute | solution.py:524
  64.7 11.6 %collective-permute-start.24 = (bf16[128,1024]{1,0:T(8,128)(2,1)S(1)}, bf16[128,1024]{1,0:T(8,128)(2,1)S(1)}, u32[]{:S(2)}, u32[]{:S(2)}) collective-permute-start(bf16[128,1024]{1,0:T(8,128)(2,1)S(1)} %get-tuple-element.134), channel_id=1, source_target_pairs={{0,1},{1,0},{2,3},{3,2},{4,5},{5,4},{6,7},{7,6},{8,9},{9,8},{10,11... | collective-permute-start | bytes 786440 | tf_op jit(solution)/shard_map/ppermute | solution.py:530
  69.2 26.7 %collective-permute-start.20 = (bf16[128,1024]{1,0:T(8,128)(2,1)S(1)}, bf16[128,1024]{1,0:T(8,128)(2,1)S(1)}, u32[]{:S(2)}, u32[]{:S(2)}) collective-permute-start(bf16[128,1024]{1,0:T(8,128)(2,1)S(1)} %get-tuple-element.122), channel_id=1, source_target_pairs={{0,1},{1,0},{2,3},{3,2},{4,5},{5,4},{6,7},{7,6},{8,9},{9,8},{10,11... | collective-permute-start | bytes 786440 | tf_op jit(solution)/shard_map/ppermute | solution.py:530
  69.3 26.7 %collective-permute-start.26 = (bf16[128,1024]{1,0:T(8,128)(2,1)S(1)}, bf16[128,1024]{1,0:T(8,128)(2,1)S(1)}, u32[]{:S(2)}, u32[]{:S(2)}) collective-permute-start(bf16[128,1024]{1,0:T(8,128)(2,1)S(1)} %get-tuple-element.134), channel_id=1, source_target_pairs={{0,0},{1,2},{2,1},{3,3},{4,4},{5,6},{6,5},{7,7},{8,8},{9,10},{10,9... | collective-permute-start | bytes 786440 | tf_op jit(solution)/shard_map/ppermute | solution.py:539
  77.0 19.0 %collective-permute-start.25 = (bf16[128,1024]{1,0:T(8,128)(2,1)S(1)}, bf16[128,1024]{1,0:T(8,128)(2,1)S(1)}, u32[]{:S(2)}, u32[]{:S(2)}) collective-permute-start(bf16[128,1024]{1,0:T(8,128)(2,1)S(1)} %branch_relay.1), channel_id=1, source_target_pairs={{0,2},{1,3},{2,0},{3,1},{4,6},{5,7},{6,4},{7,5},{8,10},{9,11},{10,... | collective-permute-start | bytes 786440 | tf_op jit(solution)/shard_map/ppermute | solution.py:530
  80.0 15.9 %collective-permute-start.27 = (bf16[256,640]{1,0:T(8,128)(2,1)S(1)}, bf16[256,640]{1,0:T(8,128)(2,1)S(1)}, u32[]{:S(2)}, u32[]{:S(2)}) collective-permute-start(bf16[256,640]{1,0:T(8,128)(2,1)S(1)} %get-tuple-element.135), channel_id=1, source_target_pairs={{0,16},{4,20},{8,24},{12,28},{16,0},{20,4},{24,8},{28,12},{1,17},{... | collective-permute-start | bytes 983048 | tf_op jit(solution)/shard_map/ppermute | solution.py:527
  81.6 14.4 %collective-permute-start.28 = (bf16[256,640]{1,0:T(8,128)(2,1)S(1)}, bf16[256,640]{1,0:T(8,128)(2,1)S(1)}, u32[]{:S(2)}, u32[]{:S(2)}) collective-permute-start(bf16[256,640]{1,0:T(8,128)(2,1)S(1)} %get-tuple-element.136), channel_id=1, source_target_pairs={{0,8},{4,12},{8,0},{12,4},{16,24},{20,28},{24,16},{28,20},{1,9},{5... | collective-permute-start | bytes 983048 | tf_op jit(solution)/shard_map/ppermute | solution.py:527
  96.0 9.0 %collective-permute-start.33 = (bf16[528,1024]{1,0:T(8,128)(2,1)S(1)}, bf16[528,1024]{1,0:T(8,128)(2,1)S(1)}, u32[]{:S(2)}, u32[]{:S(2)}) collective-permute-start(bf16[528,1024]{1,0:T(8,128)(2,1)S(1)} %get-tuple-element.162), channel_id=1, source_target_pairs={{0,4},{4,0},{8,12},{12,8},{16,20},{20,16},{24,28},{28,24},{1,5},{5... | collective-permute-start | bytes 3244040 | tf_op jit(solution)/shard_map/ppermute | solution.py:524
  96.1 4.0 %collective-permute-start.29 = (f32[8,1024]{1,0:T(8,128)S(1)}, f32[8,1024]{1,0:T(8,128)S(1)}, u32[]{:S(2)}, u32[]{:S(2)}) collective-permute-start(f32[8,1024]{1,0:T(8,128)S(1)} %get-tuple-element.157.refs_0_), channel_id=1, source_target_pairs={{0,8},{4,12},{8,0},{12,4},{16,24},{20,28},{24,16},{28,20},{1,9},{5... | collective-permute-start | bytes 98312 | tf_op jit(solution)/shard_map/ppermute | solution.py:527
  96.7 3.9 %collective-permute-start.30 = (f32[8,1024]{1,0:T(8,128)S(1)}, f32[8,1024]{1,0:T(8,128)S(1)}, u32[]{:S(2)}, u32[]{:S(2)}) collective-permute-start(f32[8,1024]{1,0:T(8,128)S(1)} %get-tuple-element.157.refs_0_), channel_id=1, source_target_pairs={{0,16},{4,20},{8,24},{12,28},{16,0},{20,4},{24,8},{28,12},{1,17},{... | collective-permute-start | bytes 98312 | tf_op jit(solution)/shard_map/ppermute | solution.py:527
  97.2 4.8 %collective-permute-start.31 = (f32[8,1024]{1,0:T(8,128)S(1)}, f32[8,1024]{1,0:T(8,128)S(1)}, u32[]{:S(2)}, u32[]{:S(2)}) collective-permute-start(f32[8,1024]{1,0:T(8,128)S(1)} %get-tuple-element.157.refs_0_), channel_id=1, source_target_pairs={{0,24},{4,28},{8,16},{12,20},{16,8},{20,12},{24,0},{28,4},{1,25},{... | collective-permute-start | bytes 98312 | tf_op jit(solution)/shard_map/ppermute | solution.py:527
  102.0 11.2 %collective-permute-start.32 = (bf16[256,896]{1,0:T(8,128)(2,1)S(1)}, bf16[256,896]{1,0:T(8,128)(2,1)S(1)}, u32[]{:S(2)}, u32[]{:S(2)}) collective-permute-start(bf16[256,896]{1,0:T(8,128)(2,1)S(1)} %get-tuple-element.158), channel_id=1, source_target_pairs={{0,8},{4,12},{8,0},{12,4},{16,24},{20,28},{24,16},{28,20},{1,9},{5... | collective-permute-start | bytes 1376264 | tf_op jit(solution)/shard_map/ppermute | solution.py:527
  103.5 10.9 %collective-permute-start.36 = (bf16[256,896]{1,0:T(8,128)(2,1)S(1)}, bf16[256,896]{1,0:T(8,128)(2,1)S(1)}, u32[]{:S(2)}, u32[]{:S(2)}) collective-permute-start(bf16[256,896]{1,0:T(8,128)(2,1)S(1)} %get-tuple-element.172), channel_id=1, source_target_pairs={{0,16},{4,20},{8,24},{12,28},{16,0},{20,4},{24,8},{28,12},{1,17},{... | collective-permute-start | bytes 1376264 | tf_op jit(solution)/shard_map/ppermute | solution.py:527
  105.8 2.8 %collective-permute-start.34 = (bf16[128,1024]{1,0:T(8,128)(2,1)S(1)}, bf16[128,1024]{1,0:T(8,128)(2,1)S(1)}, u32[]{:S(2)}, u32[]{:S(2)}) collective-permute-start(bf16[128,1024]{1,0:T(8,128)(2,1)S(1)} %get-tuple-element.166), channel_id=1, source_target_pairs={{0,0},{1,2},{2,1},{3,3},{4,4},{5,6},{6,5},{7,7},{8,8},{9,10},{10,9... | collective-permute-start | bytes 786440 | tf_op jit(solution)/shard_map/ppermute | solution.py:539
  106.5 7.9 %collective-permute-start.35 = (bf16[128,1024]{1,0:T(8,128)(2,1)S(1)}, bf16[128,1024]{1,0:T(8,128)(2,1)S(1)}, u32[]{:S(2)}, u32[]{:S(2)}) collective-permute-start(bf16[128,1024]{1,0:T(8,128)(2,1)S(1)} %get-tuple-element.166), channel_id=1, source_target_pairs={{0,1},{1,0},{2,3},{3,2},{4,5},{5,4},{6,7},{7,6},{8,9},{9,8},{10,11... | collective-permute-start | bytes 786440 | tf_op jit(solution)/shard_map/ppermute | solution.py:530
  108.4 6.0 %collective-permute-start.37 = (f32[8,1024]{1,0:T(8,128)S(1)}, f32[8,1024]{1,0:T(8,128)S(1)}, u32[]{:S(2)}, u32[]{:S(2)}) collective-permute-start(f32[8,1024]{1,0:T(8,128)S(1)} %get-tuple-element.176.refs_8_), channel_id=1, source_target_pairs={{0,4},{4,0},{8,12},{12,8},{16,20},{20,16},{24,28},{28,24},{1,5},{5... | collective-permute-start | bytes 98312 | tf_op jit(solution)/shard_map/ppermute | solution.py:524
  114.4 4.5 %copy-start = (bf16[128,1024]{1,0:T(8,128)(2,1)S(1)}, bf16[128,1024]{1,0:T(8,128)(2,1)}, u32[]{:S(2)}) copy-start(bf16[128,1024]{1,0:T(8,128)(2,1)} %param.15) | copy-start | bytes 786436
  114.4 4.5 %copy-start.3 = (f32[1024]{0:T(1024)S(1)}, f32[1024]{0:T(1024)}, u32[]{:S(2)}) copy-start(f32[1024]{0:T(1024)} %param.28) | copy-start | bytes 12292
  114.4 4.5 %copy-start.4 = (f32[1024]{0:T(1024)S(1)}, f32[1024]{0:T(1024)}, u32[]{:S(2)}) copy-start(f32[1024]{0:T(1024)} %param.24) | copy-start | bytes 12292
  115.2 8.6 %collective-permute-start.38 = (bf16[128,1536]{1,0:T(8,128)(2,1)S(1)}, bf16[128,1536]{1,0:T(8,128)(2,1)S(1)}, u32[]{:S(2)}, u32[]{:S(2)}) collective-permute-start(bf16[128,1536]{1,0:T(8,128)(2,1)S(1)} %get-tuple-element.177), channel_id=1, source_target_pairs={{0,16},{4,20},{8,24},{12,28},{16,0},{20,4},{24,8},{28,12},{1,17},{... | collective-permute-start | bytes 1179656 | tf_op jit(solution)/shard_map/ppermute | solution.py:527
  116.8 13.0 %collective-permute-start.39 = (bf16[144,1024]{1,0:T(8,128)(2,1)S(1)}, bf16[144,1024]{1,0:T(8,128)(2,1)S(1)}, u32[]{:S(2)}, u32[]{:S(2)}) collective-permute-start(bf16[144,1024]{1,0:T(8,128)(2,1)S(1)} %get-tuple-element.180), channel_id=1, source_target_pairs={{0,1},{1,0},{2,3},{3,2},{4,5},{5,4},{6,7},{7,6},{8,9},{9,8},{10,11... | collective-permute-start | bytes 884744 | tf_op jit(solution)/shard_map/ppermute | solution.py:530
  116.9 14.5 %collective-permute-start.40 = (bf16[144,1024]{1,0:T(8,128)(2,1)S(1)}, bf16[144,1024]{1,0:T(8,128)(2,1)S(1)}, u32[]{:S(2)}, u32[]{:S(2)}) collective-permute-start(bf16[144,1024]{1,0:T(8,128)(2,1)S(1)} %get-tuple-element.181), channel_id=1, source_target_pairs={{0,2},{1,3},{2,0},{3,1},{4,6},{5,7},{6,4},{7,5},{8,10},{9,11},{10,... | collective-permute-start | bytes 884744 | tf_op jit(solution)/shard_map/ppermute | solution.py:530
  119.7 10.1 %collective-permute-start.41 = (f32[8,1024]{1,0:T(8,128)S(1)}, f32[8,1024]{1,0:T(8,128)S(1)}, u32[]{:S(2)}, u32[]{:S(2)}) collective-permute-start(f32[8,1024]{1,0:T(8,128)S(1)} %get-tuple-element.182.sums), channel_id=1, source_target_pairs={{0,3},{1,2},{2,1},{3,0},{4,7},{5,6},{6,5},{7,4},{8,11},{9,10},{10,... | collective-permute-start | bytes 98312 | tf_op jit(solution)/shard_map/ppermute | solution.py:530
  123.3 10.7 %collective-permute-start.42 = (bf16[128,1536]{1,0:T(8,128)(2,1)S(1)}, bf16[128,1536]{1,0:T(8,128)(2,1)S(1)}, u32[]{:S(2)}, u32[]{:S(2)}) collective-permute-start(bf16[128,1536]{1,0:T(8,128)(2,1)S(1)} %get-tuple-element.185), channel_id=1, source_target_pairs={{0,8},{4,12},{8,0},{12,4},{16,24},{20,28},{24,16},{28,20},{1,9},{5... | collective-permute-start | bytes 1179656 | tf_op jit(solution)/shard_map/ppermute | solution.py:527
  124.6 9.5 %collective-permute-start.43 = (bf16[128,1536]{1,0:T(8,128)(2,1)S(1)}, bf16[128,1536]{1,0:T(8,128)(2,1)S(1)}, u32[]{:S(2)}, u32[]{:S(2)}) collective-permute-start(bf16[128,1536]{1,0:T(8,128)(2,1)S(1)} %other_sums.1), channel_id=1, source_target_pairs={{0,4},{4,0},{8,12},{12,8},{16,20},{20,16},{24,28},{28,24},{1,5},{5... | collective-permute-start | bytes 1179656 | tf_op jit(solution)/shard_map/ppermute | solution.py:524
  133.1 2.7 %copy-start.1 = (f32[1,1024]{1,0:T(1,128)}, f32[1,1024]{1,0:T(1,128)S(1)}, u32[]{:S(2)}) copy-start(f32[1,1024]{1,0:T(1,128)S(1)} %get-tuple-element.206) | copy-start | bytes 12292
